TPU v7x, 32 devices: a whole 2x2x4 slice. The times are simulated.
32 devices in a mesh: grp: 2 (over y), pb: 4 (over z), ha: 4 (over x, core).
Axes of the slice: x: 2, y: 2, z: 4, core: 2. Of those that a mesh axis runs over, the one named last changes fastest.
Arguments:
- latents: bfloat16 [8, 384, 3072], P(('grp', 'pb'), None, 'ha'), parts along dimension 0, may hold values from -6 to 6
- timesteps: int32 [8], P(('grp', 'pb')), parts along dimension 0, may hold values from 0 to 999
- mod_weight: bfloat16 [256, 3, 3072], P(None, None, 'ha'), may hold values from -0.375 to 0.375
- qkv_weight: bfloat16 [3072, 3, 3072], P(None, None, 'ha'), may hold values from -0.109375 to 0.109375
- out_weight: bfloat16 [3072, 3072], P('ha'), may hold values from -0.15625 to 0.15625
- noise_frame: bfloat16 [768, 3072], P('grp', 'ha'), parts along dimension 0, may hold values from -6 to 6
Outputs:
- advanced: bfloat16 [8, 384, 3072], P(('grp', 'pb'), None, 'ha'), parts along dimension 0
- queue_next: bfloat16 [8, 384, 3072], P(('grp', 'pb'), None, 'ha'), parts along dimension 0
There are 2 independent parts, one for each index of `grp`. A program takes and returns all parts, laid end to end along the dimension named above; an argument that names none is the same for every part. Nothing has to cross between parts.
All inputs are finite; a program needn't handle non-finite values.
Results may differ from a plain program's by a relative error of at most 0.0045.
Values may be sent and summed in bfloat16 or wider, within the bound.
No kernel may reach another device: no remote copies, remote signals or barrier semaphores. Data moves between devices by JAX's collectives and lax.ppermute only.
A program may use at most 64 MiB of HBM per device.

v0:
```python
import math

import jax
import jax.numpy as jnp
from jax import lax
from jax.sharding import PartitionSpec as P

HD = 128
TDIM = 256


def from_behind(x, axis, by):
    size = lax.axis_size(axis)
    pairs = [(i, i + by) for i in range(size) if 0 <= i + by < size]
    return lax.ppermute(x, axis, pairs)


def sinusoid(timesteps):
    half_width = TDIM // 2
    frequency = jnp.exp(-math.log(10000.0) * jnp.arange(half_width, dtype=jnp.float32) / half_width)
    angles = timesteps.astype(jnp.float32)[:, None] * frequency[None, :]
    return jnp.concatenate([jnp.cos(angles), jnp.sin(angles)], axis=1)


def unit_rms(vectors):
    return vectors * lax.rsqrt(jnp.mean(vectors * vectors, axis=-1, keepdims=True) + 1e-06)


def absorb(running, pieces, queries, head_local):
    key_piece, value_piece = pieces

    def one_frame(position, inner):
        numerator, denominator = inner
        key_frame = lax.dynamic_index_in_dim(key_piece, position, 0, keepdims=False)
        value_frame = lax.dynamic_index_in_dim(value_piece, position, 0, keepdims=False)
        key_count = key_frame.shape[0]
        key_frame = key_frame.reshape(key_count, head_local, -1)
        value_frame = value_frame.reshape(key_count, head_local, -1)
        scores = jnp.einsum("rhd,khd->hrk", queries, key_frame, preferred_element_type=jnp.float32)
        weights_exp = jnp.exp(scores)
        denominator = denominator + jnp.sum(weights_exp, axis=2)
        numerator = numerator + jnp.einsum(
            "hrk,khd->rhd",
            weights_exp.astype(jnp.bfloat16),
            value_frame,
            preferred_element_type=jnp.float32,
        )
        return (numerator, denominator)

    return lax.fori_loop(0, key_piece.shape[0], one_frame, running)


def on_device(latents, timesteps, mod_weight, qkv_weight, out_weight, noise_frame):
    frames, tok_count, local_width = latents.shape
    full_width = qkv_weight.shape[0]
    head_size = HD
    head_local = local_width // head_size
    row_count = frames * tok_count
    out_columns = lax.all_to_all(out_weight, "ha", split_axis=1, concat_axis=0, tiled=True)
    embedding = sinusoid(timesteps).astype(jnp.bfloat16)
    modulation = jnp.dot(
        embedding,
        mod_weight.reshape(mod_weight.shape[0], 3 * local_width),
        preferred_element_type=jnp.float32,
    )
    modulation = modulation.astype(jnp.bfloat16).reshape(frames, 3, local_width)
    whole_rows, whole_mod = (
        lax.all_gather(latents, "ha", axis=2, tiled=True),
        lax.all_gather(modulation[:, :2], "ha", axis=2, tiled=True),
    )
    whole_mod = whole_mod.astype(jnp.float32)
    latent_wide = whole_rows.astype(jnp.float32)
    row_mean = jnp.mean(latent_wide, axis=-1, keepdims=True)
    centered = latent_wide - row_mean
    row_var = jnp.mean(centered * centered, axis=-1, keepdims=True)
    normed = centered * lax.rsqrt(row_var + 1e-06)
    hidden = normed * (1.0 + whole_mod[:, 1][:, None, :]) + whole_mod[:, 0][:, None, :]
    hidden = hidden.astype(jnp.bfloat16).reshape(row_count, full_width)
    projected = jnp.dot(
        hidden, qkv_weight.reshape(full_width, 3 * local_width), preferred_element_type=jnp.float32
    )
    projected = projected.reshape(row_count, 3, head_local, head_size)
    queries = (unit_rms(projected[:, 0]) / math.sqrt(head_size)).astype(jnp.bfloat16)
    key_rows = (
        unit_rms(projected[:, 1]).astype(jnp.bfloat16).reshape(frames, tok_count, local_width)
    )
    value_rows = projected[:, 2].astype(jnp.bfloat16).reshape(frames, tok_count, local_width)
    start_carry = (
        jnp.zeros((row_count, head_local, head_size), jnp.float32),
        jnp.zeros((head_local, row_count), jnp.float32),
    )
    key_all, value_all = (
        lax.all_gather(key_rows, "pb", axis=0, tiled=True),
        lax.all_gather(value_rows, "pb", axis=0, tiled=True),
    )
    numerator, denominator = absorb(start_carry, (key_all, value_all), queries, head_local)
    attended = (
        (numerator / denominator.T[:, :, None]).astype(jnp.bfloat16).reshape(row_count, local_width)
    )
    branch = jnp.dot(
        lax.all_gather(attended, "ha", axis=1, tiled=True),
        out_columns,
        preferred_element_type=jnp.float32,
    )
    branch = branch.reshape(frames, tok_count, local_width)
    gate_wide = modulation[:, 2].astype(jnp.float32)[:, None, :]
    advanced = (latents.astype(jnp.float32) + gate_wide * branch).astype(jnp.bfloat16)
    incoming = from_behind(advanced, "pb", -1)
    is_last = lax.axis_index("pb") == lax.axis_size("pb") - 1
    tail_frame = jnp.where(is_last, noise_frame[None], incoming)
    queue_next = jnp.concatenate([advanced[1:], tail_frame], axis=0)
    return (advanced, queue_next)


def solution(mesh):
    placed = (
        P(("grp", "pb"), None, "ha"),
        P(("grp", "pb")),
        P(None, None, "ha"),
        P(None, None, "ha"),
        P("ha", None),
        P("grp", "ha"),
    )
    return jax.shard_map(
        on_device,
        mesh=mesh,
        in_specs=placed,
        out_specs=(P(("grp", "pb"), None, "ha"), P(("grp", "pb"), None, "ha")),
        check_vma=False,
    )
```

profile of v0, /device:TPU:0, one launch (start us, length us, event | category | flops | bytes accessed | tf_op | source)
XLA Modules:
  0.0 259.0 jit_solution(10674421774756293584)
XLA Ops:
  11.3 6.1 %all_gather.16 = bf16[1,2,3072]{2,1,0:T(2,128)(2,1)S(1)} all-gather(bf16[1,2,768]{2,1,0:T(2,128)(2,1)S(1)} %slice.30), channel_id=1, replica_groups=mesh['grp'=2,'pb'=4,'ha'=4] {'ha'}, dimensions={2}, use_global_device_ids=true | all-gather | bytes 15360 | tf_op jit(solution)/shard_map/all_gather | solution.py:69
  17.5 17.4 %copy.27 = bf16[3072,3,768]{0,2,1:T(8,128)(2,1)} copy(bf16[3072,3,768]{2,0,1:T(8,128)(2,1)} %param.11) | data formatting | bytes 28311552 | tf_op args[3]
  36.4 2.2 convert_reduce_fusion
  39.5 10.7 %fusion.10 = f32[384,3,6,128]{0,3,2,1:T(8,128)S(1)} fusion(bf16[3,6,128,3072]{3,2,1,0:T(8,128)(2,1)} %bitcast.84, bf16[1,384,3072]{2,1,0:T(8,128)(2,1)S(1)} %copy-done, f32[3072]{0:T(1024)S(1)} %bitcast.88, f32[3072]{0:T(1024)S(1)} %bitcast.89, f32[384]{0:T(512)S(1)} %add_rsqrt_fusion.2, f32[384]{0:T(512)S(1)} %broadcast_multiply_fusion), kind=kOutput, calls=%fused_computation.17 | convolution fusion | flops 5442895872 | bytes 20081664 | tf_op jit(solution)/shard_map/dot_general | solution.py:79
  51.3 2.1 copy.29
  54.4 2.1 copy.28
  56.5 6.7 %copy.33 = bf16[768,3072]{0,1:T(8,128)(2,1)} copy(bf16[768,3072]{1,0:T(8,128)(2,1)} %param.12) | data formatting | bytes 9437184 | tf_op args[4]
  63.3 4.9 %all-to-all-start = ((bf16[768,4,768]{0,2,1:T(8,128)(2,1)}), bf16[768,4,768]{0,2,1:T(8,128)(2,1)}, u32[]{:S(2)}, u32[]{:S(2)}) async-start(bf16[768,4,768]{0,2,1:T(8,128)(2,1)} %bitcast.83), calls=%async_computation | async-start | bytes 9437184 | tf_op jit(solution)/shard_map/all_to_all | solution.py:59
  69.3 2.2 copy.32
  71.5 34.8 %all-gather.9.cloned.1.call-done = bf16[4,384,768]{2,1,0:T(8,128)(2,1)} async-done(((bf16[1,384,768]{2,1,0:T(8,128)(2,1)}), bf16[4,384,768]{2,1,0:T(8,128)(2,1)}) %all-gather.9.cloned.1.call-update) | async-done | bytes 2359312 | tf_op jit(solution)/shard_map/all_gather | solution.py:93
  106.3 51.5 %all-gather.7.cloned.1.call-done = bf16[4,384,768]{2,1,0:T(8,128)(2,1)} async-done(((bf16[1,384,768]{2,1,0:T(8,128)(2,1)}), bf16[4,384,768]{2,1,0:T(8,128)(2,1)}) %all-gather.7.cloned.1.call-update) | async-done | bytes 2359312 | tf_op jit(solution)/shard_map/all_gather | solution.py:94
  157.8 45.9 %while.16 = (s32[]{:T(128)}, f32[384,6,128]{0,2,1:T(8,128)}, f32[6,384]{1,0:T(8,128)}, bf16[4,384,768]{2,1,0:T(8,128)(2,1)}, bf16[4,384,768]{2,1,0:T(8,128)(2,1)...) while((s32[]{:T(128)}, f32[384,6,128]{0,2,1:T(8,128)}, f32[6,384]{1,0:T(8,128)}, ...), condition=%wide.region_6.7_spmd.clone, body=%wide.region_4.6_spmd.clone.sunk | while | flops 455346432 | bytes 15962212 | solution.py:50
  157.8 2.1 constant_dynamic-slice_fusion.3
  161.0 2.0 bitcast_reduce_fusion.2
  163.0 2.1 copy.42
  165.1 2.8 %fusion.36 = f32[384,6,128]{0,2,1:T(8,128)} fusion(bf16[384,6,128]{0,2,1:T(8,128)(2,1)} %bitcast.80, f32[6,384,384]{2,1,0:T(8,128)S(1)} %get-tuple-element.222, f32[384,6,128]{0,2,1:T(8,128)} %get-tuple-element.233, pred[]{:T(512)S(6)} %compare.3), kind=kOutput, calls=%fused_computation.4.clone.1 | convolution fusion | flops 227966976 | bytes 6488065 | tf_op jit(solution)/shard_map/while/body/eval_jaxpr/hrk,khd->rhd/dot_general | solution.py:42
  168.5 2.1 constant_dynamic-slice_fusion.3
  171.7 2.0 bitcast_reduce_fusion.2
  173.7 2.1 copy.42
  175.8 3.1 %fusion.36 = f32[384,6,128]{0,2,1:T(8,128)} fusion(bf16[384,6,128]{0,2,1:T(8,128)(2,1)} %bitcast.80, f32[6,384,384]{2,1,0:T(8,128)S(1)} %get-tuple-element.222, f32[384,6,128]{0,2,1:T(8,128)} %get-tuple-element.233, pred[]{:T(512)S(6)} %compare.3), kind=kOutput, calls=%fused_computation.4.clone.1 | convolution fusion | flops 227966976 | bytes 6488065 | tf_op jit(solution)/shard_map/while/body/eval_jaxpr/hrk,khd->rhd/dot_general | solution.py:42
  180.2 2.1 constant_dynamic-slice_fusion.3
  185.4 2.1 copy.42
  187.5 3.1 %fusion.36 = f32[384,6,128]{0,2,1:T(8,128)} fusion(bf16[384,6,128]{0,2,1:T(8,128)(2,1)} %bitcast.80, f32[6,384,384]{2,1,0:T(8,128)S(1)} %get-tuple-element.222, f32[384,6,128]{0,2,1:T(8,128)} %get-tuple-element.233, pred[]{:T(512)S(6)} %compare.3), kind=kOutput, calls=%fused_computation.4.clone.1 | convolution fusion | flops 227966976 | bytes 6488065 | tf_op jit(solution)/shard_map/while/body/eval_jaxpr/hrk,khd->rhd/dot_general | solution.py:42
  192.0 2.1 constant_dynamic-slice_fusion.3
  195.2 2.0 bitcast_reduce_fusion.2
  197.2 2.1 copy.42
  199.3 3.1 %fusion.36 = f32[384,6,128]{0,2,1:T(8,128)} fusion(bf16[384,6,128]{0,2,1:T(8,128)(2,1)} %bitcast.80, f32[6,384,384]{2,1,0:T(8,128)S(1)} %get-tuple-element.222, f32[384,6,128]{0,2,1:T(8,128)} %get-tuple-element.233, pred[]{:T(512)S(6)} %compare.3), kind=kOutput, calls=%fused_computation.4.clone.1 | convolution fusion | flops 227966976 | bytes 6488065 | tf_op jit(solution)/shard_map/while/body/eval_jaxpr/hrk,khd->rhd/dot_general | solution.py:42
  203.8 2.2 divide_convert_fusion
  206.0 6.8 %copy.34 = bf16[4,768,768]{2,1,0:T(8,128)(2,1)} copy(bf16[4,768,768]{1,2,0:T(8,128)(2,1)} %bitcast.17) | data formatting | bytes 9437184 | tf_op jit(solution)/shard_map/all_to_all | solution.py:59
  212.8 16.2 %all-gather.11.cloned.1.call-done = bf16[384,3072]{0,1:T(8,128)(2,1)} async-done(((bf16[384,768]{0,1:T(8,128)(2,1)}), bf16[384,3072]{0,1:T(8,128)(2,1)}) %all-gather.11.cloned.1.call-update) | async-done | bytes 2359312 | tf_op jit(solution)/shard_map/all_gather | solution.py:101
  229.0 5.1 %fusion.18 = bf16[1,384,768]{2,1,0:T(8,128)(2,1)S(1)} fusion(bf16[384,3072]{0,1:T(8,128)(2,1)} %all-gather.11.cloned.1.call-done, bf16[3072,768]{1,0:T(8,128)(2,1)} %bitcast.82, bf16[1,384,768]{2,1,0:T(8,128)(2,1)S(1)} %copy-done.1, f32[768]{0:T(1024)S(1)} %fusion.20), kind=kOutput, calls=%fused_computation.25 | convolution fusion | flops 1813118976 | bytes 8260608 | tf_op jit(solution)/shard_map/dot_general | solution.py:100
  235.5 16.1 %collective-permute-done = bf16[1,384,768]{2,1,0:T(8,128)(2,1)S(1)} collective-permute-done((bf16[1,384,768]{2,1,0:T(8,128)(2,1)S(1)}, bf16[1,384,768]{2,1,0:T(8,128)(2,1)S(1)}, u32[]{:S(2)}, u32[]{:S(2)}) %collective-permute-start) | collective-permute-done | bytes 589856 | tf_op jit(solution)/shard_map/ppermute | solution.py:15
  (58 shorter events, 21.9 us)
Async XLA Ops:
  7.2 29.2 %all-gather.5.cloned.1.call-start = ((), (), s32[]{:S(2)}) async-start(), calls=%async_computation.1 | async-start | bytes 2949120 | tf_op jit(solution)/shard_map/all_gather | solution.py:68
  7.9 98.4 %all-gather.9.cloned.1.call-start = ((), (), s32[]{:S(2)}) async-start(), calls=%async_computation.3 | async-start | bytes 2949120 | tf_op jit(solution)/shard_map/all_gather | solution.py:93
  10.7 0.6 copy-start.4
  36.4 2.4 copy-start
  36.4 3.1 %copy-start.6 = (f32[1,1,3072]{2,1,0:T(1,128)S(1)}, f32[1,1,3072]{2,1,0:T(1,128)}, u32[]{:S(2)}) copy-start(f32[1,1,3072]{2,1,0:T(1,128)} %slice_add_fusion) | copy-start | bytes 36868
  53.5 104.3 %all-gather.7.cloned.1.call-start = ((), (), s32[]{:S(2)}) async-start(), calls=%async_computation.2 | async-start | bytes 2949120 | tf_op jit(solution)/shard_map/all_gather | solution.py:94
  63.3 142.8 %all-to-all-start = ((bf16[768,4,768]{0,2,1:T(8,128)(2,1)}), bf16[768,4,768]{0,2,1:T(8,128)(2,1)}, u32[]{:S(2)}, u32[]{:S(2)}) async-start(bf16[768,4,768]{0,2,1:T(8,128)(2,1)} %bitcast.83), calls=%async_computation | async-start | bytes 9437184 | tf_op jit(solution)/shard_map/all_to_all | solution.py:59
  68.2 160.8 %all-gather.11.cloned.1.call-start = ((), (), s32[]{:S(2)}) async-start(), calls=%async_computation.4 | async-start | bytes 2949120 | tf_op jit(solution)/shard_map/all_gather | solution.py:101
  203.7 2.2 copy-start.5
  206.0 23.0 %copy-start.1 = (bf16[1,384,768]{2,1,0:T(8,128)(2,1)S(1)}, bf16[1,384,768]{2,1,0:T(8,128)(2,1)}, u32[]{:S(2)}) copy-start(bf16[1,384,768]{2,1,0:T(8,128)(2,1)} %param.8) | copy-start | bytes 1769476
  229.0 22.5 %copy-start.3 = (bf16[384,768]{1,0:T(8,128)(2,1)S(1)}, bf16[384,768]{1,0:T(8,128)(2,1)}, u32[]{:S(2)}) copy-start(bf16[384,768]{1,0:T(8,128)(2,1)} %param.13) | copy-start | bytes 1769476
  234.2 18.3 %copy-start.2 = (bf16[1,384,768]{2,1,0:T(8,128)(2,1)}, bf16[1,384,768]{2,1,0:T(8,128)(2,1)S(1)}, u32[]{:S(2)}) copy-start(bf16[1,384,768]{2,1,0:T(8,128)(2,1)S(1)} %fusion.18) | copy-start | bytes 1769476
  234.2 17.4 %collective-permute-start = (bf16[1,384,768]{2,1,0:T(8,128)(2,1)S(1)}, bf16[1,384,768]{2,1,0:T(8,128)(2,1)S(1)}, u32[]{:S(2)}, u32[]{:S(2)}) collective-permute-start(bf16[1,384,768]{2,1,0:T(8,128)(2,1)S(1)} %fusion.18), channel_id=1, source_target_pairs={{4,0},{8,4},{12,8},{5,1},{9,5},{13,9},{6,2},{10,6},{14,10},{7,3},{... | collective-permute-start | bytes 1769480 | tf_op jit(solution)/shard_map/ppermute | solution.py:15
Sparse Core Ops, SparseCore 0:
  9.6 26.7 all-gather.4
  53.6 52.6 all-gather.8
  108.5 49.2 all-gather.6
  206.1 22.8 all-gather.10
where the time goes:
time: 261 us; the launch traced here: 259 us
  waiting for transfers between devices  120 us (46%)
  local copies, waits for them, and re-layouts  61.8 us (24%)
  matrix products  36.4 us (14%)
  between operations  14.6 us (6%)
  other arithmetic  13.4 us (5%)
  starting transfers between devices  6.4 us (2%)
  blocking collectives  6.14 us (2%)
    all_gather x1, waiting for transfers between devices, on_device(): lax.all_gather(value_rows, 'pb', axis=0, tiled=True)  51.5 us
    all_gather x1, waiting for transfers between devices, on_device(): lax.all_gather(key_rows, 'pb', axis=0, tiled=True)  34.8 us
    unnamed x18, local copies, waits for them, and re-layouts  28.6 us
    all_gather x1, waiting for transfers between devices, on_device(): lax.all_gather(attended, 'ha', axis=1, tiled=True)  16.2 us
    ppermute x1, waiting for transfers between devices, from_behind(): return lax.ppermute(x, axis, pairs)  16.1 us
    dynamic_slice x8, local copies, waits for them, and re-layouts, one_frame(): key_frame = lax.dynamic_index_in_dim(key_piece, position, 0, keepdims=False)  12.7 us
    dot_general x4, matrix products, one_frame(): jnp.einsum('hrk,khd->rhd', weights_exp.astype(jnp.bfloat16), value_frame,...  12.2 us
    dot_general x1, matrix products, on_device(): jnp.dot(hidden, qkv_weight.reshape(full_width, 3 * local_width), preferre...  10.7 us
  transfers between devices with their start and end apart: 6, of which 5 were waited for; matrix products, arithmetic and copies ran while one was open for 34% of the time, Pallas kernels for 0%

commit v1 on v0

v1 whole, which is shorter than its diff:
```python
import functools
import math

import jax
import jax.numpy as jnp
from jax import lax
from jax.experimental import pallas as pl
from jax.experimental.pallas import tpu as pltpu
from jax.sharding import PartitionSpec as P

HD = 128
TDIM = 256
F32 = jnp.float32
BF16 = jnp.bfloat16
VMEM_LIMIT = 40 * 1024 * 1024


def flip(x, axis, bit):
    size = lax.axis_size(axis)
    return lax.ppermute(x, axis, [(i, i ^ bit) for i in range(size)])


def from_behind(x, axis, by):
    size = lax.axis_size(axis)
    pairs = [(i, i + by) for i in range(size) if 0 <= i + by < size]
    return lax.ppermute(x, axis, pairs)


def sinusoid(timesteps):
    half_width = TDIM // 2
    frequency = jnp.exp(-math.log(10000.0) * jnp.arange(half_width, dtype=F32) / half_width)
    angles = timesteps.astype(F32)[:, None] * frequency[None, :]
    return jnp.concatenate([jnp.cos(angles), jnp.sin(angles)], axis=1)


def unit_rms(vectors):
    return vectors * lax.rsqrt(jnp.mean(vectors * vectors, axis=-1, keepdims=True) + 1e-06)


def norm_rows(ids_ref, piece_refs, mod_ref, hidden_ref):
    ha, frame = ids_ref[0], ids_ref[1]
    count = len(piece_refs)
    rows, width = piece_refs[0].shape
    step = 16

    def one(i, carry):
        at = pl.ds(pl.multiple_of(i * step, step), step)
        wide = [ref[at, :].astype(F32) for ref in piece_refs]
        total = sum(jnp.sum(w, axis=-1, keepdims=True) for w in wide)
        mean = total / (count * width)
        wide = [w - mean for w in wide]
        square = sum(jnp.sum(w * w, axis=-1, keepdims=True) for w in wide)
        inverse = lax.rsqrt(square / (count * width) + 1e-06)
        for j in range(count):
            block = lax.bitwise_xor(ha, j)
            mod = mod_ref[frame * count + block]
            out = wide[j] * inverse * (1.0 + mod[1:2]) + mod[0:1]
            hidden_ref[at, pl.ds(pl.multiple_of(block * width, HD), width)] = out.astype(BF16)
        return carry

    lax.fori_loop(0, rows // step, one, 0, unroll=2)


def attend(q, k, v, num, den):
    scores = lax.dot_general(q, k, (((1,), (1,)), ((), ())), preferred_element_type=F32)
    weights = jnp.exp(scores)
    for start in range(0, weights.shape[1], HD):
        part = weights[:, start : start + HD]
        den = part if den is None else den + part
    more = jnp.dot(weights.astype(BF16), v, preferred_element_type=F32)
    return more if num is None else num + more, den


def frame_body(own, last, count, heads, ids_ref, *refs):
    pieces, refs = refs[:count], refs[count:]
    mod_ref, refs = refs[0], refs[1:]
    if own:
        wq_ref, wk_ref, wv_ref, q_out, num_out, den_out, hidden_ref = refs
    elif last:
        wk_ref, wv_ref, q_ref, num_ref, den_ref, att_out, hidden_ref = refs
    else:
        wk_ref, wv_ref, q_ref, num_ref, den_ref, num_out, den_out, hidden_ref = refs

    @pl.when(pl.program_id(0) == 0)
    def _():
        norm_rows(ids_ref, pieces, mod_ref, hidden_ref)

    hidden = hidden_ref[...]
    key_all = jnp.dot(hidden, wk_ref[0], preferred_element_type=F32)
    value_all = jnp.dot(hidden, wv_ref[0], preferred_element_type=F32)
    query_all = jnp.dot(hidden, wq_ref[0], preferred_element_type=F32) if own else None
    for head in range(heads):
        at = slice(head * HD, (head + 1) * HD)
        k = unit_rms(key_all[:, at]).astype(BF16)
        v = value_all[:, at].astype(BF16)
        if own:
            q = (unit_rms(query_all[:, at]) * (1.0 / math.sqrt(HD))).astype(BF16)
            q_out[:, at] = q
            num, den = attend(q, k, v, None, None)
        else:
            num, den = attend(q_ref[:, at], k, v, num_ref[:, at], den_ref[:, at])
        if last:
            att_out[:, at] = (num / jnp.sum(den, axis=-1, keepdims=True)).astype(BF16)
        else:
            num_out[:, at] = num
            den_out[:, at] = den


def frame_step(ids, pieces, mods, weight, state, last):
    own = state is None
    count = len(pieces)
    rows, width = pieces[0].shape
    full = weight.shape[1]
    head_local = width // HD
    heads = 2 if head_local % 2 == 0 else 1
    block = heads * HD
    weight_at = lambda j: pl.BlockSpec((1, full, block), lambda h, ids: (j, 0, h))
    whole = pl.BlockSpec((rows, width), lambda h, ids: (0, 0))
    queries = rows if own else state[0].shape[0]
    column = pl.BlockSpec((queries, block), lambda h, ids: (0, h))
    in_specs = [whole] * count + [pl.BlockSpec(mods.shape, lambda h, ids: (0, 0, 0))]
    args = [ids, *pieces, mods]
    used = (0, 1, 2) if own else (1, 2)
    in_specs += [weight_at(j) for j in used]
    args += [weight] * len(used)
    wide = jax.ShapeDtypeStruct((queries, width), F32)
    thin = jax.ShapeDtypeStruct((queries, width), BF16)
    if own:
        outs = (thin, wide, wide)
    else:
        in_specs += [column] * 3
        args += state
        outs = (thin,) if last else (wide, wide)
    flops = 2 * rows * full * width * len(used) + 4 * queries * rows * width
    return pl.pallas_call(
        functools.partial(frame_body, own, last, count, heads),
        grid_spec=pltpu.PrefetchScalarGridSpec(
            num_scalar_prefetch=1,
            grid=(head_local // heads,),
            in_specs=in_specs,
            out_specs=tuple(column for _ in outs),
            scratch_shapes=[pltpu.VMEM((rows, full), BF16)],
        ),
        out_shape=outs,
        compiler_params=pltpu.CompilerParams(vmem_limit_bytes=VMEM_LIMIT),
        cost_estimate=pl.CostEstimate(
            flops=flops, bytes_accessed=2 * full * width * len(used), transcendentals=queries * rows * head_local
        ),
    )(*args)


def project_body(ids_ref, *refs):
    *ins, out_ref = refs
    half = len(ins) // 2
    total = None
    for att_ref, weight_ref in zip(ins[:half], ins[half:]):
        part = jnp.dot(att_ref[...], weight_ref[...], preferred_element_type=F32)
        total = part if total is None else total + part
    out_ref[...] = total.astype(out_ref.dtype)


def project(ids, attended, weights, index_maps, dtype):
    rows, width = attended[0].shape
    flops = 2 * rows * width * width * len(attended)
    return pl.pallas_call(
        project_body,
        grid_spec=pltpu.PrefetchScalarGridSpec(
            num_scalar_prefetch=1,
            grid=(1,),
            in_specs=[pl.BlockSpec((rows, width), lambda i, ids: (0, 0)) for _ in attended]
            + [pl.BlockSpec((width, width), index_map) for index_map in index_maps],
            out_specs=pl.BlockSpec((rows, width), lambda i, ids: (0, 0)),
        ),
        out_shape=jax.ShapeDtypeStruct((rows, width), dtype),
        compiler_params=pltpu.CompilerParams(vmem_limit_bytes=VMEM_LIMIT),
        cost_estimate=pl.CostEstimate(
            flops=flops, bytes_accessed=2 * width * width * len(attended), transcendentals=0
        ),
    )(ids, *attended, *weights)


def spread(piece):
    size = lax.axis_size("ha")
    out = [None] * size
    out[0] = piece
    for step in range(2, size, 2):
        out[step] = flip(piece, "ha", step)
    for step in range(0, size, 2):
        out[step + 1] = flip(out[step], "ha", 1)
    return out


def on_device(latents, timesteps, mod_weight, qkv_weight, out_weight, noise_frame):
    frames, tok_count, width = latents.shape
    ha_size, pb_size = lax.axis_size("ha"), lax.axis_size("pb")
    ha, pb = lax.axis_index("ha"), lax.axis_index("pb")
    piece = latents.reshape(tok_count, width)
    weight = jnp.transpose(qkv_weight, (1, 0, 2))

    embedding = sinusoid(timesteps).astype(BF16)
    modulation = jnp.einsum(
        "pe,jef->pjf", embedding, jnp.transpose(mod_weight, (1, 0, 2)), preferred_element_type=F32
    ).astype(BF16)
    mods = lax.all_gather(modulation[:, :2], ("pb", "ha"), axis=0, tiled=True).astype(F32)
    gate = modulation[:, 2].astype(F32)

    columns = [
        lax.dynamic_slice_in_dim(out_weight, lax.bitwise_xor(ha, step + 1) * width, width, 1)
        for step in range(0, ha_size, 2)
    ]
    other_weight = [flip(c, "ha", 1) for c in columns]

    def ids_of(bit):
        return jnp.stack([ha, lax.bitwise_xor(pb, bit)]).astype(jnp.int32)

    own_pieces = spread(piece)
    order = list(range(1, pb_size))
    arrived = []
    for n, bit in enumerate(order):
        if n == len(order) - 1 and tok_count == 384:
            arrived.append((bit, flip(piece[:256], "pb", bit)))
            arrived.append((bit, flip(piece[256:], "pb", bit)))
        else:
            arrived.append((bit, flip(piece, "pb", bit)))
    q, num, den = frame_step(ids_of(0), own_pieces, mods, weight, None, False)
    for n, (bit, got) in enumerate(arrived):
        last = n == len(arrived) - 1
        result = frame_step(ids_of(bit), spread(got), mods, weight, (q, num, den), last)
        if last:
            (attended,) = result
        else:
            num, den = result

    ids = ids_of(0)
    is_last = pb == pb_size - 1
    done, following = [], []
    for start, stop in ((0, tok_count // 2), (tok_count // 2, tok_count)):
        mine = attended[start:stop]
        both = (mine, flip(mine, "ha", 1))
        branch = None
        for step in range(ha_size - 2, -1, -2):
            at = lambda i, ids, step=step: (0, lax.bitwise_xor(ids[0], step))
            zero = lambda i, ids: (0, 0)
            part = project(
                ids, both, (out_weight, other_weight[step // 2]), (at, zero), BF16 if step else F32
            )
            if step:
                part = flip(part, "ha", step).astype(F32)
            branch = part if branch is None else branch + part
        advanced = (piece[start:stop].astype(F32) + gate * branch).astype(BF16)
        incoming = from_behind(advanced, "pb", -1)
        done.append(advanced)
        following.append(jnp.where(is_last, noise_frame[start:stop], incoming))
    return jnp.concatenate(done, axis=0)[None], jnp.concatenate(following, axis=0)[None]


def solution(mesh):
    placed = (
        P(("grp", "pb"), None, "ha"),
        P(("grp", "pb")),
        P(None, None, "ha"),
        P(None, None, "ha"),
        P("ha", None),
        P("grp", "ha"),
    )
    return jax.shard_map(
        on_device,
        mesh=mesh,
        in_specs=placed,
        out_specs=(P(("grp", "pb"), None, "ha"), P(("grp", "pb"), None, "ha")),
        check_vma=False,
    )
```

time: 261 us -> 172 us (0.66)
  waiting for transfers between devices: 120 us -> 55.9 us
  Pallas kernels: 0 us -> 63 us
  local copies, waits for them, and re-layouts: 61.8 us -> 5.87 us
  matrix products: 36.4 us -> 0.27 us
  blocking collectives: 6.14 us -> 24.4 us
  between operations: 14.6 us -> 1.59 us
  starting transfers between devices: 6.4 us -> 18.2 us
  other arithmetic: 13.4 us -> 2.43 us
    all_gather x4 -> x0, waiting for transfers between devices: 103 us -> none  [the longest x1 51.5 us: on_device(): lax.all_gather(value_rows, 'pb', axis=0, tiled=True)]
    pallas_call x0 -> x9, Pallas kernels: none -> 63 us  [the longest x5 58.3 us: frame_step(): pl.pallas_call(functools.partial(frame_body, own, last, count, heads), gr...]
    ppermute x0 -> x25, waiting for transfers between devices: none -> 43 us  [flip(): return lax.ppermute(x, axis, [(i, i ^ bit) for i in range(size)])]
    dot_general x11 -> x1, matrix products: 36.4 us -> 0.27 us  [on_device(): jnp.einsum('pe,jef->pjf', embedding, jnp.transpose(mod_weight, (1, 0, 2))...]
    unnamed x18 -> x16, local copies, waits for them, and re-layouts: 28.6 us -> 0.04 us
    all_gather x1, blocking collectives: 6.14 us -> 24.4 us  [on_device(): lax.all_gather(modulation[:, :2], ('pb', 'ha'), axis=0, tiled=True)]
    dynamic_slice x12 -> x1, local copies, waits for them, and re-layouts: 21.2 us -> 3.28 us  [on_device(): lax.dynamic_slice_in_dim(out_weight, lax.bitwise_xor(ha, step + 1) * widt...]
    ppermute x0 -> x25, starting transfers between devices: none -> 15.5 us  [flip(): return lax.ppermute(x, axis, [(i, i ^ bit) for i in range(size)])]
  transfers between devices with their start and end apart: 6 -> 27, of which waited for: 5 -> 8; matrix products, arithmetic and copies ran while one was open for 34% -> 4% of each run, Pallas kernels for 0% -> 37%
where the time goes in v1:
time: 172 us
  Pallas kernels  63 us (37%)
  waiting for transfers between devices  55.9 us (32%)
  blocking collectives  24.4 us (14%)
  starting transfers between devices  18.2 us (11%)
  local copies, waits for them, and re-layouts  5.87 us (3%)
  other arithmetic  2.43 us (1%)
    pallas_call x5, Pallas kernels, frame_step(): pl.pallas_call(functools.partial(frame_body, own, last, count, heads), gr...  58.3 us
    ppermute x25, waiting for transfers between devices, flip(): return lax.ppermute(x, axis, [(i, i ^ bit) for i in range(size)])  43 us
    all_gather x1, blocking collectives, on_device(): lax.all_gather(modulation[:, :2], ('pb', 'ha'), axis=0, tiled=True)  24.4 us
    ppermute x25, starting transfers between devices, flip(): return lax.ppermute(x, axis, [(i, i ^ bit) for i in range(size)])  15.5 us
    ppermute x2, waiting for transfers between devices, from_behind(): return lax.ppermute(x, axis, pairs)  13 us
    pallas_call x4, Pallas kernels, project(): pl.pallas_call(project_body, grid_spec=pltpu.PrefetchScalarGridSpec(num_s...  4.72 us
  transfers between devices with their start and end apart: 27, of which 8 were waited for; matrix products, arithmetic and copies ran while one was open for 4% of the time, Pallas kernels for 37%

profile of v1, /device:TPU:0, one launch (start us, length us, event | category | flops | bytes accessed | tf_op | source)
XLA Modules:
  0.0 171.7 jit_solution(15507418255844323749)
XLA Ops:
  0.6 3.0 %collective-permute-start.5 = (bf16[384,768]{1,0:T(8,128)(2,1)}, bf16[384,768]{1,0:T(8,128)(2,1)S(1)}, u32[]{:S(2)}, u32[]{:S(2)}) collective-permute-start(bf16[384,768]{1,0:T(8,128)(2,1)} %bitcast.36), channel_id=1, source_target_pairs={{0,2},{1,3},{2,0},{3,1},{4,6},{5,7},{6,4},{7,5},{8,10},{9,11},{10,... | collective-permute-start | bytes 1769480 | tf_op jit(solution)/shard_map/ppermute | solution.py:20
  3.7 1.6 collective-permute-start.15
  5.2 2.6 %collective-permute-start.11 = (bf16[384,768]{1,0:T(8,128)(2,1)}, bf16[384,768]{1,0:T(8,128)(2,1)S(1)}, u32[]{:S(2)}, u32[]{:S(2)}) collective-permute-start(bf16[384,768]{1,0:T(8,128)(2,1)} %bitcast.39), channel_id=1, source_target_pairs={{0,8},{4,12},{8,0},{12,4},{1,9},{5,13},{9,1},{13,5},{2,10},{6,14},... | collective-permute-start | bytes 1769480 | tf_op jit(solution)/shard_map/ppermute | solution.py:20
  7.8 1.8 %slice_bitcast_fusion = bf16[256,768]{1,0:T(8,128)(2,1)} fusion(bf16[1,384,768]{2,1,0:T(8,128)(2,1)} %param.6), kind=kLoop, calls=%fused_computation.8 | loop fusion | bytes 786432 | tf_op jit(solution)/shard_map/slice | solution.py:221
  10.6 3.3 %constant_dynamic-slice_fusion.1 = (bf16[768,768]{1,0:T(8,128)(2,1)}, bf16[768,768]{1,0:T(8,128)(2,1)}) fusion(bf16[768,3072]{1,0:T(8,128)(2,1)} %refs_2_.7, s32[]{:T(128)S(6)} %select_n.18, s32[]{:T(128)S(6)} %select_n.19), kind=kLoop, calls=%fused_computation.22 | loop fusion | bytes 4718600 | tf_op jit(solution)/shard_map/dynamic_slice | solution.py:208
  13.9 0.7 slice_bitcast_fusion.1
  14.6 17.2 %collective-permute-done.15.refs_0_ = bf16[384,768]{1,0:T(8,128)(2,1)S(1)} collective-permute-done((bf16[384,768]{1,0:T(8,128)(2,1)}, bf16[384,768]{1,0:T(8,128)(2,1)S(1)}, u32[]{:S(2)}, u32[]{:S(2)}) %collective-permute-start.15) | collective-permute-done | bytes 589856 | tf_op jit(solution)/shard_map/ppermute | solution.py:20
  32.3 11.3 %collective-permute-done.11.refs_0_ = bf16[384,768]{1,0:T(8,128)(2,1)S(1)} collective-permute-done((bf16[384,768]{1,0:T(8,128)(2,1)}, bf16[384,768]{1,0:T(8,128)(2,1)S(1)}, u32[]{:S(2)}, u32[]{:S(2)}) %collective-permute-start.11) | collective-permute-done | bytes 589856 | tf_op jit(solution)/shard_map/ppermute | solution.py:20
  43.6 0.5 collective-permute-start.13
  44.6 3.6 %collective-permute-done.17.refs_2_ = bf16[384,768]{1,0:T(8,128)(2,1)} collective-permute-done((bf16[384,768]{1,0:T(8,128)(2,1)S(1)}, bf16[384,768]{1,0:T(8,128)(2,1)}, u32[]{:S(2)}, u32[]{:S(2)}) %collective-permute-start.17) | collective-permute-done | bytes 589856 | tf_op jit(solution)/shard_map/ppermute | solution.py:20
  48.3 24.4 %all_gather.3 = bf16[16,2,768]{2,1,0:T(2,128)(2,1)S(1)} all-gather(bf16[1,2,768]{2,1,0:T(2,128)(2,1)S(1)} %slice.51), channel_id=1, replica_groups=mesh['grp'=2,'pb'=4,'ha'=4] {'pb','ha'}, dimensions={0}, use_global_device_ids=true | all-gather | bytes 52224 | tf_op jit(solution)/shard_map/all_gather | solution.py:204
  73.4 16.3 %shard_map.77 = (bf16[384,768]{1,0:T(8,128)(2,1)S(1)}, f32[384,768]{1,0:T(8,128)S(1)}, f32[384,768]{1,0:T(8,128)S(1)}) custom-call(s32[2]{0:T(128)S(1)} %pad_add_fusion.ids_ref, bf16[384,768]{1,0:T(8,128)(2,1)S(1)} %bitcast.40, bf16[384,768]{1,0:T(8,128)(2,1)} %collective-permute-done.4.refs_1_, bf16[384,768]{1,0:T(8,128)(2,1)S(1)} %collective-permute-done.5.refs_2_, ...), custom_call_target="tpu_custom_call" | custom-call | flops 5888802816 | bytes 14155776 | tf_op jit(solution)/shard_map/pallas_call | solution.py:135
  90.5 12.3 %shard_map.78 = (f32[384,768]{1,0:T(8,128)S(1)}, f32[384,768]{1,0:T(8,128)S(1)}) custom-call(s32[2]{0:T(128)S(1)} %pad_add_fusion.3.ids_ref, bf16[384,768]{1,0:T(8,128)(2,1)S(1)} %collective-permute-done.15.refs_0_, bf16[384,768]{1,0:T(8,128)(2,1)S(1)} %collective-permute-done.16.refs_1_, bf16[384,768]{1,0:T(8,128)(2,1)} %collective-permute-done.17.refs_2_, ...), custom_call_target="tpu_custom_call" | custom-call | flops 4076863488 | bytes 9437184 | tf_op jit(solution)/shard_map/pallas_call | solution.py:135
  103.4 1.8 %collective-permute-start.2 = (bf16[128,768]{1,0:T(8,128)(2,1)S(1)}, bf16[128,768]{1,0:T(8,128)(2,1)S(1)}, u32[]{:S(2)}, u32[]{:S(2)}) collective-permute-start(bf16[128,768]{1,0:T(8,128)(2,1)S(1)} %collective-permute-done.refs_0_), channel_id=1, source_target_pairs={{0,2},{1,3},{2,0},{3,1},{4,6},{5,7},{6,4},{7,5},{8,10},{9,11},{10,... | collective-permute-start | bytes 589832 | tf_op jit(solution)/shard_map/ppermute | solution.py:20
  105.2 12.2 %shard_map.79 = (f32[384,768]{1,0:T(8,128)S(1)}, f32[384,768]{1,0:T(8,128)S(1)}) custom-call(s32[2]{0:T(128)S(1)} %pad_add_fusion.2.ids_ref, bf16[384,768]{1,0:T(8,128)(2,1)S(1)} %collective-permute-done.11.refs_0_, bf16[384,768]{1,0:T(8,128)(2,1)S(1)} %collective-permute-done.12.refs_1_, bf16[384,768]{1,0:T(8,128)(2,1)} %collective-permute-done.13.refs_2_, ...), custom_call_target="tpu_custom_call" | custom-call | flops 4076863488 | bytes 9437184 | tf_op jit(solution)/shard_map/pallas_call | solution.py:135
  117.5 0.5 collective-permute-start.3
  118.0 9.8 %shard_map.80 = (f32[384,768]{1,0:T(8,128)S(1)}, f32[384,768]{1,0:T(8,128)S(1)}) custom-call(s32[2]{0:T(128)S(1)} %pad_add_fusion.1.ids_ref, bf16[256,768]{1,0:T(8,128)(2,1)} %collective-permute-done.7.refs_0_, bf16[256,768]{1,0:T(8,128)(2,1)S(1)} %collective-permute-done.8.refs_1_, bf16[256,768]{1,0:T(8,128)(2,1)S(1)} %collective-permute-done.9.refs_2_, ...), custom_call_target="tpu_custom_call" | custom-call | flops 2717908992 | bytes 9437184 | tf_op jit(solution)/shard_map/pallas_call | solution.py:135
  127.8 7.8 %shard_map.81 = bf16[384,768]{1,0:T(8,128)(2,1)S(1)} custom-call(s32[2]{0:T(128)S(1)} %pad_add_fusion.1.ids_ref, bf16[128,768]{1,0:T(8,128)(2,1)S(1)} %collective-permute-done.refs_0_, bf16[128,768]{1,0:T(8,128)(2,1)S(1)} %collective-permute-done.1.refs_1_, bf16[128,768]{1,0:T(8,128)(2,1)S(1)} %collective-permute-done.2.refs_2_, ...), custom_call_target="tpu_custom_call" | custom-call | flops 1358954496 | bytes 9437184 | tf_op jit(solution)/shard_map/pallas_call | solution.py:135
  136.2 1.1 collective-permute-done.23.refs_1_
  137.3 1.2 shard_map.84
  138.7 1.2 shard_map.82
  139.9 1.9 %collective-permute-start.21 = (bf16[192,768]{1,0:T(8,128)(2,1)S(1)}, bf16[192,768]{1,0:T(8,128)(2,1)S(1)}, u32[]{:S(2)}, u32[]{:S(2)}) collective-permute-start(bf16[192,768]{1,0:T(8,128)(2,1)S(1)} %shard_map.82), channel_id=1, source_target_pairs={{0,2},{1,3},{2,0},{3,1},{4,6},{5,7},{6,4},{7,5},{8,10},{9,11},{10,... | collective-permute-start | bytes 884744 | tf_op jit(solution)/shard_map/ppermute | solution.py:20
  141.9 1.2 shard_map.85
  143.0 1.2 shard_map.83
  144.2 4.2 %collective-permute-done.24 = bf16[192,768]{1,0:T(8,128)(2,1)S(1)} collective-permute-done((bf16[192,768]{1,0:T(8,128)(2,1)S(1)}, bf16[192,768]{1,0:T(8,128)(2,1)S(1)}, u32[]{:S(2)}, u32[]{:S(2)}) %collective-permute-start.24) | collective-permute-done | bytes 294944 | tf_op jit(solution)/shard_map/ppermute | solution.py:20
  148.4 5.5 %collective-permute-done.21 = bf16[192,768]{1,0:T(8,128)(2,1)S(1)} collective-permute-done((bf16[192,768]{1,0:T(8,128)(2,1)S(1)}, bf16[192,768]{1,0:T(8,128)(2,1)S(1)}, u32[]{:S(2)}, u32[]{:S(2)}) %collective-permute-start.21) | collective-permute-done | bytes 294944 | tf_op jit(solution)/shard_map/ppermute | solution.py:20
  154.2 1.4 collective-permute-start.25
  155.6 1.3 collective-permute-start.26
  156.9 0.9 maximum_bitcast_fusion
  157.8 8.4 %collective-permute-done.25 = bf16[192,768]{1,0:T(8,128)(2,1)S(1)} collective-permute-done((bf16[192,768]{1,0:T(8,128)(2,1)S(1)}, bf16[192,768]{1,0:T(8,128)(2,1)S(1)}, u32[]{:S(2)}, u32[]{:S(2)}) %collective-permute-start.25) | collective-permute-done | bytes 294944 | tf_op jit(solution)/shard_map/ppermute | solution.py:26
  166.2 4.6 %collective-permute-done.26 = bf16[192,768]{1,0:T(8,128)(2,1)S(1)} collective-permute-done((bf16[192,768]{1,0:T(8,128)(2,1)S(1)}, bf16[192,768]{1,0:T(8,128)(2,1)S(1)}, u32[]{:S(2)}, u32[]{:S(2)}) %collective-permute-start.26) | collective-permute-done | bytes 294944 | tf_op jit(solution)/shard_map/ppermute | solution.py:26
  170.8 0.9 maximum_bitcast_fusion.1
  (69 shorter events, 4.7 us)
Async XLA Ops:
  0.6 43.6 %copy-start = (bf16[256,3,768]{2,0,1:T(8,128)(2,1)S(1)}, bf16[256,3,768]{2,0,1:T(8,128)(2,1)}, u32[]{:S(2)}) copy-start(bf16[256,3,768]{2,0,1:T(8,128)(2,1)} %param.8) | copy-start | bytes 3538948
  0.6 31.6 %collective-permute-start.5 = (bf16[384,768]{1,0:T(8,128)(2,1)}, bf16[384,768]{1,0:T(8,128)(2,1)S(1)}, u32[]{:S(2)}, u32[]{:S(2)}) collective-permute-start(bf16[384,768]{1,0:T(8,128)(2,1)} %bitcast.36), channel_id=1, source_target_pairs={{0,2},{1,3},{2,0},{3,1},{4,6},{5,7},{6,4},{7,5},{8,10},{9,11},{10,... | collective-permute-start | bytes 1769480 | tf_op jit(solution)/shard_map/ppermute | solution.py:20
  3.6 69.0 %collective-permute-start.4 = (bf16[384,768]{1,0:T(8,128)(2,1)}, bf16[384,768]{1,0:T(8,128)(2,1)}, u32[]{:S(2)}, u32[]{:S(2)}) collective-permute-start(bf16[384,768]{1,0:T(8,128)(2,1)} %bitcast.37), channel_id=1, source_target_pairs={{0,1},{1,0},{2,3},{3,2},{4,5},{5,4},{6,7},{7,6},{8,9},{9,8},{10,11... | collective-permute-start | bytes 1769480 | tf_op jit(solution)/shard_map/ppermute | solution.py:20
  3.7 28.2 %collective-permute-start.15 = (bf16[384,768]{1,0:T(8,128)(2,1)}, bf16[384,768]{1,0:T(8,128)(2,1)S(1)}, u32[]{:S(2)}, u32[]{:S(2)}) collective-permute-start(bf16[384,768]{1,0:T(8,128)(2,1)} %bitcast.38), channel_id=1, source_target_pairs={{0,4},{4,0},{8,12},{12,8},{1,5},{5,1},{9,13},{13,9},{2,6},{6,2},{1... | collective-permute-start | bytes 1769480 | tf_op jit(solution)/shard_map/ppermute | solution.py:20
  5.2 38.4 %collective-permute-start.11 = (bf16[384,768]{1,0:T(8,128)(2,1)}, bf16[384,768]{1,0:T(8,128)(2,1)S(1)}, u32[]{:S(2)}, u32[]{:S(2)}) collective-permute-start(bf16[384,768]{1,0:T(8,128)(2,1)} %bitcast.39), channel_id=1, source_target_pairs={{0,8},{4,12},{8,0},{12,4},{1,9},{5,13},{9,1},{13,5},{2,10},{6,14},... | collective-permute-start | bytes 1769480 | tf_op jit(solution)/shard_map/ppermute | solution.py:20
  9.6 34.9 %collective-permute-start.7 = (bf16[256,768]{1,0:T(8,128)(2,1)}, bf16[256,768]{1,0:T(8,128)(2,1)}, u32[]{:S(2)}, u32[]{:S(2)}) collective-permute-start(bf16[256,768]{1,0:T(8,128)(2,1)} %slice_bitcast_fusion), channel_id=1, source_target_pairs={{0,12},{4,8},{8,4},{12,0},{1,13},{5,9},{9,5},{13,1},{2,14},{6,10},... | collective-permute-start | bytes 1179656 | tf_op jit(solution)/shard_map/ppermute | solution.py:20
  31.8 16.3 %collective-permute-start.17 = (bf16[384,768]{1,0:T(8,128)(2,1)S(1)}, bf16[384,768]{1,0:T(8,128)(2,1)}, u32[]{:S(2)}, u32[]{:S(2)}) collective-permute-start(bf16[384,768]{1,0:T(8,128)(2,1)S(1)} %collective-permute-done.15.refs_0_), channel_id=1, source_target_pairs={{0,2},{1,3},{2,0},{3,1},{4,6},{5,7},{6,4},{7,5},{8,10},{9,11},{10,... | collective-permute-start | bytes 1769480 | tf_op jit(solution)/shard_map/ppermute | solution.py:20
  32.3 40.5 %collective-permute-start.6 = (bf16[384,768]{1,0:T(8,128)(2,1)S(1)}, bf16[384,768]{1,0:T(8,128)(2,1)}, u32[]{:S(2)}, u32[]{:S(2)}) collective-permute-start(bf16[384,768]{1,0:T(8,128)(2,1)S(1)} %collective-permute-done.5.refs_2_), channel_id=1, source_target_pairs={{0,1},{1,0},{2,3},{3,2},{4,5},{5,4},{6,7},{7,6},{8,9},{9,8},{10,11... | collective-permute-start | bytes 1769480 | tf_op jit(solution)/shard_map/ppermute | solution.py:20
  43.6 29.6 %collective-permute-start.13 = (bf16[384,768]{1,0:T(8,128)(2,1)S(1)}, bf16[384,768]{1,0:T(8,128)(2,1)}, u32[]{:S(2)}, u32[]{:S(2)}) collective-permute-start(bf16[384,768]{1,0:T(8,128)(2,1)S(1)} %collective-permute-done.11.refs_0_), channel_id=1, source_target_pairs={{0,2},{1,3},{2,0},{3,1},{4,6},{5,7},{6,4},{7,5},{8,10},{9,11},{10,... | collective-permute-start | bytes 1769480 | tf_op jit(solution)/shard_map/ppermute | solution.py:20
  44.5 45.4 %collective-permute-start.16 = (bf16[384,768]{1,0:T(8,128)(2,1)S(1)}, bf16[384,768]{1,0:T(8,128)(2,1)S(1)}, u32[]{:S(2)}, u32[]{:S(2)}) collective-permute-start(bf16[384,768]{1,0:T(8,128)(2,1)S(1)} %collective-permute-done.15.refs_0_), channel_id=1, source_target_pairs={{0,1},{1,0},{2,3},{3,2},{4,5},{5,4},{6,7},{7,6},{8,9},{9,8},{10,11... | collective-permute-start | bytes 1769480 | tf_op jit(solution)/shard_map/ppermute | solution.py:20
  48.2 42.0 %collective-permute-start.18 = (bf16[384,768]{1,0:T(8,128)(2,1)}, bf16[384,768]{1,0:T(8,128)(2,1)S(1)}, u32[]{:S(2)}, u32[]{:S(2)}) collective-permute-start(bf16[384,768]{1,0:T(8,128)(2,1)} %collective-permute-done.17.refs_2_), channel_id=1, source_target_pairs={{0,1},{1,0},{2,3},{3,2},{4,5},{5,4},{6,7},{7,6},{8,9},{9,8},{10,11... | collective-permute-start | bytes 1769480 | tf_op jit(solution)/shard_map/ppermute | solution.py:20
  72.7 17.0 %collective-permute-start.9 = (bf16[256,768]{1,0:T(8,128)(2,1)}, bf16[256,768]{1,0:T(8,128)(2,1)S(1)}, u32[]{:S(2)}, u32[]{:S(2)}) collective-permute-start(bf16[256,768]{1,0:T(8,128)(2,1)} %collective-permute-done.7.refs_0_), channel_id=1, source_target_pairs={{0,2},{1,3},{2,0},{3,1},{4,6},{5,7},{6,4},{7,5},{8,10},{9,11},{10,... | collective-permute-start | bytes 1179656 | tf_op jit(solution)/shard_map/ppermute | solution.py:20
  72.8 30.3 %collective-permute-start.12 = (bf16[384,768]{1,0:T(8,128)(2,1)S(1)}, bf16[384,768]{1,0:T(8,128)(2,1)S(1)}, u32[]{:S(2)}, u32[]{:S(2)}) collective-permute-start(bf16[384,768]{1,0:T(8,128)(2,1)S(1)} %collective-permute-done.11.refs_0_), channel_id=1, source_target_pairs={{0,1},{1,0},{2,3},{3,2},{4,5},{5,4},{6,7},{7,6},{8,9},{9,8},{10,11... | collective-permute-start | bytes 1769480 | tf_op jit(solution)/shard_map/ppermute | solution.py:20
  73.2 30.2 %collective-permute-start.14 = (bf16[384,768]{1,0:T(8,128)(2,1)}, bf16[384,768]{1,0:T(8,128)(2,1)S(1)}, u32[]{:S(2)}, u32[]{:S(2)}) collective-permute-start(bf16[384,768]{1,0:T(8,128)(2,1)} %collective-permute-done.13.refs_2_), channel_id=1, source_target_pairs={{0,1},{1,0},{2,3},{3,2},{4,5},{5,4},{6,7},{7,6},{8,9},{9,8},{10,11... | collective-permute-start | bytes 1769480 | tf_op jit(solution)/shard_map/ppermute | solution.py:20
  73.4 16.3 %copy-start.5 = (bf16[128,768]{1,0:T(8,128)(2,1)S(1)}, bf16[128,768]{1,0:T(8,128)(2,1)}, u32[]{:S(2)}) copy-start(bf16[128,768]{1,0:T(8,128)(2,1)} %slice_bitcast_fusion.1) | copy-start | bytes 589828
  89.7 13.1 %collective-permute-start = (bf16[128,768]{1,0:T(8,128)(2,1)S(1)}, bf16[128,768]{1,0:T(8,128)(2,1)S(1)}, u32[]{:S(2)}, u32[]{:S(2)}) collective-permute-start(bf16[128,768]{1,0:T(8,128)(2,1)S(1)} %copy-done.5), channel_id=1, source_target_pairs={{0,12},{4,8},{8,4},{12,0},{1,13},{5,9},{9,5},{13,1},{2,14},{6,10},... | collective-permute-start | bytes 589832 | tf_op jit(solution)/shard_map/ppermute | solution.py:20
  90.0 27.5 %collective-permute-start.8 = (bf16[256,768]{1,0:T(8,128)(2,1)}, bf16[256,768]{1,0:T(8,128)(2,1)S(1)}, u32[]{:S(2)}, u32[]{:S(2)}) collective-permute-start(bf16[256,768]{1,0:T(8,128)(2,1)} %collective-permute-done.7.refs_0_), channel_id=1, source_target_pairs={{0,1},{1,0},{2,3},{3,2},{4,5},{5,4},{6,7},{7,6},{8,9},{9,8},{10,11... | collective-permute-start | bytes 1179656 | tf_op jit(solution)/shard_map/ppermute | solution.py:20
  90.2 27.8 %collective-permute-start.10 = (bf16[256,768]{1,0:T(8,128)(2,1)S(1)}, bf16[256,768]{1,0:T(8,128)(2,1)S(1)}, u32[]{:S(2)}, u32[]{:S(2)}) collective-permute-start(bf16[256,768]{1,0:T(8,128)(2,1)S(1)} %collective-permute-done.9.refs_2_), channel_id=1, source_target_pairs={{0,1},{1,0},{2,3},{3,2},{4,5},{5,4},{6,7},{7,6},{8,9},{9,8},{10,11... | collective-permute-start | bytes 1179656 | tf_op jit(solution)/shard_map/ppermute | solution.py:20
  90.5 12.3 %copy-start.3 = (bf16[768,768]{1,0:T(8,128)(2,1)S(1)}, bf16[768,768]{1,0:T(8,128)(2,1)}, u32[]{:S(2)}) copy-start(bf16[768,768]{1,0:T(8,128)(2,1)} %get-tuple-element.20) | copy-start | bytes 3538948
  90.5 12.6 %copy-start.2 = (bf16[768,768]{1,0:T(8,128)(2,1)S(1)}, bf16[768,768]{1,0:T(8,128)(2,1)}, u32[]{:S(2)}) copy-start(bf16[768,768]{1,0:T(8,128)(2,1)} %get-tuple-element.21) | copy-start | bytes 3538948
  102.8 33.4 %collective-permute-start.20 = (bf16[768,768]{1,0:T(8,128)(2,1)S(1)}, bf16[768,768]{1,0:T(8,128)(2,1)S(1)}, u32[]{:S(2)}, u32[]{:S(2)}) collective-permute-start(bf16[768,768]{1,0:T(8,128)(2,1)S(1)} %copy-done.3), channel_id=1, source_target_pairs={{0,1},{1,0},{2,3},{3,2},{4,5},{5,4},{6,7},{7,6},{8,9},{9,8},{10,11... | collective-permute-start | bytes 3538952 | tf_op jit(solution)/shard_map/ppermute | solution.py:20
  103.1 38.8 %collective-permute-start.22 = (bf16[768,768]{1,0:T(8,128)(2,1)S(1)}, bf16[768,768]{1,0:T(8,128)(2,1)S(1)}, u32[]{:S(2)}, u32[]{:S(2)}) collective-permute-start(bf16[768,768]{1,0:T(8,128)(2,1)S(1)} %copy-done.2), channel_id=1, source_target_pairs={{0,1},{1,0},{2,3},{3,2},{4,5},{5,4},{6,7},{7,6},{8,9},{9,8},{10,11... | collective-permute-start | bytes 3538952 | tf_op jit(solution)/shard_map/ppermute | solution.py:20
  103.4 14.0 %collective-permute-start.2 = (bf16[128,768]{1,0:T(8,128)(2,1)S(1)}, bf16[128,768]{1,0:T(8,128)(2,1)S(1)}, u32[]{:S(2)}, u32[]{:S(2)}) collective-permute-start(bf16[128,768]{1,0:T(8,128)(2,1)S(1)} %collective-permute-done.refs_0_), channel_id=1, source_target_pairs={{0,2},{1,3},{2,0},{3,1},{4,6},{5,7},{6,4},{7,5},{8,10},{9,11},{10,... | collective-permute-start | bytes 589832 | tf_op jit(solution)/shard_map/ppermute | solution.py:20
  117.4 10.4 %collective-permute-start.1 = (bf16[128,768]{1,0:T(8,128)(2,1)S(1)}, bf16[128,768]{1,0:T(8,128)(2,1)S(1)}, u32[]{:S(2)}, u32[]{:S(2)}) collective-permute-start(bf16[128,768]{1,0:T(8,128)(2,1)S(1)} %collective-permute-done.refs_0_), channel_id=1, source_target_pairs={{0,1},{1,0},{2,3},{3,2},{4,5},{5,4},{6,7},{7,6},{8,9},{9,8},{10,11... | collective-permute-start | bytes 589832 | tf_op jit(solution)/shard_map/ppermute | solution.py:20
  117.5 10.3 %collective-permute-start.3 = (bf16[128,768]{1,0:T(8,128)(2,1)S(1)}, bf16[128,768]{1,0:T(8,128)(2,1)S(1)}, u32[]{:S(2)}, u32[]{:S(2)}) collective-permute-start(bf16[128,768]{1,0:T(8,128)(2,1)S(1)} %collective-permute-done.2.refs_2_), channel_id=1, source_target_pairs={{0,1},{1,0},{2,3},{3,2},{4,5},{5,4},{6,7},{7,6},{8,9},{9,8},{10,11... | collective-permute-start | bytes 589832 | tf_op jit(solution)/shard_map/ppermute | solution.py:20
  135.6 1.6 collective-permute-start.23
  135.8 2.9 %collective-permute-start.19 = (bf16[192,768]{1,0:T(8,128)(2,1)S(1)}, bf16[192,768]{1,0:T(8,128)(2,1)S(1)}, u32[]{:S(2)}, u32[]{:S(2)}) collective-permute-start(bf16[192,768]{1,0:T(8,128)(2,1)S(1)} %get-tuple-element.26.refs_0_), channel_id=1, source_target_pairs={{0,1},{1,0},{2,3},{3,2},{4,5},{5,4},{6,7},{7,6},{8,9},{9,8},{10,11... | collective-permute-start | bytes 884744 | tf_op jit(solution)/shard_map/ppermute | solution.py:20
  138.5 9.9 %collective-permute-start.24 = (bf16[192,768]{1,0:T(8,128)(2,1)S(1)}, bf16[192,768]{1,0:T(8,128)(2,1)S(1)}, u32[]{:S(2)}, u32[]{:S(2)}) collective-permute-start(bf16[192,768]{1,0:T(8,128)(2,1)S(1)} %shard_map.84), channel_id=1, source_target_pairs={{0,2},{1,3},{2,0},{3,1},{4,6},{5,7},{6,4},{7,5},{8,10},{9,11},{10,... | collective-permute-start | bytes 884744 | tf_op jit(solution)/shard_map/ppermute | solution.py:20
  139.9 14.0 %collective-permute-start.21 = (bf16[192,768]{1,0:T(8,128)(2,1)S(1)}, bf16[192,768]{1,0:T(8,128)(2,1)S(1)}, u32[]{:S(2)}, u32[]{:S(2)}) collective-permute-start(bf16[192,768]{1,0:T(8,128)(2,1)S(1)} %shard_map.82), channel_id=1, source_target_pairs={{0,2},{1,3},{2,0},{3,1},{4,6},{5,7},{6,4},{7,5},{8,10},{9,11},{10,... | collective-permute-start | bytes 884744 | tf_op jit(solution)/shard_map/ppermute | solution.py:20
  154.2 16.6 %copy-start.4 = (bf16[384,768]{1,0:T(8,128)(2,1)S(1)}, bf16[384,768]{1,0:T(8,128)(2,1)}, u32[]{:S(2)}) copy-start(bf16[384,768]{1,0:T(8,128)(2,1)} %param.11) | copy-start | bytes 1769476
  154.2 12.0 %collective-permute-start.25 = (bf16[192,768]{1,0:T(8,128)(2,1)S(1)}, bf16[192,768]{1,0:T(8,128)(2,1)S(1)}, u32[]{:S(2)}, u32[]{:S(2)}) collective-permute-start(bf16[192,768]{1,0:T(8,128)(2,1)S(1)} %get-tuple-element.22), channel_id=1, source_target_pairs={{4,0},{8,4},{12,8},{5,1},{9,5},{13,9},{6,2},{10,6},{14,10},{7,3},{... | collective-permute-start | bytes 884744 | tf_op jit(solution)/shard_map/ppermute | solution.py:26
  155.6 15.1 %collective-permute-start.26 = (bf16[192,768]{1,0:T(8,128)(2,1)S(1)}, bf16[192,768]{1,0:T(8,128)(2,1)S(1)}, u32[]{:S(2)}, u32[]{:S(2)}) collective-permute-start(bf16[192,768]{1,0:T(8,128)(2,1)S(1)} %get-tuple-element.23), channel_id=1, source_target_pairs={{4,0},{8,4},{12,8},{5,1},{9,5},{13,9},{6,2},{10,6},{14,10},{7,3},{... | collective-permute-start | bytes 884744 | tf_op jit(solution)/shard_map/ppermute | solution.py:26
  (3 other events, 22.3 us)

commit v2 on v0

v2 whole, which is shorter than its diff:
```python
import functools
import math

import jax
import jax.numpy as jnp
from jax import lax
from jax.experimental import pallas as pl
from jax.experimental.pallas import tpu as pltpu
from jax.sharding import PartitionSpec as P

HD = 128
TDIM = 256
F32 = jnp.float32
BF16 = jnp.bfloat16
VMEM_LIMIT = 20 * 1024 * 1024
MOD_ROWS = 16


def flip(x, axis, bit):
    size = lax.axis_size(axis)
    return lax.ppermute(x, axis, [(i, i ^ bit) for i in range(size)])


def from_behind(x, axis, by):
    size = lax.axis_size(axis)
    pairs = [(i, i + by) for i in range(size) if 0 <= i + by < size]
    return lax.ppermute(x, axis, pairs)


def sinusoid(timesteps):
    half_width = TDIM // 2
    frequency = jnp.exp(-math.log(10000.0) * jnp.arange(half_width, dtype=F32) / half_width)
    angles = timesteps.astype(F32)[:, None] * frequency[None, :]
    return jnp.concatenate([jnp.cos(angles), jnp.sin(angles)], axis=1)


def unit_rms(vectors):
    return vectors * lax.rsqrt(jnp.mean(vectors * vectors, axis=-1, keepdims=True) + 1e-06)


def norm_rows(ha, piece_refs, mod_refs, offset, hidden_ref, scale_ref, shift_ref):
    count = len(piece_refs)
    rows, full = hidden_ref.shape
    width = full // count
    step = 64
    spots = []
    for j in range(count):
        spot = pl.ds(pl.multiple_of(lax.bitwise_xor(ha, j) * width, HD), width)
        mod = mod_refs[j][0:MOD_ROWS, :].astype(F32)
        shift_ref[j] = jnp.broadcast_to(mod[0:1], (8, width))
        scale_ref[j] = jnp.broadcast_to(1.0 + mod[1:2], (8, width))
        spots.append(spot)

    def one(i, carry):
        at = pl.ds(pl.multiple_of(offset + i * step, 16), step)
        to = pl.ds(pl.multiple_of(i * step, step), step)

        def sum_rows(parts):
            total = None
            for part in parts:
                for k in range(0, width, HD):
                    tile = part[:, k : k + HD]
                    total = tile if total is None else total + tile
            return jnp.sum(total, axis=-1, keepdims=True) * (1.0 / full)

        mean = sum_rows(ref[at, :].astype(F32) for ref in piece_refs)
        inverse = lax.rsqrt(sum_rows(jnp.square(ref[at, :].astype(F32) - mean) for ref in piece_refs) + 1e-06)
        for j, ref in enumerate(piece_refs):
            normed = ((ref[at, :].astype(F32) - mean) * inverse).reshape(step // 8, 8, width)
            out = normed * scale_ref[j][None] + shift_ref[j][None]
            hidden_ref[to, spots[j]] = out.reshape(step, width).astype(BF16)
        return carry

    lax.fori_loop(0, rows // step, one, 0)


def attend(q, k, v, num, den):
    scores = lax.dot_general(q, k, (((1,), (1,)), ((), ())), preferred_element_type=F32)
    weights = jnp.exp(scores)
    for start in range(0, weights.shape[1], HD):
        part = weights[:, start : start + HD]
        if part.shape[1] < HD:
            part = jnp.concatenate([part, jnp.zeros((part.shape[0], HD - part.shape[1]), F32)], axis=1)
        den = part if den is None else den + part
    more = jnp.dot(weights.astype(BF16), v, preferred_element_type=F32)
    return more if num is None else num + more, den


def frame_body(own, last, count, offset, separate, ids_ref, *refs):
    refs = list(refs)
    pieces, refs = refs[:count], refs[count:]
    mods = pieces
    if separate:
        mods, refs = refs[:count], refs[count:]
    weight_ref, refs = refs[0], refs[1:]
    hidden_ref, scale_ref, shift_ref = refs[-3:]
    if own:
        q_out, num_out, den_out = refs[:-3]
    elif last:
        q_ref, num_ref, den_ref, att_out = refs[:-3]
    else:
        q_ref, num_ref, den_ref, num_out, den_out = refs[:-3]
    norm_rows(ids_ref[0], pieces, mods, offset, hidden_ref, scale_ref, shift_ref)
    width = weight_ref.shape[2]
    block = 2 * HD if width % (2 * HD) == 0 else HD
    for start in range(0, width, block):
        hidden = hidden_ref[...]
        columns = slice(start, start + block)
        key_all = jnp.dot(hidden, weight_ref[1, :, columns], preferred_element_type=F32)
        value_all = jnp.dot(hidden, weight_ref[2, :, columns], preferred_element_type=F32)
        query_all = jnp.dot(hidden, weight_ref[0, :, columns], preferred_element_type=F32) if own else None
        for head in range(0, block, HD):
            inner = slice(head, head + HD)
            at = slice(start + head, start + head + HD)
            k = unit_rms(key_all[:, inner]).astype(BF16)
            v = value_all[:, inner].astype(BF16)
            if own:
                q = (unit_rms(query_all[:, inner]) * (1.0 / math.sqrt(HD))).astype(BF16)
                q_out[:, at] = q
                num, den = attend(q, k, v, None, None)
            else:
                num, den = attend(q_ref[:, at], k, v, num_ref[:, at], den_ref[:, at])
            if last:
                att_out[:, at] = (num / jnp.sum(den, axis=-1, keepdims=True)).astype(BF16)
            else:
                num_out[:, at] = num
                den_out[:, at] = den


def frame_step(ids, pieces, mods, weight, state, last=False, offset=0):
    own = state is None
    count = len(pieces)
    width = pieces[0].shape[1]
    rows = pieces[0].shape[0] - offset
    full = weight.shape[1]
    queries = rows if own else state[0].shape[0]
    args = [*pieces, *(mods or ()), weight, *(state or ())]
    wide = jax.ShapeDtypeStruct((queries, width), F32)
    thin = jax.ShapeDtypeStruct((queries, width), BF16)
    outs = (thin, wide, wide) if own else (thin,) if last else (wide, wide)
    used = 3 if own else 2
    args = [pltpu.with_memory_space_constraint(x, pltpu.VMEM) if x is weight else x for x in args]
    vmem = pl.BlockSpec(memory_space=pltpu.VMEM)
    return pl.pallas_call(
        functools.partial(frame_body, own, last, count, offset, mods is not None),
        in_specs=[pl.BlockSpec(memory_space=pltpu.SMEM)] + [vmem] * len(args),
        out_specs=tuple(vmem for _ in outs),
        scratch_shapes=[
            pltpu.VMEM((rows, full), BF16),
            pltpu.VMEM((count, 8, width), F32),
            pltpu.VMEM((count, 8, width), F32),
        ],
        out_shape=outs,
        compiler_params=pltpu.CompilerParams(vmem_limit_bytes=VMEM_LIMIT),
        cost_estimate=pl.CostEstimate(
            flops=rows * full * width // 8, bytes_accessed=rows * full // 8, transcendentals=0
        ),
    )(ids, *args)


def fetch_body(ids_ref, weight_ref, out_ref, weight_out, out_out, *rest):
    *column_outs, sems = rest
    width = out_ref.shape[0]
    copies = [
        pltpu.make_async_copy(weight_ref, weight_out, sems.at[0]),
        pltpu.make_async_copy(out_ref, out_out, sems.at[1]),
    ]
    for n, column_out in enumerate(column_outs):
        at = pl.ds(pl.multiple_of(lax.bitwise_xor(ids_ref[0], 2 * n + 1) * width, HD), width)
        copies.append(pltpu.make_async_copy(out_ref.at[:, at], column_out, sems.at[n + 2]))
    for copy in copies:
        copy.start()
    for copy in copies:
        copy.wait()


def fetch(ids, weight, out_weight, ha_size):
    width = out_weight.shape[0]
    columns = ha_size // 2
    anywhere, vmem = pl.BlockSpec(memory_space=pltpu.HBM), pl.BlockSpec(memory_space=pltpu.VMEM)
    return pl.pallas_call(
        fetch_body,
        in_specs=[pl.BlockSpec(memory_space=pltpu.SMEM), anywhere, anywhere],
        out_specs=(vmem, vmem) + (anywhere,) * columns,
        out_shape=(pltpu.VMEM(weight.shape, weight.dtype), pltpu.VMEM(out_weight.shape, out_weight.dtype))
        + (jax.ShapeDtypeStruct((width, width), out_weight.dtype),) * columns,
        scratch_shapes=[pltpu.SemaphoreType.DMA((columns + 2,))],
        compiler_params=pltpu.CompilerParams(vmem_limit_bytes=VMEM_LIMIT),
        cost_estimate=pl.CostEstimate(flops=0, bytes_accessed=weight.size // 8, transcendentals=0),
    )(ids, weight, out_weight)


def project_body(step, ids_ref, mine_ref, theirs_ref, weight_ref, other_ref, out_ref):
    width = other_ref.shape[0]
    at = pl.ds(pl.multiple_of(lax.bitwise_xor(ids_ref[0], step) * width, HD), width)
    total = jnp.dot(mine_ref[...], weight_ref[:, at], preferred_element_type=F32)
    total = total + jnp.dot(theirs_ref[...], other_ref[...], preferred_element_type=F32)
    out_ref[...] = total.astype(out_ref.dtype)


def project(ids, mine, theirs, weight, other, step, dtype):
    rows, width = mine.shape
    vmem = pl.BlockSpec(memory_space=pltpu.VMEM)
    pin = lambda x: pltpu.with_memory_space_constraint(x, pltpu.VMEM)
    return pl.pallas_call(
        functools.partial(project_body, step),
        in_specs=[pl.BlockSpec(memory_space=pltpu.SMEM)] + [vmem] * 4,
        out_specs=vmem,
        out_shape=jax.ShapeDtypeStruct((rows, width), dtype),
        compiler_params=pltpu.CompilerParams(vmem_limit_bytes=VMEM_LIMIT),
        cost_estimate=pl.CostEstimate(
            flops=rows * width * width * (4 if step else 64), bytes_accessed=rows * width, transcendentals=0
        ),
    )(ids, mine, theirs, pin(weight), pin(other))


def cross(piece):
    size = lax.axis_size("ha")
    return [piece] + [flip(piece, "ha", step) for step in range(2, size, 2)]


def paired(pieces):
    return [shard for piece in pieces for shard in (piece, flip(piece, "ha", 1))]


def spread(piece):
    return paired(cross(piece))


def after_all(pieces, other):
    return [pieces[0]] + [after(piece, other) for piece in pieces[1:]]


def after(x, *others):
    return lax.optimization_barrier((x, *others))[0]


def on_device(latents, timesteps, mod_weight, qkv_weight, out_weight, noise_frame):
    frames, tok_count, width = latents.shape
    ha_size, pb_size = lax.axis_size("ha"), lax.axis_size("pb")
    ha, pb = lax.axis_index("ha"), lax.axis_index("pb")
    ids = jnp.stack([ha, pb]).astype(jnp.int32)
    piece = latents.reshape(tok_count, width)
    weight = jnp.transpose(qkv_weight, (1, 0, 2))

    embedding = sinusoid(timesteps).astype(BF16)
    modulation = jnp.einsum(
        "pe,jef->pjf", embedding, jnp.transpose(mod_weight, (1, 0, 2)), preferred_element_type=F32
    ).astype(BF16)
    gate = modulation[:, 2].astype(F32)
    mod_rows = jnp.pad(modulation[0, :2], ((0, MOD_ROWS - 2), (0, 0)))
    carried = jnp.concatenate([mod_rows, piece], axis=0)

    weight, out_local, *columns = fetch(after(ids, carried), weight, out_weight, ha_size)
    other_weight = [flip(c, "ha", 1) for c in columns]

    def frame(pieces, state, mods=None, last=False):
        got = frame_step(ids, pieces, mods, weight, state, last, 0 if mods else MOD_ROWS)
        return got[0] if last else got if state is None else (state[0], *got)

    half = MOD_ROWS + tok_count // 2
    if pb_size == 4:
        pairs, middle, outward = [(0, 1), (1, 0), (2, 3), (3, 2)], [(1, 2), (2, 1)], [(1, 0), (2, 3)]
        first = after(lax.ppermute(carried, "pb", pairs), weight)
        crossed = after(lax.ppermute(carried, "pb", middle), weight)
        own = cross(carried)
        first_over = cross(first)
        beyond = lax.ppermute(crossed, "pb", outward)
        passed = lax.ppermute(first, "pb", middle)
        state = frame(paired(after_all(own, weight)), None)
        beyond, passed = after(beyond, state[0]), after(passed, state[0])
        second = crossed + beyond
        second_over = cross(second)
        onward = lax.ppermute(passed, "pb", outward)
        state = frame(paired([after(p, state[0]) for p in first_over]), state)
        third = passed + after(onward, state[1])
        third_parts = [cross(third[:half]), cross(third[half:])]
        state = frame(paired([after(p, state[1]) for p in second_over]), state)
        pieces = paired([after(p, state[1]) for p in third_parts[0]])
        state = frame(pieces, state)
        attended = frame(paired([after(p, state[1]) for p in third_parts[1]]), state, pieces, True)
    else:
        state = frame(spread(carried), None)
        for bit in range(1, pb_size):
            state = frame(spread(flip(carried, "pb", bit)), state, None, bit == pb_size - 1)
        attended = state

    is_last = pb == pb_size - 1
    done, following = [], []
    chunk = tok_count // 3
    parts = []
    for start in range(0, tok_count, chunk):
        mine = attended[start : start + chunk]
        both = (mine, flip(mine, "ha", 1))
        sent = [
            flip(project(ids, *both, out_local, other_weight[step // 2], step, BF16), "ha", step)
            for step in range(2, ha_size, 2)
        ]
        parts.append((start, both, sent))
    for start, both, sent in parts:
        both = tuple(after(x, *done[-1:]) for x in both)
        branch = project(ids, *both, out_local, other_weight[0], 0, F32)
        for part in sent:
            part = after(part, *done[-1:])
            branch = branch + part.astype(F32)
        advanced = (piece[start : start + chunk].astype(F32) + gate * branch).astype(BF16)
        done.append(advanced)
        following.append(from_behind(advanced, "pb", -1))
    following = [
        jnp.where(is_last, noise_frame[n * chunk : (n + 1) * chunk], incoming) for n, incoming in enumerate(following)
    ]
    return jnp.concatenate(done, axis=0)[None], jnp.concatenate(following, axis=0)[None]


def solution(mesh):
    placed = (
        P(("grp", "pb"), None, "ha"),
        P(("grp", "pb")),
        P(None, None, "ha"),
        P(None, None, "ha"),
        P("ha", None),
        P("grp", "ha"),
    )
    return jax.shard_map(
        on_device,
        mesh=mesh,
        in_specs=placed,
        out_specs=(P(("grp", "pb"), None, "ha"), P(("grp", "pb"), None, "ha")),
        check_vma=False,
    )
```

time: 261 us -> 126 us (0.48)
  waiting for transfers between devices: 120 us -> 42.3 us
  local copies, waits for them, and re-layouts: 61.8 us -> 2.88 us
  Pallas kernels: 0 us -> 51.9 us
  matrix products: 36.4 us -> 0.27 us
  starting transfers between devices: 6.4 us -> 23.1 us
  between operations: 14.6 us -> 1.74 us
  other arithmetic: 13.4 us -> 3.6 us
  blocking collectives: 6.14 us -> 0 us
    all_gather x4 -> x0, waiting for transfers between devices: 103 us -> none  [the longest x1 51.5 us: on_device(): lax.all_gather(value_rows, 'pb', axis=0, tiled=True)]
    pallas_call x0 -> x12, Pallas kernels: none -> 51.9 us  [the longest x5 40.1 us: frame_step(): pl.pallas_call(functools.partial(frame_body, own, last, count, offset, mo...]
    dot_general x11 -> x1, matrix products: 36.4 us -> 0.27 us  [on_device(): jnp.einsum('pe,jef->pjf', embedding, jnp.transpose(mod_weight, (1, 0, 2))...]
    ppermute x0 -> x28, waiting for transfers between devices: none -> 30.6 us  [the longest x23 20.1 us: flip(): return lax.ppermute(x, axis, [(i, i ^ bit) for i in range(size)])]
    unnamed x18 -> x10, local copies, waits for them, and re-layouts: 28.6 us -> 2.77 us
    dynamic_slice x12 -> x0, local copies, waits for them, and re-layouts: 21.2 us -> none  [the longest x8 12.7 us: one_frame(): key_frame = lax.dynamic_index_in_dim(key_piece, position, 0, keepdims=False)]
    ppermute x0 -> x28, starting transfers between devices: none -> 19.1 us  [the longest x23 12.6 us: flip(): return lax.ppermute(x, axis, [(i, i ^ bit) for i in range(size)])]
    all_to_all x1 -> x0, local copies, waits for them, and re-layouts: 6.79 us -> none  [on_device(): lax.all_to_all(out_weight, 'ha', split_axis=1, concat_axis=0, tiled=True)]
  transfers between devices with their start and end apart: 6 -> 31, of which waited for: 5 -> 16; matrix products, arithmetic and copies ran while one was open for 34% -> 2% of each run, Pallas kernels for 0% -> 40%
where the time goes in v2:
time: 126 us
  Pallas kernels  51.9 us (41%)
  waiting for transfers between devices  42.3 us (34%)
  starting transfers between devices  23.1 us (18%)
  other arithmetic  3.6 us (3%)
  local copies, waits for them, and re-layouts  2.88 us (2%)
  between operations  1.74 us (1%)
    pallas_call x5, Pallas kernels, frame_step(): pl.pallas_call(functools.partial(frame_body, own, last, count, offset, mo...  40.1 us
    ppermute x23, waiting for transfers between devices, flip(): return lax.ppermute(x, axis, [(i, i ^ bit) for i in range(size)])  20.1 us
    ppermute x23, starting transfers between devices, flip(): return lax.ppermute(x, axis, [(i, i ^ bit) for i in range(size)])  12.6 us
    ppermute x3, waiting for transfers between devices, from_behind(): return lax.ppermute(x, axis, pairs)  11.7 us
    pallas_call x6, Pallas kernels, project(): pl.pallas_call(functools.partial(project_body, step), in_specs=[pl.BlockS...  6.21 us
    pallas_call x1, Pallas kernels, fetch(): pl.pallas_call(fetch_body, in_specs=[pl.BlockSpec(memory_space=pltpu.SMEM...  5.6 us
    ppermute x1, waiting for transfers between devices, on_device(): onward = lax.ppermute(passed, 'pb', outward)  5.52 us
    ppermute x3, starting transfers between devices, from_behind(): return lax.ppermute(x, axis, pairs)  4.01 us
  transfers between devices with their start and end apart: 31, of which 16 were waited for; matrix products, arithmetic and copies ran while one was open for 2% of the time, Pallas kernels for 40%

profile of v2, /device:TPU:0, one launch (start us, length us, event | category | flops | bytes accessed | tf_op | source)
XLA Modules:
  0.0 125.8 jit_solution(10055202521259711743)
XLA Ops:
  2.3 3.0 %collective-permute-start.3 = (bf16[400,768]{1,0:T(8,128)(2,1)S(1)}, bf16[400,768]{1,0:T(8,128)(2,1)S(1)}, u32[]{:S(2)}, u32[]{:S(2)}) collective-permute-start(bf16[400,768]{1,0:T(8,128)(2,1)S(1)} %fusion.3.refs_0_), channel_id=1, source_target_pairs={{0,2},{1,3},{2,0},{3,1},{4,6},{5,7},{6,4},{7,5},{8,10},{9,11},{10,... | collective-permute-start | bytes 1843208 | tf_op jit(solution)/shard_map/ppermute | solution.py:21
  5.3 1.6 %collective-permute-start = (bf16[400,768]{1,0:T(8,128)(2,1)S(1)}, bf16[400,768]{1,0:T(8,128)(2,1)S(1)}, u32[]{:S(2)}, u32[]{:S(2)}) collective-permute-start(bf16[400,768]{1,0:T(8,128)(2,1)S(1)} %fusion.3.refs_0_), channel_id=1, source_target_pairs={{0,4},{4,0},{8,12},{12,8},{1,5},{5,1},{9,13},{13,9},{2,6},{6,2},{1... | collective-permute-start | bytes 1843208 | tf_op jit(solution)/shard_map/ppermute | solution.py:264
  6.9 1.5 %collective-permute-start.9 = (bf16[400,768]{1,0:T(8,128)(2,1)S(1)}, bf16[400,768]{1,0:T(8,128)(2,1)}, u32[]{:S(2)}, u32[]{:S(2)}) collective-permute-start(bf16[400,768]{1,0:T(8,128)(2,1)S(1)} %fusion.3.refs_0_), channel_id=1, source_target_pairs={{4,8},{8,4},{5,9},{9,5},{6,10},{10,6},{7,11},{11,7},{20,24},{24,20... | collective-permute-start | bytes 1843208 | tf_op jit(solution)/shard_map/ppermute | solution.py:265
  8.4 2.3 %copy-done.2 = bf16[768,3072]{1,0:T(8,128)(2,1)S(1)} copy-done((bf16[768,3072]{1,0:T(8,128)(2,1)S(1)}, bf16[768,3072]{1,0:T(8,128)(2,1)}, u32[]{:S(2)}) %copy-start.2) | copy-done | bytes 4718616
  10.8 5.6 %shard_map.77 = (bf16[3,3072,768]{2,1,0:T(8,128)(2,1)S(1)}, bf16[768,3072]{1,0:T(8,128)(2,1)S(1)}, bf16[768,768]{1,0:T(8,128)(2,1)S(1)}, bf16[768,768]{1,0:T(8,128)(2,1)S(1)}) custom-call(s32[2]{0:T(128)S(1)} %pad_add_fusion.ids_ref, bf16[3,3072,768]{2,1,0:T(8,128)(2,1)} %bitcast.32, bf16[768,3072]{1,0:T(8,128)(2,1)S(1)} %copy-done.2), custom_call_target="tpu_custom_call" | custom-call | bytes 884736 | tf_op jit(solution)/shard_map/pallas_call | solution.py:181
  16.4 2.8 %collective-permute-done.3.refs_2_ = bf16[400,768]{1,0:T(8,128)(2,1)S(1)} collective-permute-done((bf16[400,768]{1,0:T(8,128)(2,1)S(1)}, bf16[400,768]{1,0:T(8,128)(2,1)S(1)}, u32[]{:S(2)}, u32[]{:S(2)}) %collective-permute-start.3) | collective-permute-done | bytes 614432 | tf_op jit(solution)/shard_map/ppermute | solution.py:21
  19.1 1.5 %collective-permute-done.refs_0_ = bf16[400,768]{1,0:T(8,128)(2,1)S(1)} collective-permute-done((bf16[400,768]{1,0:T(8,128)(2,1)S(1)}, bf16[400,768]{1,0:T(8,128)(2,1)S(1)}, u32[]{:S(2)}, u32[]{:S(2)}) %collective-permute-start) | collective-permute-done | bytes 614432 | tf_op jit(solution)/shard_map/ppermute | solution.py:264
  21.0 1.3 %collective-permute-start.10 = (bf16[400,768]{1,0:T(8,128)(2,1)}, bf16[400,768]{1,0:T(8,128)(2,1)S(1)}, u32[]{:S(2)}, u32[]{:S(2)}) collective-permute-start(bf16[400,768]{1,0:T(8,128)(2,1)} %collective-permute-done.9), channel_id=1, source_target_pairs={{4,0},{8,12},{5,1},{9,13},{6,2},{10,14},{7,3},{11,15},{20,16},{24,... | collective-permute-start | bytes 1843208 | tf_op jit(solution)/shard_map/ppermute | solution.py:268
  23.0 12.3 %shard_map.78 = (bf16[384,768]{1,0:T(8,128)(2,1)S(1)}, f32[384,768]{1,0:T(8,128)S(1)}, f32[384,768]{1,0:T(8,128)S(1)}) custom-call(s32[2]{0:T(128)S(1)} %pad_add_fusion.ids_ref, bf16[400,768]{1,0:T(8,128)(2,1)S(1)} %fusion.3.refs_0_, bf16[400,768]{1,0:T(8,128)(2,1)S(1)} %collective-permute-done.2.refs_1_, ...), custom_call_target="tpu_custom_call" | custom-call | flops 113246208 | bytes 147456 | tf_op jit(solution)/shard_map/pallas_call | solution.py:144
  35.9 3.5 %collective-permute-done.10 = bf16[400,768]{1,0:T(8,128)(2,1)S(1)} collective-permute-done((bf16[400,768]{1,0:T(8,128)(2,1)}, bf16[400,768]{1,0:T(8,128)(2,1)S(1)}, u32[]{:S(2)}, u32[]{:S(2)}) %collective-permute-start.10) | collective-permute-done | bytes 614432 | tf_op jit(solution)/shard_map/ppermute | solution.py:268
  39.4 1.2 add.27.refs_0_
  41.3 1.5 %collective-permute-start.5 = (bf16[400,768]{1,0:T(8,128)(2,1)S(1)}, bf16[400,768]{1,0:T(8,128)(2,1)S(1)}, u32[]{:S(2)}, u32[]{:S(2)}) collective-permute-start(bf16[400,768]{1,0:T(8,128)(2,1)S(1)} %collective-permute-done.1), channel_id=1, source_target_pairs={{4,0},{8,12},{5,1},{9,13},{6,2},{10,14},{7,3},{11,15},{20,16},{24,... | collective-permute-start | bytes 1843208 | tf_op jit(solution)/shard_map/ppermute | solution.py:274
  42.8 8.6 %shard_map.79 = (f32[384,768]{1,0:T(8,128)S(1)}, f32[384,768]{1,0:T(8,128)S(1)}) custom-call(s32[2]{0:T(128)S(1)} %pad_add_fusion.ids_ref, bf16[400,768]{1,0:T(8,128)(2,1)S(1)} %collective-permute-done.refs_0_, bf16[400,768]{1,0:T(8,128)(2,1)S(1)} %collective-permute-done.6.refs_1_, bf16[400,768]{1,0:T(8,128)(2,1)S(1)} %collective-permute-done.7.refs_2_, ...), custom_call_target="tpu_custom_call" | custom-call | flops 113246208 | bytes 147456 | tf_op jit(solution)/shard_map/pallas_call | solution.py:144
  51.4 3.1 %collective-permute-done.12.refs_2_ = bf16[400,768]{1,0:T(8,128)(2,1)S(1)} collective-permute-done((bf16[400,768]{1,0:T(8,128)(2,1)S(1)}, bf16[400,768]{1,0:T(8,128)(2,1)S(1)}, u32[]{:S(2)}, u32[]{:S(2)}) %collective-permute-start.12) | collective-permute-done | bytes 614432 | tf_op jit(solution)/shard_map/ppermute | solution.py:21
  55.0 5.5 %collective-permute-done.5 = bf16[400,768]{1,0:T(8,128)(2,1)S(1)} collective-permute-done((bf16[400,768]{1,0:T(8,128)(2,1)S(1)}, bf16[400,768]{1,0:T(8,128)(2,1)S(1)}, u32[]{:S(2)}, u32[]{:S(2)}) %collective-permute-start.5) | collective-permute-done | bytes 614432 | tf_op jit(solution)/shard_map/ppermute | solution.py:274
  60.7 1.2 collective-permute-start.15
  62.4 8.6 %shard_map.80 = (f32[384,768]{1,0:T(8,128)S(1)}, f32[384,768]{1,0:T(8,128)S(1)}) custom-call(s32[2]{0:T(128)S(1)} %pad_add_fusion.ids_ref, bf16[400,768]{1,0:T(8,128)(2,1)S(1)} %add.27.refs_0_, bf16[400,768]{1,0:T(8,128)(2,1)S(1)} %collective-permute-done.11.refs_1_, bf16[400,768]{1,0:T(8,128)(2,1)S(1)} %collective-permute-done.12.refs_2_, ...), custom_call_target="tpu_custom_call" | custom-call | flops 113246208 | bytes 147456 | tf_op jit(solution)/shard_map/pallas_call | solution.py:144
  73.2 5.3 %shard_map.81 = (f32[384,768]{1,0:T(8,128)S(1)}, f32[384,768]{1,0:T(8,128)S(1)}) custom-call(s32[2]{0:T(128)S(1)} %pad_add_fusion.ids_ref, bf16[208,768]{1,0:T(8,128)(2,1)S(1)} %slice.58.refs_0_.refs_4_, bf16[208,768]{1,0:T(8,128)(2,1)S(1)} %collective-permute-done.14.refs_1_.refs_5_, bf16[208,768]{1,0:T(8,128)(2,1)S(1)} %collective-permute-done.15.refs_2_.refs_6_, ...), custom_call_target="tpu_custom_call" | custom-call | flops 56623104 | bytes 73728 | tf_op jit(solution)/shard_map/pallas_call | solution.py:144
  78.5 2.2 %collective-permute-done.18.refs_2_ = bf16[192,768]{1,0:T(8,128)(2,1)S(1)} collective-permute-done((bf16[192,768]{1,0:T(8,128)(2,1)S(1)}, bf16[192,768]{1,0:T(8,128)(2,1)S(1)}, u32[]{:S(2)}, u32[]{:S(2)}) %collective-permute-start.18) | collective-permute-done | bytes 294944 | tf_op jit(solution)/shard_map/ppermute | solution.py:21
  81.2 1.1 collective-permute-done.19.refs_3_
  82.7 5.2 %shard_map.82 = bf16[384,768]{1,0:T(8,128)(2,1)S(1)} custom-call(s32[2]{0:T(128)S(1)} %pad_add_fusion.ids_ref, bf16[192,768]{1,0:T(8,128)(2,1)S(1)} %slice.57.refs_0_, bf16[192,768]{1,0:T(8,128)(2,1)S(1)} %collective-permute-done.17.refs_1_, bf16[192,768]{1,0:T(8,128)(2,1)S(1)} %collective-permute-done.18.refs_2_, ...), custom_call_target="tpu_custom_call" | custom-call | flops 56623104 | bytes 73728 | tf_op jit(solution)/shard_map/pallas_call | solution.py:144
  89.4 1.0 shard_map.88
  91.4 1.1 shard_map.86
  92.5 1.2 collective-permute-start.25
  93.7 1.1 shard_map.84
  96.7 9.2 %collective-permute-done.23 = bf16[128,768]{1,0:T(8,128)(2,1)S(1)} collective-permute-done((bf16[128,768]{1,0:T(8,128)(2,1)S(1)}, bf16[128,768]{1,0:T(8,128)(2,1)S(1)}, u32[]{:S(2)}, u32[]{:S(2)}) %collective-permute-start.23) | collective-permute-done | bytes 196640 | tf_op jit(solution)/shard_map/ppermute | solution.py:21
  108.2 1.4 %collective-permute-start.30 = (bf16[128,768]{1,0:T(8,128)(2,1)S(1)}, bf16[128,768]{1,0:T(8,128)(2,1)S(1)}, u32[]{:S(2)}, u32[]{:S(2)}) collective-permute-start(bf16[128,768]{1,0:T(8,128)(2,1)S(1)} %fusion.4), channel_id=1, source_target_pairs={{4,0},{8,4},{12,8},{5,1},{9,5},{13,9},{6,2},{10,6},{14,10},{7,3},{... | collective-permute-start | bytes 589832 | tf_op jit(solution)/shard_map/ppermute | solution.py:27
  109.7 1.3 %collective-permute-start.29 = (bf16[128,768]{1,0:T(8,128)(2,1)S(1)}, bf16[128,768]{1,0:T(8,128)(2,1)S(1)}, u32[]{:S(2)}, u32[]{:S(2)}) collective-permute-start(bf16[128,768]{1,0:T(8,128)(2,1)S(1)} %fusion.5), channel_id=1, source_target_pairs={{4,0},{8,4},{12,8},{5,1},{9,5},{13,9},{6,2},{10,6},{14,10},{7,3},{... | collective-permute-start | bytes 589832 | tf_op jit(solution)/shard_map/ppermute | solution.py:27
  111.0 1.3 %collective-permute-start.28 = (bf16[128,768]{1,0:T(8,128)(2,1)S(1)}, bf16[128,768]{1,0:T(8,128)(2,1)S(1)}, u32[]{:S(2)}, u32[]{:S(2)}) collective-permute-start(bf16[128,768]{1,0:T(8,128)(2,1)S(1)} %fusion.6), channel_id=1, source_target_pairs={{4,0},{8,4},{12,8},{5,1},{9,5},{13,9},{6,2},{10,6},{14,10},{7,3},{... | collective-permute-start | bytes 589832 | tf_op jit(solution)/shard_map/ppermute | solution.py:27
  113.2 5.0 %collective-permute-done.30 = bf16[128,768]{1,0:T(8,128)(2,1)S(1)} collective-permute-done((bf16[128,768]{1,0:T(8,128)(2,1)S(1)}, bf16[128,768]{1,0:T(8,128)(2,1)S(1)}, u32[]{:S(2)}, u32[]{:S(2)}) %collective-permute-start.30) | collective-permute-done | bytes 196640 | tf_op jit(solution)/shard_map/ppermute | solution.py:27
  118.1 4.2 %collective-permute-done.29 = bf16[128,768]{1,0:T(8,128)(2,1)S(1)} collective-permute-done((bf16[128,768]{1,0:T(8,128)(2,1)S(1)}, bf16[128,768]{1,0:T(8,128)(2,1)S(1)}, u32[]{:S(2)}, u32[]{:S(2)}) %collective-permute-start.29) | collective-permute-done | bytes 196640 | tf_op jit(solution)/shard_map/ppermute | solution.py:27
  122.3 2.5 %collective-permute-done.28 = bf16[128,768]{1,0:T(8,128)(2,1)S(1)} collective-permute-done((bf16[128,768]{1,0:T(8,128)(2,1)S(1)}, bf16[128,768]{1,0:T(8,128)(2,1)S(1)}, u32[]{:S(2)}, u32[]{:S(2)}) %collective-permute-start.28) | collective-permute-done | bytes 196640 | tf_op jit(solution)/shard_map/ppermute | solution.py:27
  (72 shorter events, 16.0 us)
Async XLA Ops:
  2.3 16.9 %collective-permute-start.3 = (bf16[400,768]{1,0:T(8,128)(2,1)S(1)}, bf16[400,768]{1,0:T(8,128)(2,1)S(1)}, u32[]{:S(2)}, u32[]{:S(2)}) collective-permute-start(bf16[400,768]{1,0:T(8,128)(2,1)S(1)} %fusion.3.refs_0_), channel_id=1, source_target_pairs={{0,2},{1,3},{2,0},{3,1},{4,6},{5,7},{6,4},{7,5},{8,10},{9,11},{10,... | collective-permute-start | bytes 1843208 | tf_op jit(solution)/shard_map/ppermute | solution.py:21
  5.3 15.3 %collective-permute-start = (bf16[400,768]{1,0:T(8,128)(2,1)S(1)}, bf16[400,768]{1,0:T(8,128)(2,1)S(1)}, u32[]{:S(2)}, u32[]{:S(2)}) collective-permute-start(bf16[400,768]{1,0:T(8,128)(2,1)S(1)} %fusion.3.refs_0_), channel_id=1, source_target_pairs={{0,4},{4,0},{8,12},{12,8},{1,5},{5,1},{9,13},{13,9},{2,6},{6,2},{1... | collective-permute-start | bytes 1843208 | tf_op jit(solution)/shard_map/ppermute | solution.py:264
  6.9 14.1 %collective-permute-start.9 = (bf16[400,768]{1,0:T(8,128)(2,1)S(1)}, bf16[400,768]{1,0:T(8,128)(2,1)}, u32[]{:S(2)}, u32[]{:S(2)}) collective-permute-start(bf16[400,768]{1,0:T(8,128)(2,1)S(1)} %fusion.3.refs_0_), channel_id=1, source_target_pairs={{4,8},{8,4},{5,9},{9,5},{6,10},{10,6},{7,11},{11,7},{20,24},{24,20... | collective-permute-start | bytes 1843208 | tf_op jit(solution)/shard_map/ppermute | solution.py:265
  8.4 14.6 %collective-permute-start.2 = (bf16[400,768]{1,0:T(8,128)(2,1)S(1)}, bf16[400,768]{1,0:T(8,128)(2,1)S(1)}, u32[]{:S(2)}, u32[]{:S(2)}) collective-permute-start(bf16[400,768]{1,0:T(8,128)(2,1)S(1)} %fusion.3.refs_0_), channel_id=1, source_target_pairs={{0,1},{1,0},{2,3},{3,2},{4,5},{5,4},{6,7},{7,6},{8,9},{9,8},{10,11... | collective-permute-start | bytes 1843208 | tf_op jit(solution)/shard_map/ppermute | solution.py:21
  19.1 3.8 %collective-permute-start.4 = (bf16[400,768]{1,0:T(8,128)(2,1)S(1)}, bf16[400,768]{1,0:T(8,128)(2,1)S(1)}, u32[]{:S(2)}, u32[]{:S(2)}) collective-permute-start(bf16[400,768]{1,0:T(8,128)(2,1)S(1)} %collective-permute-done.3.refs_2_), channel_id=1, source_target_pairs={{0,1},{1,0},{2,3},{3,2},{4,5},{5,4},{6,7},{7,6},{8,9},{9,8},{10,11... | collective-permute-start | bytes 1843208 | tf_op jit(solution)/shard_map/ppermute | solution.py:21
  20.6 14.8 %collective-permute-start.7 = (bf16[400,768]{1,0:T(8,128)(2,1)S(1)}, bf16[400,768]{1,0:T(8,128)(2,1)S(1)}, u32[]{:S(2)}, u32[]{:S(2)}) collective-permute-start(bf16[400,768]{1,0:T(8,128)(2,1)S(1)} %collective-permute-done.refs_0_), channel_id=1, source_target_pairs={{0,2},{1,3},{2,0},{3,1},{4,6},{5,7},{6,4},{7,5},{8,10},{9,11},{10,... | collective-permute-start | bytes 1843208 | tf_op jit(solution)/shard_map/ppermute | solution.py:21
  21.0 18.5 %collective-permute-start.10 = (bf16[400,768]{1,0:T(8,128)(2,1)}, bf16[400,768]{1,0:T(8,128)(2,1)S(1)}, u32[]{:S(2)}, u32[]{:S(2)}) collective-permute-start(bf16[400,768]{1,0:T(8,128)(2,1)} %collective-permute-done.9), channel_id=1, source_target_pairs={{4,0},{8,12},{5,1},{9,13},{6,2},{10,14},{7,3},{11,15},{20,16},{24,... | collective-permute-start | bytes 1843208 | tf_op jit(solution)/shard_map/ppermute | solution.py:268
  22.3 19.0 %collective-permute-start.1 = (bf16[400,768]{1,0:T(8,128)(2,1)S(1)}, bf16[400,768]{1,0:T(8,128)(2,1)S(1)}, u32[]{:S(2)}, u32[]{:S(2)}) collective-permute-start(bf16[400,768]{1,0:T(8,128)(2,1)S(1)} %collective-permute-done.refs_0_), channel_id=1, source_target_pairs={{4,8},{8,4},{5,9},{9,5},{6,10},{10,6},{7,11},{11,7},{20,24},{24,20... | collective-permute-start | bytes 1843208 | tf_op jit(solution)/shard_map/ppermute | solution.py:269
  35.4 7.3 %collective-permute-start.8 = (bf16[400,768]{1,0:T(8,128)(2,1)S(1)}, bf16[400,768]{1,0:T(8,128)(2,1)S(1)}, u32[]{:S(2)}, u32[]{:S(2)}) collective-permute-start(bf16[400,768]{1,0:T(8,128)(2,1)S(1)} %collective-permute-done.7.refs_2_), channel_id=1, source_target_pairs={{0,1},{1,0},{2,3},{3,2},{4,5},{5,4},{6,7},{7,6},{8,9},{9,8},{10,11... | collective-permute-start | bytes 1843208 | tf_op jit(solution)/shard_map/ppermute | solution.py:21
  35.6 7.2 %collective-permute-start.6 = (bf16[400,768]{1,0:T(8,128)(2,1)S(1)}, bf16[400,768]{1,0:T(8,128)(2,1)S(1)}, u32[]{:S(2)}, u32[]{:S(2)}) collective-permute-start(bf16[400,768]{1,0:T(8,128)(2,1)S(1)} %collective-permute-done.refs_0_), channel_id=1, source_target_pairs={{0,1},{1,0},{2,3},{3,2},{4,5},{5,4},{6,7},{7,6},{8,9},{9,8},{10,11... | collective-permute-start | bytes 1843208 | tf_op jit(solution)/shard_map/ppermute | solution.py:21
  40.7 13.8 %collective-permute-start.12 = (bf16[400,768]{1,0:T(8,128)(2,1)S(1)}, bf16[400,768]{1,0:T(8,128)(2,1)S(1)}, u32[]{:S(2)}, u32[]{:S(2)}) collective-permute-start(bf16[400,768]{1,0:T(8,128)(2,1)S(1)} %add.27.refs_0_), channel_id=1, source_target_pairs={{0,2},{1,3},{2,0},{3,1},{4,6},{5,7},{6,4},{7,5},{8,10},{9,11},{10,... | collective-permute-start | bytes 1843208 | tf_op jit(solution)/shard_map/ppermute | solution.py:21
  41.3 19.3 %collective-permute-start.5 = (bf16[400,768]{1,0:T(8,128)(2,1)S(1)}, bf16[400,768]{1,0:T(8,128)(2,1)S(1)}, u32[]{:S(2)}, u32[]{:S(2)}) collective-permute-start(bf16[400,768]{1,0:T(8,128)(2,1)S(1)} %collective-permute-done.1), channel_id=1, source_target_pairs={{4,0},{8,12},{5,1},{9,13},{6,2},{10,14},{7,3},{11,15},{20,16},{24,... | collective-permute-start | bytes 1843208 | tf_op jit(solution)/shard_map/ppermute | solution.py:274
  54.5 7.9 %collective-permute-start.13 = (bf16[400,768]{1,0:T(8,128)(2,1)S(1)}, bf16[400,768]{1,0:T(8,128)(2,1)S(1)}, u32[]{:S(2)}, u32[]{:S(2)}) collective-permute-start(bf16[400,768]{1,0:T(8,128)(2,1)S(1)} %collective-permute-done.12.refs_2_), channel_id=1, source_target_pairs={{0,1},{1,0},{2,3},{3,2},{4,5},{5,4},{6,7},{7,6},{8,9},{9,8},{10,11... | collective-permute-start | bytes 1843208 | tf_op jit(solution)/shard_map/ppermute | solution.py:21
  54.5 7.9 %collective-permute-start.11 = (bf16[400,768]{1,0:T(8,128)(2,1)S(1)}, bf16[400,768]{1,0:T(8,128)(2,1)S(1)}, u32[]{:S(2)}, u32[]{:S(2)}) collective-permute-start(bf16[400,768]{1,0:T(8,128)(2,1)S(1)} %add.27.refs_0_), channel_id=1, source_target_pairs={{0,1},{1,0},{2,3},{3,2},{4,5},{5,4},{6,7},{7,6},{8,9},{9,8},{10,11... | collective-permute-start | bytes 1843208 | tf_op jit(solution)/shard_map/ppermute | solution.py:21
  60.7 10.3 %collective-permute-start.15 = (bf16[208,768]{1,0:T(8,128)(2,1)S(1)}, bf16[208,768]{1,0:T(8,128)(2,1)S(1)}, u32[]{:S(2)}, u32[]{:S(2)}) collective-permute-start(bf16[208,768]{1,0:T(8,128)(2,1)S(1)} %slice.58.refs_0_.refs_4_), channel_id=1, source_target_pairs={{0,2},{1,3},{2,0},{3,1},{4,6},{5,7},{6,4},{7,5},{8,10},{9,11},{10,... | collective-permute-start | bytes 958472 | tf_op jit(solution)/shard_map/ppermute | solution.py:21
  61.9 26.8 %collective-permute-start.22 = (bf16[768,768]{1,0:T(8,128)(2,1)S(1)}, bf16[768,768]{1,0:T(8,128)(2,1)S(1)}, u32[]{:S(2)}, u32[]{:S(2)}) collective-permute-start(bf16[768,768]{1,0:T(8,128)(2,1)S(1)} %get-tuple-element.63), channel_id=1, source_target_pairs={{0,1},{1,0},{2,3},{3,2},{4,5},{5,4},{6,7},{7,6},{8,9},{9,8},{10,11... | collective-permute-start | bytes 3538952 | tf_op jit(solution)/shard_map/ppermute | solution.py:21
  61.9 33.8 %collective-permute-start.21 = (bf16[768,768]{1,0:T(8,128)(2,1)S(1)}, bf16[768,768]{1,0:T(8,128)(2,1)S(1)}, u32[]{:S(2)}, u32[]{:S(2)}) collective-permute-start(bf16[768,768]{1,0:T(8,128)(2,1)S(1)} %get-tuple-element.62), channel_id=1, source_target_pairs={{0,1},{1,0},{2,3},{3,2},{4,5},{5,4},{6,7},{7,6},{8,9},{9,8},{10,11... | collective-permute-start | bytes 3538952 | tf_op jit(solution)/shard_map/ppermute | solution.py:21
  71.0 1.7 %collective-permute-start.16 = (bf16[208,768]{1,0:T(8,128)(2,1)S(1)}, bf16[208,768]{1,0:T(8,128)(2,1)S(1)}, u32[]{:S(2)}, u32[]{:S(2)}) collective-permute-start(bf16[208,768]{1,0:T(8,128)(2,1)S(1)} %collective-permute-done.15.refs_2_.refs_6_), channel_id=1, source_target_pairs={{0,1},{1,0},{2,3},{3,2},{4,5},{5,4},{6,7},{7,6},{8,9},{9,8},{10,11... | collective-permute-start | bytes 958472 | tf_op jit(solution)/shard_map/ppermute | solution.py:21
  71.1 2.1 %collective-permute-start.14 = (bf16[208,768]{1,0:T(8,128)(2,1)S(1)}, bf16[208,768]{1,0:T(8,128)(2,1)S(1)}, u32[]{:S(2)}, u32[]{:S(2)}) collective-permute-start(bf16[208,768]{1,0:T(8,128)(2,1)S(1)} %slice.58.refs_0_.refs_4_), channel_id=1, source_target_pairs={{0,1},{1,0},{2,3},{3,2},{4,5},{5,4},{6,7},{7,6},{8,9},{9,8},{10,11... | collective-permute-start | bytes 958472 | tf_op jit(solution)/shard_map/ppermute | solution.py:21
  71.6 9.1 %collective-permute-start.18 = (bf16[192,768]{1,0:T(8,128)(2,1)S(1)}, bf16[192,768]{1,0:T(8,128)(2,1)S(1)}, u32[]{:S(2)}, u32[]{:S(2)}) collective-permute-start(bf16[192,768]{1,0:T(8,128)(2,1)S(1)} %slice.57.refs_0_), channel_id=1, source_target_pairs={{0,2},{1,3},{2,0},{3,1},{4,6},{5,7},{6,4},{7,5},{8,10},{9,11},{10,... | collective-permute-start | bytes 884744 | tf_op jit(solution)/shard_map/ppermute | solution.py:21
  80.7 1.6 %collective-permute-start.19 = (bf16[192,768]{1,0:T(8,128)(2,1)S(1)}, bf16[192,768]{1,0:T(8,128)(2,1)S(1)}, u32[]{:S(2)}, u32[]{:S(2)}) collective-permute-start(bf16[192,768]{1,0:T(8,128)(2,1)S(1)} %collective-permute-done.18.refs_2_), channel_id=1, source_target_pairs={{0,1},{1,0},{2,3},{3,2},{4,5},{5,4},{6,7},{7,6},{8,9},{9,8},{10,11... | collective-permute-start | bytes 884744 | tf_op jit(solution)/shard_map/ppermute | solution.py:21
  80.7 2.0 %collective-permute-start.17 = (bf16[192,768]{1,0:T(8,128)(2,1)S(1)}, bf16[192,768]{1,0:T(8,128)(2,1)S(1)}, u32[]{:S(2)}, u32[]{:S(2)}) collective-permute-start(bf16[192,768]{1,0:T(8,128)(2,1)S(1)} %slice.57.refs_0_), channel_id=1, source_target_pairs={{0,1},{1,0},{2,3},{3,2},{4,5},{5,4},{6,7},{7,6},{8,9},{9,8},{10,11... | collective-permute-start | bytes 884744 | tf_op jit(solution)/shard_map/ppermute | solution.py:21
  87.9 1.5 %collective-permute-start.26 = (bf16[128,768]{1,0:T(8,128)(2,1)S(1)}, bf16[128,768]{1,0:T(8,128)(2,1)S(1)}, u32[]{:S(2)}, u32[]{:S(2)}) collective-permute-start(bf16[128,768]{1,0:T(8,128)(2,1)S(1)} %get-tuple-element.67.mine_ref), channel_id=1, source_target_pairs={{0,1},{1,0},{2,3},{3,2},{4,5},{5,4},{6,7},{7,6},{8,9},{9,8},{10,11... | collective-permute-start | bytes 589832 | tf_op jit(solution)/shard_map/ppermute | solution.py:21
  88.1 3.3 %collective-permute-start.24 = (bf16[128,768]{1,0:T(8,128)(2,1)S(1)}, bf16[128,768]{1,0:T(8,128)(2,1)S(1)}, u32[]{:S(2)}, u32[]{:S(2)}) collective-permute-start(bf16[128,768]{1,0:T(8,128)(2,1)S(1)} %get-tuple-element.64.mine_ref), channel_id=1, source_target_pairs={{0,1},{1,0},{2,3},{3,2},{4,5},{5,4},{6,7},{7,6},{8,9},{9,8},{10,11... | collective-permute-start | bytes 589832 | tf_op jit(solution)/shard_map/ppermute | solution.py:21
  88.5 5.2 %collective-permute-start.20 = (bf16[128,768]{1,0:T(8,128)(2,1)S(1)}, bf16[128,768]{1,0:T(8,128)(2,1)S(1)}, u32[]{:S(2)}, u32[]{:S(2)}) collective-permute-start(bf16[128,768]{1,0:T(8,128)(2,1)S(1)} %get-tuple-element.73.mine_ref), channel_id=1, source_target_pairs={{0,1},{1,0},{2,3},{3,2},{4,5},{5,4},{6,7},{7,6},{8,9},{9,8},{10,11... | collective-permute-start | bytes 589832 | tf_op jit(solution)/shard_map/ppermute | solution.py:21
  90.5 16.6 %collective-permute-start.27 = (bf16[128,768]{1,0:T(8,128)(2,1)S(1)}, bf16[128,768]{1,0:T(8,128)(2,1)S(1)}, u32[]{:S(2)}, u32[]{:S(2)}) collective-permute-start(bf16[128,768]{1,0:T(8,128)(2,1)S(1)} %shard_map.88), channel_id=1, source_target_pairs={{0,2},{1,3},{2,0},{3,1},{4,6},{5,7},{6,4},{7,5},{8,10},{9,11},{10,... | collective-permute-start | bytes 589832 | tf_op jit(solution)/shard_map/ppermute | solution.py:21
  92.5 13.5 %collective-permute-start.25 = (bf16[128,768]{1,0:T(8,128)(2,1)S(1)}, bf16[128,768]{1,0:T(8,128)(2,1)S(1)}, u32[]{:S(2)}, u32[]{:S(2)}) collective-permute-start(bf16[128,768]{1,0:T(8,128)(2,1)S(1)} %shard_map.86), channel_id=1, source_target_pairs={{0,2},{1,3},{2,0},{3,1},{4,6},{5,7},{6,4},{7,5},{8,10},{9,11},{10,... | collective-permute-start | bytes 589832 | tf_op jit(solution)/shard_map/ppermute | solution.py:21
  94.7 11.2 %collective-permute-start.23 = (bf16[128,768]{1,0:T(8,128)(2,1)S(1)}, bf16[128,768]{1,0:T(8,128)(2,1)S(1)}, u32[]{:S(2)}, u32[]{:S(2)}) collective-permute-start(bf16[128,768]{1,0:T(8,128)(2,1)S(1)} %shard_map.84), channel_id=1, source_target_pairs={{0,2},{1,3},{2,0},{3,1},{4,6},{5,7},{6,4},{7,5},{8,10},{9,11},{10,... | collective-permute-start | bytes 589832 | tf_op jit(solution)/shard_map/ppermute | solution.py:21
  108.1 16.7 %copy-start.4 = (bf16[384,768]{1,0:T(8,128)(2,1)S(1)}, bf16[384,768]{1,0:T(8,128)(2,1)}, u32[]{:S(2)}) copy-start(bf16[384,768]{1,0:T(8,128)(2,1)} %param.11) | copy-start | bytes 1769476
  108.2 9.9 %collective-permute-start.30 = (bf16[128,768]{1,0:T(8,128)(2,1)S(1)}, bf16[128,768]{1,0:T(8,128)(2,1)S(1)}, u32[]{:S(2)}, u32[]{:S(2)}) collective-permute-start(bf16[128,768]{1,0:T(8,128)(2,1)S(1)} %fusion.4), channel_id=1, source_target_pairs={{4,0},{8,4},{12,8},{5,1},{9,5},{13,9},{6,2},{10,6},{14,10},{7,3},{... | collective-permute-start | bytes 589832 | tf_op jit(solution)/shard_map/ppermute | solution.py:27
  109.7 12.6 %collective-permute-start.29 = (bf16[128,768]{1,0:T(8,128)(2,1)S(1)}, bf16[128,768]{1,0:T(8,128)(2,1)S(1)}, u32[]{:S(2)}, u32[]{:S(2)}) collective-permute-start(bf16[128,768]{1,0:T(8,128)(2,1)S(1)} %fusion.5), channel_id=1, source_target_pairs={{4,0},{8,4},{12,8},{5,1},{9,5},{13,9},{6,2},{10,6},{14,10},{7,3},{... | collective-permute-start | bytes 589832 | tf_op jit(solution)/shard_map/ppermute | solution.py:27
  111.0 13.9 %collective-permute-start.28 = (bf16[128,768]{1,0:T(8,128)(2,1)S(1)}, bf16[128,768]{1,0:T(8,128)(2,1)S(1)}, u32[]{:S(2)}, u32[]{:S(2)}) collective-permute-start(bf16[128,768]{1,0:T(8,128)(2,1)S(1)} %fusion.6), channel_id=1, source_target_pairs={{4,0},{8,4},{12,8},{5,1},{9,5},{13,9},{6,2},{10,6},{14,10},{7,3},{... | collective-permute-start | bytes 589832 | tf_op jit(solution)/shard_map/ppermute | solution.py:27
  (4 other events, 18.7 us)

commit v3 on v2

--- a/solution.py
+++ b/solution.py
@@ -158,16 +158,15 @@
     )(ids, *args)
 
 
-def fetch_body(ids_ref, weight_ref, out_ref, weight_out, out_out, *rest):
-    *column_outs, sems = rest
+def fetch_body(ids_ref, weight_ref, out_ref, weight_out, out_out, columns_out, sems):
     width = out_ref.shape[0]
     copies = [
         pltpu.make_async_copy(weight_ref, weight_out, sems.at[0]),
         pltpu.make_async_copy(out_ref, out_out, sems.at[1]),
     ]
-    for n, column_out in enumerate(column_outs):
+    for n in range(columns_out.shape[0]):
         at = pl.ds(pl.multiple_of(lax.bitwise_xor(ids_ref[0], 2 * n + 1) * width, HD), width)
-        copies.append(pltpu.make_async_copy(out_ref.at[:, at], column_out, sems.at[n + 2]))
+        copies.append(pltpu.make_async_copy(out_ref.at[:, at], columns_out.at[n], sems.at[n + 2]))
     for copy in copies:
         copy.start()
     for copy in copies:
@@ -181,35 +180,37 @@
     return pl.pallas_call(
         fetch_body,
         in_specs=[pl.BlockSpec(memory_space=pltpu.SMEM), anywhere, anywhere],
-        out_specs=(vmem, vmem) + (anywhere,) * columns,
+        out_specs=(vmem, vmem, anywhere),
         out_shape=(pltpu.VMEM(weight.shape, weight.dtype), pltpu.VMEM(out_weight.shape, out_weight.dtype))
-        + (jax.ShapeDtypeStruct((width, width), out_weight.dtype),) * columns,
+        + (jax.ShapeDtypeStruct((columns, width, width), out_weight.dtype),),
         scratch_shapes=[pltpu.SemaphoreType.DMA((columns + 2,))],
         compiler_params=pltpu.CompilerParams(vmem_limit_bytes=VMEM_LIMIT),
         cost_estimate=pl.CostEstimate(flops=0, bytes_accessed=weight.size // 8, transcendentals=0),
     )(ids, weight, out_weight)
 
 
-def project_body(step, ids_ref, mine_ref, theirs_ref, weight_ref, other_ref, out_ref):
-    width = other_ref.shape[0]
+def project_body(step, cuts, ids_ref, mine_ref, theirs_ref, weight_ref, other_ref, *out_refs):
+    width = other_ref.shape[1]
     at = pl.ds(pl.multiple_of(lax.bitwise_xor(ids_ref[0], step) * width, HD), width)
     total = jnp.dot(mine_ref[...], weight_ref[:, at], preferred_element_type=F32)
-    total = total + jnp.dot(theirs_ref[...], other_ref[...], preferred_element_type=F32)
-    out_ref[...] = total.astype(out_ref.dtype)
-
-
-def project(ids, mine, theirs, weight, other, step, dtype):
+    total = total + jnp.dot(theirs_ref[...], other_ref[step // 2], preferred_element_type=F32)
+    for start, stop, out_ref in zip(cuts, cuts[1:], out_refs):
+        out_ref[...] = total[start:stop].astype(out_ref.dtype)
+
+
+def project(ids, mine, theirs, weight, other, step, cuts, dtype):
     rows, width = mine.shape
     vmem = pl.BlockSpec(memory_space=pltpu.VMEM)
     pin = lambda x: pltpu.with_memory_space_constraint(x, pltpu.VMEM)
+    outs = tuple(jax.ShapeDtypeStruct((stop - start, width), dtype) for start, stop in zip(cuts, cuts[1:]))
     return pl.pallas_call(
-        functools.partial(project_body, step),
+        functools.partial(project_body, step, cuts),
         in_specs=[pl.BlockSpec(memory_space=pltpu.SMEM)] + [vmem] * 4,
-        out_specs=vmem,
-        out_shape=jax.ShapeDtypeStruct((rows, width), dtype),
+        out_specs=(vmem,) * len(outs),
+        out_shape=outs,
         compiler_params=pltpu.CompilerParams(vmem_limit_bytes=VMEM_LIMIT),
         cost_estimate=pl.CostEstimate(
-            flops=rows * width * width * (4 if step else 64), bytes_accessed=rows * width, transcendentals=0
+            flops=rows * width * width // 4, bytes_accessed=rows * width // 4, transcendentals=0
         ),
     )(ids, mine, theirs, pin(weight), pin(other))
 
@@ -251,35 +252,33 @@
     mod_rows = jnp.pad(modulation[0, :2], ((0, MOD_ROWS - 2), (0, 0)))
     carried = jnp.concatenate([mod_rows, piece], axis=0)
 
-    weight, out_local, *columns = fetch(after(ids, carried), weight, out_weight, ha_size)
-    other_weight = [flip(c, "ha", 1) for c in columns]
+    weight, out_local, columns = fetch(after(ids, carried), weight, out_weight, ha_size)
 
     def frame(pieces, state, mods=None, last=False):
         got = frame_step(ids, pieces, mods, weight, state, last, 0 if mods else MOD_ROWS)
         return got[0] if last else got if state is None else (state[0], *got)
 
-    half = MOD_ROWS + tok_count // 2
     if pb_size == 4:
         pairs, middle, outward = [(0, 1), (1, 0), (2, 3), (3, 2)], [(1, 2), (2, 1)], [(1, 0), (2, 3)]
+        own = cross(carried)
         first = after(lax.ppermute(carried, "pb", pairs), weight)
-        crossed = after(lax.ppermute(carried, "pb", middle), weight)
-        own = cross(carried)
         first_over = cross(first)
+        passed = lax.ppermute(first, "pb", middle)
+        crossed = after(lax.ppermute(carried, "pb", middle), weight, first)
         beyond = lax.ppermute(crossed, "pb", outward)
-        passed = lax.ppermute(first, "pb", middle)
         state = frame(paired(after_all(own, weight)), None)
-        beyond, passed = after(beyond, state[0]), after(passed, state[0])
-        second = crossed + beyond
+        passed = after(passed, state[0])
+        onward = lax.ppermute(passed, "pb", outward)
+        second = crossed + after(beyond, passed)
         second_over = cross(second)
-        onward = lax.ppermute(passed, "pb", outward)
-        state = frame(paired([after(p, state[0]) for p in first_over]), state)
-        third = passed + after(onward, state[1])
-        third_parts = [cross(third[:half]), cross(third[half:])]
+        state = frame(paired([after(p, passed) for p in first_over]), state)
+        third = cross(passed + after(onward, state[1]))
         state = frame(paired([after(p, state[1]) for p in second_over]), state)
-        pieces = paired([after(p, state[1]) for p in third_parts[0]])
-        state = frame(pieces, state)
-        attended = frame(paired([after(p, state[1]) for p in third_parts[1]]), state, pieces, True)
+        rest = paired([after(p, state[1]) for p in third])
+        other_weight = flip(after(columns, *rest), "ha", 1)
+        attended = frame(rest, state, None, True)
     else:
+        other_weight = flip(columns, "ha", 1)
         state = frame(spread(carried), None)
         for bit in range(1, pb_size):
             state = frame(spread(flip(carried, "pb", bit)), state, None, bit == pb_size - 1)
@@ -287,29 +286,23 @@
 
     is_last = pb == pb_size - 1
     done, following = [], []
-    chunk = tok_count // 3
-    parts = []
-    for start in range(0, tok_count, chunk):
-        mine = attended[start : start + chunk]
-        both = (mine, flip(mine, "ha", 1))
-        sent = [
-            flip(project(ids, *both, out_local, other_weight[step // 2], step, BF16), "ha", step)
-            for step in range(2, ha_size, 2)
-        ]
-        parts.append((start, both, sent))
-    for start, both, sent in parts:
-        both = tuple(after(x, *done[-1:]) for x in both)
-        branch = project(ids, *both, out_local, other_weight[0], 0, F32)
-        for part in sent:
-            part = after(part, *done[-1:])
+    cuts = (0, tok_count // 3, 2 * tok_count // 3, tok_count)
+    both = (attended, flip(attended, "ha", 1))
+    sent = []
+    for step in range(2, ha_size, 2):
+        parts = project(ids, *both, out_local, other_weight, step, cuts, BF16)
+        sent.append([flip(part, "ha", step) for part in parts])
+    mine = project(ids, *both, out_local, other_weight, 0, cuts, F32)
+    for n, (start, stop, branch) in enumerate(zip(cuts, cuts[1:], mine)):
+        for parts in sent:
+            part = after(parts[n], *mine, *done[-1:])
             branch = branch + part.astype(F32)
-        advanced = (piece[start : start + chunk].astype(F32) + gate * branch).astype(BF16)
+        advanced = (piece[start:stop].astype(F32) + gate * branch).astype(BF16)
         done.append(advanced)
         following.append(from_behind(advanced, "pb", -1))
-    following = [
-        jnp.where(is_last, noise_frame[n * chunk : (n + 1) * chunk], incoming) for n, incoming in enumerate(following)
-    ]
-    return jnp.concatenate(done, axis=0)[None], jnp.concatenate(following, axis=0)[None]
+    following = [after(part, *following[:n]) for n, part in enumerate(following)]
+    queue_next = jnp.where(is_last, noise_frame, jnp.concatenate(following, axis=0))
+    return jnp.concatenate(done, axis=0)[None], queue_next[None]
 
 
 def solution(mesh):

time: 126 us -> 114 us (0.905)
  waiting for transfers between devices: 42.3 us -> 37.5 us
  Pallas kernels: 51.9 us -> 47.3 us
  starting transfers between devices: 23.1 us -> 20.8 us
    ppermute x3, waiting for transfers between devices: 11.7 us -> 6.21 us  [from_behind(): return lax.ppermute(x, axis, pairs)]
    ppermute x1, waiting for transfers between devices: 5.52 us -> 1.9 us  [on_device(): onward = lax.ppermute(passed, 'pb', outward)]
    ppermute x23 -> x17, waiting for transfers between devices: 20.1 us -> 23.2 us  [flip(): return lax.ppermute(x, axis, [(i, i ^ bit) for i in range(size)])]
    pallas_call x6 -> x2, Pallas kernels: 6.21 us -> 3.25 us  [project(): pl.pallas_call(functools.partial(project_body, step, cuts), in_specs=[pl....]
    ppermute x23 -> x17, starting transfers between devices: 12.6 us -> 10.3 us  [flip(): return lax.ppermute(x, axis, [(i, i ^ bit) for i in range(size)])]
    pallas_call x5 -> x4, Pallas kernels: 40.1 us -> 38.5 us  [frame_step(): pl.pallas_call(functools.partial(frame_body, own, last, count, offset, mo...]
  transfers between devices with their start and end apart: 31 -> 25, of which waited for: 16 -> 14; matrix products, arithmetic and copies ran while one was open for 2% -> 2% of each run, Pallas kernels for 40% -> 40%
where the time goes in v3:
time: 114 us
  Pallas kernels  47.3 us (41%)
  waiting for transfers between devices  37.5 us (33%)
  starting transfers between devices  20.8 us (18%)
  other arithmetic  3.63 us (3%)
  local copies, waits for them, and re-layouts  2.8 us (2%)
  between operations  1.68 us (1%)
    pallas_call x4, Pallas kernels, frame_step(): pl.pallas_call(functools.partial(frame_body, own, last, count, offset, mo...  38.5 us
    ppermute x17, waiting for transfers between devices, flip(): return lax.ppermute(x, axis, [(i, i ^ bit) for i in range(size)])  23.2 us
    ppermute x17, starting transfers between devices, flip(): return lax.ppermute(x, axis, [(i, i ^ bit) for i in range(size)])  10.3 us
    ppermute x3, waiting for transfers between devices, from_behind(): return lax.ppermute(x, axis, pairs)  6.21 us
    pallas_call x1, Pallas kernels, fetch(): pl.pallas_call(fetch_body, in_specs=[pl.BlockSpec(memory_space=pltpu.SMEM...  5.6 us
    ppermute x1, waiting for transfers between devices, on_device(): beyond = lax.ppermute(crossed, 'pb', outward)  4.77 us
    ppermute x3, starting transfers between devices, from_behind(): return lax.ppermute(x, axis, pairs)  4.01 us
    pallas_call x2, Pallas kernels, project(): pl.pallas_call(functools.partial(project_body, step, cuts), in_specs=[pl....  3.25 us
  transfers between devices with their start and end apart: 25, of which 14 were waited for; matrix products, arithmetic and copies ran while one was open for 2% of the time, Pallas kernels for 40%

profile of v3, /device:TPU:0, one launch (start us, length us, event | category | flops | bytes accessed | tf_op | source)
XLA Modules:
  0.0 114.0 jit_solution(10138850760179908762)
XLA Ops:
  2.3 3.0 %collective-permute-start.3 = (bf16[400,768]{1,0:T(8,128)(2,1)S(1)}, bf16[400,768]{1,0:T(8,128)(2,1)S(1)}, u32[]{:S(2)}, u32[]{:S(2)}) collective-permute-start(bf16[400,768]{1,0:T(8,128)(2,1)S(1)} %fusion.3.refs_0_), channel_id=1, source_target_pairs={{0,2},{1,3},{2,0},{3,1},{4,6},{5,7},{6,4},{7,5},{8,10},{9,11},{10,... | collective-permute-start | bytes 1843208 | tf_op jit(solution)/shard_map/ppermute | solution.py:21
  5.3 1.6 %collective-permute-start = (bf16[400,768]{1,0:T(8,128)(2,1)S(1)}, bf16[400,768]{1,0:T(8,128)(2,1)S(1)}, u32[]{:S(2)}, u32[]{:S(2)}) collective-permute-start(bf16[400,768]{1,0:T(8,128)(2,1)S(1)} %fusion.3.refs_0_), channel_id=1, source_target_pairs={{0,4},{4,0},{8,12},{12,8},{1,5},{5,1},{9,13},{13,9},{2,6},{6,2},{1... | collective-permute-start | bytes 1843208 | tf_op jit(solution)/shard_map/ppermute | solution.py:264
  6.9 1.5 %collective-permute-start.9 = (bf16[400,768]{1,0:T(8,128)(2,1)S(1)}, bf16[400,768]{1,0:T(8,128)(2,1)}, u32[]{:S(2)}, u32[]{:S(2)}) collective-permute-start(bf16[400,768]{1,0:T(8,128)(2,1)S(1)} %fusion.3.refs_0_), channel_id=1, source_target_pairs={{4,8},{8,4},{5,9},{9,5},{6,10},{10,6},{7,11},{11,7},{20,24},{24,20... | collective-permute-start | bytes 1843208 | tf_op jit(solution)/shard_map/ppermute | solution.py:267
  8.4 2.3 %copy-done.2 = bf16[768,3072]{1,0:T(8,128)(2,1)S(1)} copy-done((bf16[768,3072]{1,0:T(8,128)(2,1)S(1)}, bf16[768,3072]{1,0:T(8,128)(2,1)}, u32[]{:S(2)}) %copy-start.2) | copy-done | bytes 4718616
  10.8 5.6 %shard_map.77 = (bf16[3,3072,768]{2,1,0:T(8,128)(2,1)S(1)}, bf16[768,3072]{1,0:T(8,128)(2,1)S(1)}, bf16[2,768,768]{2,1,0:T(8,128)(2,1)S(1)}) custom-call(s32[2]{0:T(128)S(1)} %pad_add_fusion.ids_ref, bf16[3,3072,768]{2,1,0:T(8,128)(2,1)} %bitcast.32, bf16[768,3072]{1,0:T(8,128)(2,1)S(1)} %copy-done.2), custom_call_target="tpu_custom_call" | custom-call | bytes 884736 | tf_op jit(solution)/shard_map/pallas_call | solution.py:180
  16.4 2.8 %collective-permute-done.3.refs_2_ = bf16[400,768]{1,0:T(8,128)(2,1)S(1)} collective-permute-done((bf16[400,768]{1,0:T(8,128)(2,1)S(1)}, bf16[400,768]{1,0:T(8,128)(2,1)S(1)}, u32[]{:S(2)}, u32[]{:S(2)}) %collective-permute-start.3) | collective-permute-done | bytes 614432 | tf_op jit(solution)/shard_map/ppermute | solution.py:21
  19.1 1.5 %collective-permute-done.refs_0_ = bf16[400,768]{1,0:T(8,128)(2,1)S(1)} collective-permute-done((bf16[400,768]{1,0:T(8,128)(2,1)S(1)}, bf16[400,768]{1,0:T(8,128)(2,1)S(1)}, u32[]{:S(2)}, u32[]{:S(2)}) %collective-permute-start) | collective-permute-done | bytes 614432 | tf_op jit(solution)/shard_map/ppermute | solution.py:264
  21.7 1.3 %collective-permute-start.10 = (bf16[400,768]{1,0:T(8,128)(2,1)}, bf16[400,768]{1,0:T(8,128)(2,1)S(1)}, u32[]{:S(2)}, u32[]{:S(2)}) collective-permute-start(bf16[400,768]{1,0:T(8,128)(2,1)} %collective-permute-done.9), channel_id=1, source_target_pairs={{4,0},{8,12},{5,1},{9,13},{6,2},{10,14},{7,3},{11,15},{20,16},{24,... | collective-permute-start | bytes 1843208 | tf_op jit(solution)/shard_map/ppermute | solution.py:268
  23.0 12.3 %shard_map.78 = (bf16[384,768]{1,0:T(8,128)(2,1)S(1)}, f32[384,768]{1,0:T(8,128)S(1)}, f32[384,768]{1,0:T(8,128)S(1)}) custom-call(s32[2]{0:T(128)S(1)} %pad_add_fusion.ids_ref, bf16[400,768]{1,0:T(8,128)(2,1)S(1)} %fusion.3.refs_0_, bf16[400,768]{1,0:T(8,128)(2,1)S(1)} %collective-permute-done.2.refs_1_, ...), custom_call_target="tpu_custom_call" | custom-call | flops 113246208 | bytes 147456 | tf_op jit(solution)/shard_map/pallas_call | solution.py:144
  36.7 4.8 %collective-permute-done.10 = bf16[400,768]{1,0:T(8,128)(2,1)S(1)} collective-permute-done((bf16[400,768]{1,0:T(8,128)(2,1)}, bf16[400,768]{1,0:T(8,128)(2,1)S(1)}, u32[]{:S(2)}, u32[]{:S(2)}) %collective-permute-start.10) | collective-permute-done | bytes 614432 | tf_op jit(solution)/shard_map/ppermute | solution.py:268
  41.5 1.2 %add.27.refs_0_ = bf16[400,768]{1,0:T(8,128)(2,1)S(1)} add(bf16[400,768]{1,0:T(8,128)(2,1)} %collective-permute-done.9, bf16[400,768]{1,0:T(8,128)(2,1)S(1)} %collective-permute-done.10) | non-fusion elementwise | flops 307200 | bytes 1843200 | tf_op jit(solution)/shard_map/add | solution.py:272
  43.3 1.5 %collective-permute-start.5 = (bf16[400,768]{1,0:T(8,128)(2,1)S(1)}, bf16[400,768]{1,0:T(8,128)(2,1)S(1)}, u32[]{:S(2)}, u32[]{:S(2)}) collective-permute-start(bf16[400,768]{1,0:T(8,128)(2,1)S(1)} %collective-permute-done.1), channel_id=1, source_target_pairs={{4,0},{8,12},{5,1},{9,13},{6,2},{10,14},{7,3},{11,15},{20,16},{24,... | collective-permute-start | bytes 1843208 | tf_op jit(solution)/shard_map/ppermute | solution.py:271
  44.8 8.6 %shard_map.79 = (f32[384,768]{1,0:T(8,128)S(1)}, f32[384,768]{1,0:T(8,128)S(1)}) custom-call(s32[2]{0:T(128)S(1)} %pad_add_fusion.ids_ref, bf16[400,768]{1,0:T(8,128)(2,1)S(1)} %collective-permute-done.refs_0_, bf16[400,768]{1,0:T(8,128)(2,1)S(1)} %collective-permute-done.6.refs_1_, bf16[400,768]{1,0:T(8,128)(2,1)S(1)} %collective-permute-done.7.refs_2_, ...), custom_call_target="tpu_custom_call" | custom-call | flops 113246208 | bytes 147456 | tf_op jit(solution)/shard_map/pallas_call | solution.py:144
  53.5 4.1 %collective-permute-done.12.refs_2_ = bf16[400,768]{1,0:T(8,128)(2,1)S(1)} collective-permute-done((bf16[400,768]{1,0:T(8,128)(2,1)S(1)}, bf16[400,768]{1,0:T(8,128)(2,1)S(1)}, u32[]{:S(2)}, u32[]{:S(2)}) %collective-permute-start.12) | collective-permute-done | bytes 614432 | tf_op jit(solution)/shard_map/ppermute | solution.py:21
  57.6 1.9 %collective-permute-done.5 = bf16[400,768]{1,0:T(8,128)(2,1)S(1)} collective-permute-done((bf16[400,768]{1,0:T(8,128)(2,1)S(1)}, bf16[400,768]{1,0:T(8,128)(2,1)S(1)}, u32[]{:S(2)}, u32[]{:S(2)}) %collective-permute-start.5) | collective-permute-done | bytes 614432 | tf_op jit(solution)/shard_map/ppermute | solution.py:271
  59.7 1.8 %collective-permute-start.15 = (bf16[400,768]{1,0:T(8,128)(2,1)S(1)}, bf16[400,768]{1,0:T(8,128)(2,1)S(1)}, u32[]{:S(2)}, u32[]{:S(2)}) collective-permute-start(bf16[400,768]{1,0:T(8,128)(2,1)S(1)} %add.26.refs_0_), channel_id=1, source_target_pairs={{0,2},{1,3},{2,0},{3,1},{4,6},{5,7},{6,4},{7,5},{8,10},{9,11},{10,... | collective-permute-start | bytes 1843208 | tf_op jit(solution)/shard_map/ppermute | solution.py:21
  61.5 8.6 %shard_map.80 = (f32[384,768]{1,0:T(8,128)S(1)}, f32[384,768]{1,0:T(8,128)S(1)}) custom-call(s32[2]{0:T(128)S(1)} %pad_add_fusion.ids_ref, bf16[400,768]{1,0:T(8,128)(2,1)S(1)} %add.27.refs_0_, bf16[400,768]{1,0:T(8,128)(2,1)S(1)} %collective-permute-done.11.refs_1_, bf16[400,768]{1,0:T(8,128)(2,1)S(1)} %collective-permute-done.12.refs_2_, ...), custom_call_target="tpu_custom_call" | custom-call | flops 113246208 | bytes 147456 | tf_op jit(solution)/shard_map/pallas_call | solution.py:144
  70.2 3.9 %collective-permute-done.15.refs_2_ = bf16[400,768]{1,0:T(8,128)(2,1)S(1)} collective-permute-done((bf16[400,768]{1,0:T(8,128)(2,1)S(1)}, bf16[400,768]{1,0:T(8,128)(2,1)S(1)}, u32[]{:S(2)}, u32[]{:S(2)}) %collective-permute-start.15) | collective-permute-done | bytes 614432 | tf_op jit(solution)/shard_map/ppermute | solution.py:21
  74.1 2.0 %collective-permute-done.16.refs_3_ = bf16[400,768]{1,0:T(8,128)(2,1)S(1)} collective-permute-done((bf16[400,768]{1,0:T(8,128)(2,1)S(1)}, bf16[400,768]{1,0:T(8,128)(2,1)S(1)}, u32[]{:S(2)}, u32[]{:S(2)}) %collective-permute-start.16) | collective-permute-done | bytes 614432 | tf_op jit(solution)/shard_map/ppermute | solution.py:21
  76.3 8.9 %shard_map.81.mine_ref = bf16[384,768]{1,0:T(8,128)(2,1)S(1)} custom-call(s32[2]{0:T(128)S(1)} %pad_add_fusion.ids_ref, bf16[400,768]{1,0:T(8,128)(2,1)S(1)} %add.26.refs_0_, bf16[400,768]{1,0:T(8,128)(2,1)S(1)} %collective-permute-done.14.refs_1_, bf16[400,768]{1,0:T(8,128)(2,1)S(1)} %collective-permute-done.15.refs_2_, ...), custom_call_target="tpu_custom_call" | custom-call | flops 113246208 | bytes 147456 | tf_op jit(solution)/shard_map/pallas_call | solution.py:144
  85.6 1.6 %collective-permute-done.17.theirs_ref = bf16[384,768]{1,0:T(8,128)(2,1)S(1)} collective-permute-done((bf16[384,768]{1,0:T(8,128)(2,1)S(1)}, bf16[384,768]{1,0:T(8,128)(2,1)S(1)}, u32[]{:S(2)}, u32[]{:S(2)}) %collective-permute-start.17) | collective-permute-done | bytes 589856 | tf_op jit(solution)/shard_map/ppermute | solution.py:21
  87.3 1.6 %shard_map.83 = (bf16[128,768]{1,0:T(8,128)(2,1)S(1)}, bf16[128,768]{1,0:T(8,128)(2,1)S(1)}, bf16[128,768]{1,0:T(8,128)(2,1)S(1)}) custom-call(s32[2]{0:T(128)S(1)} %pad_add_fusion.ids_ref, bf16[384,768]{1,0:T(8,128)(2,1)S(1)} %shard_map.81.mine_ref, bf16[384,768]{1,0:T(8,128)(2,1)S(1)} %collective-permute-done.17.theirs_ref, ...), custom_call_target="tpu_custom_call" | custom-call | flops 56623104 | bytes 73728 | tf_op jit(solution)/shard_map/pallas_call | solution.py:206
  88.9 1.1 collective-permute-start.19
  92.1 1.6 %shard_map.82 = (f32[128,768]{1,0:T(8,128)S(1)}, f32[128,768]{1,0:T(8,128)S(1)}, f32[128,768]{1,0:T(8,128)S(1)}) custom-call(s32[2]{0:T(128)S(1)} %pad_add_fusion.ids_ref, bf16[384,768]{1,0:T(8,128)(2,1)S(1)} %shard_map.81.mine_ref, bf16[384,768]{1,0:T(8,128)(2,1)S(1)} %collective-permute-done.17.theirs_ref, ...), custom_call_target="tpu_custom_call" | custom-call | flops 56623104 | bytes 73728 | tf_op jit(solution)/shard_map/pallas_call | solution.py:206
  93.8 3.0 %collective-permute-done.19 = bf16[128,768]{1,0:T(8,128)(2,1)S(1)} collective-permute-done((bf16[128,768]{1,0:T(8,128)(2,1)S(1)}, bf16[128,768]{1,0:T(8,128)(2,1)S(1)}, u32[]{:S(2)}, u32[]{:S(2)}) %collective-permute-start.19) | collective-permute-done | bytes 196640 | tf_op jit(solution)/shard_map/ppermute | solution.py:21
  96.8 1.3 %collective-permute-start.22 = (bf16[128,768]{1,0:T(8,128)(2,1)S(1)}, bf16[128,768]{1,0:T(8,128)(2,1)S(1)}, u32[]{:S(2)}, u32[]{:S(2)}) collective-permute-start(bf16[128,768]{1,0:T(8,128)(2,1)S(1)} %fusion.7), channel_id=1, source_target_pairs={{4,0},{8,4},{12,8},{5,1},{9,5},{13,9},{6,2},{10,6},{14,10},{7,3},{... | collective-permute-start | bytes 589832 | tf_op jit(solution)/shard_map/ppermute | solution.py:27
  98.1 2.8 %collective-permute-done.20 = bf16[128,768]{1,0:T(8,128)(2,1)S(1)} collective-permute-done((bf16[128,768]{1,0:T(8,128)(2,1)S(1)}, bf16[128,768]{1,0:T(8,128)(2,1)S(1)}, u32[]{:S(2)}, u32[]{:S(2)}) %collective-permute-start.20) | collective-permute-done | bytes 196640 | tf_op jit(solution)/shard_map/ppermute | solution.py:21
  101.0 1.4 %collective-permute-start.23 = (bf16[128,768]{1,0:T(8,128)(2,1)S(1)}, bf16[128,768]{1,0:T(8,128)(2,1)S(1)}, u32[]{:S(2)}, u32[]{:S(2)}) collective-permute-start(bf16[128,768]{1,0:T(8,128)(2,1)S(1)} %fusion.6), channel_id=1, source_target_pairs={{4,0},{8,4},{12,8},{5,1},{9,5},{13,9},{6,2},{10,6},{14,10},{7,3},{... | collective-permute-start | bytes 589832 | tf_op jit(solution)/shard_map/ppermute | solution.py:27
  102.5 2.1 %collective-permute-done.21 = bf16[128,768]{1,0:T(8,128)(2,1)S(1)} collective-permute-done((bf16[128,768]{1,0:T(8,128)(2,1)S(1)}, bf16[128,768]{1,0:T(8,128)(2,1)S(1)}, u32[]{:S(2)}, u32[]{:S(2)}) %collective-permute-start.21) | collective-permute-done | bytes 196640 | tf_op jit(solution)/shard_map/ppermute | solution.py:21
  104.7 1.3 %collective-permute-start.24 = (bf16[128,768]{1,0:T(8,128)(2,1)S(1)}, bf16[128,768]{1,0:T(8,128)(2,1)S(1)}, u32[]{:S(2)}, u32[]{:S(2)}) collective-permute-start(bf16[128,768]{1,0:T(8,128)(2,1)S(1)} %fusion.5), channel_id=1, source_target_pairs={{4,0},{8,4},{12,8},{5,1},{9,5},{13,9},{6,2},{10,6},{14,10},{7,3},{... | collective-permute-start | bytes 589832 | tf_op jit(solution)/shard_map/ppermute | solution.py:27
  106.8 2.1 %collective-permute-done.23 = bf16[128,768]{1,0:T(8,128)(2,1)S(1)} collective-permute-done((bf16[128,768]{1,0:T(8,128)(2,1)S(1)}, bf16[128,768]{1,0:T(8,128)(2,1)S(1)}, u32[]{:S(2)}, u32[]{:S(2)}) %collective-permute-start.23) | collective-permute-done | bytes 196640 | tf_op jit(solution)/shard_map/ppermute | solution.py:27
  108.9 4.1 %collective-permute-done.24 = bf16[128,768]{1,0:T(8,128)(2,1)S(1)} collective-permute-done((bf16[128,768]{1,0:T(8,128)(2,1)S(1)}, bf16[128,768]{1,0:T(8,128)(2,1)S(1)}, u32[]{:S(2)}, u32[]{:S(2)}) %collective-permute-start.24) | collective-permute-done | bytes 196640 | tf_op jit(solution)/shard_map/ppermute | solution.py:27
  (51 shorter events, 9.0 us)
Async XLA Ops:
  0.6 1.3 %copy-start = (bf16[256,3,768]{2,0,1:T(8,128)(2,1)S(1)}, bf16[256,3,768]{2,0,1:T(8,128)(2,1)}, u32[]{:S(2)}) copy-start(bf16[256,3,768]{2,0,1:T(8,128)(2,1)} %param.8) | copy-start | bytes 3538948
  0.6 1.6 %copy-start.3 = (bf16[1,384,768]{2,1,0:T(8,128)(2,1)S(1)}, bf16[1,384,768]{2,1,0:T(8,128)(2,1)}, u32[]{:S(2)}) copy-start(bf16[1,384,768]{2,1,0:T(8,128)(2,1)} %param.6) | copy-start | bytes 1769476
  2.3 16.9 %collective-permute-start.3 = (bf16[400,768]{1,0:T(8,128)(2,1)S(1)}, bf16[400,768]{1,0:T(8,128)(2,1)S(1)}, u32[]{:S(2)}, u32[]{:S(2)}) collective-permute-start(bf16[400,768]{1,0:T(8,128)(2,1)S(1)} %fusion.3.refs_0_), channel_id=1, source_target_pairs={{0,2},{1,3},{2,0},{3,1},{4,6},{5,7},{6,4},{7,5},{8,10},{9,11},{10,... | collective-permute-start | bytes 1843208 | tf_op jit(solution)/shard_map/ppermute | solution.py:21
  5.3 15.3 %collective-permute-start = (bf16[400,768]{1,0:T(8,128)(2,1)S(1)}, bf16[400,768]{1,0:T(8,128)(2,1)S(1)}, u32[]{:S(2)}, u32[]{:S(2)}) collective-permute-start(bf16[400,768]{1,0:T(8,128)(2,1)S(1)} %fusion.3.refs_0_), channel_id=1, source_target_pairs={{0,4},{4,0},{8,12},{12,8},{1,5},{5,1},{9,13},{13,9},{2,6},{6,2},{1... | collective-permute-start | bytes 1843208 | tf_op jit(solution)/shard_map/ppermute | solution.py:264
  6.9 14.9 %collective-permute-start.9 = (bf16[400,768]{1,0:T(8,128)(2,1)S(1)}, bf16[400,768]{1,0:T(8,128)(2,1)}, u32[]{:S(2)}, u32[]{:S(2)}) collective-permute-start(bf16[400,768]{1,0:T(8,128)(2,1)S(1)} %fusion.3.refs_0_), channel_id=1, source_target_pairs={{4,8},{8,4},{5,9},{9,5},{6,10},{10,6},{7,11},{11,7},{20,24},{24,20... | collective-permute-start | bytes 1843208 | tf_op jit(solution)/shard_map/ppermute | solution.py:267
  8.4 14.7 %collective-permute-start.2 = (bf16[400,768]{1,0:T(8,128)(2,1)S(1)}, bf16[400,768]{1,0:T(8,128)(2,1)S(1)}, u32[]{:S(2)}, u32[]{:S(2)}) collective-permute-start(bf16[400,768]{1,0:T(8,128)(2,1)S(1)} %fusion.3.refs_0_), channel_id=1, source_target_pairs={{0,1},{1,0},{2,3},{3,2},{4,5},{5,4},{6,7},{7,6},{8,9},{9,8},{10,11... | collective-permute-start | bytes 1843208 | tf_op jit(solution)/shard_map/ppermute | solution.py:21
  8.4 2.3 %copy-start.2 = (bf16[768,3072]{1,0:T(8,128)(2,1)S(1)}, bf16[768,3072]{1,0:T(8,128)(2,1)}, u32[]{:S(2)}) copy-start(bf16[768,3072]{1,0:T(8,128)(2,1)} %out_ref.1) | copy-start | bytes 14155780
  19.1 3.9 %collective-permute-start.4 = (bf16[400,768]{1,0:T(8,128)(2,1)S(1)}, bf16[400,768]{1,0:T(8,128)(2,1)S(1)}, u32[]{:S(2)}, u32[]{:S(2)}) collective-permute-start(bf16[400,768]{1,0:T(8,128)(2,1)S(1)} %collective-permute-done.3.refs_2_), channel_id=1, source_target_pairs={{0,1},{1,0},{2,3},{3,2},{4,5},{5,4},{6,7},{7,6},{8,9},{9,8},{10,11... | collective-permute-start | bytes 1843208 | tf_op jit(solution)/shard_map/ppermute | solution.py:21
  20.6 14.8 %collective-permute-start.1 = (bf16[400,768]{1,0:T(8,128)(2,1)S(1)}, bf16[400,768]{1,0:T(8,128)(2,1)S(1)}, u32[]{:S(2)}, u32[]{:S(2)}) collective-permute-start(bf16[400,768]{1,0:T(8,128)(2,1)S(1)} %collective-permute-done.refs_0_), channel_id=1, source_target_pairs={{4,8},{8,4},{5,9},{9,5},{6,10},{10,6},{7,11},{11,7},{20,24},{24,20... | collective-permute-start | bytes 1843208 | tf_op jit(solution)/shard_map/ppermute | solution.py:266
  21.3 14.9 %collective-permute-start.7 = (bf16[400,768]{1,0:T(8,128)(2,1)S(1)}, bf16[400,768]{1,0:T(8,128)(2,1)S(1)}, u32[]{:S(2)}, u32[]{:S(2)}) collective-permute-start(bf16[400,768]{1,0:T(8,128)(2,1)S(1)} %collective-permute-done.refs_0_), channel_id=1, source_target_pairs={{0,2},{1,3},{2,0},{3,1},{4,6},{5,7},{6,4},{7,5},{8,10},{9,11},{10,... | collective-permute-start | bytes 1843208 | tf_op jit(solution)/shard_map/ppermute | solution.py:21
  21.7 19.7 %collective-permute-start.10 = (bf16[400,768]{1,0:T(8,128)(2,1)}, bf16[400,768]{1,0:T(8,128)(2,1)S(1)}, u32[]{:S(2)}, u32[]{:S(2)}) collective-permute-start(bf16[400,768]{1,0:T(8,128)(2,1)} %collective-permute-done.9), channel_id=1, source_target_pairs={{4,0},{8,12},{5,1},{9,13},{6,2},{10,14},{7,3},{11,15},{20,16},{24,... | collective-permute-start | bytes 1843208 | tf_op jit(solution)/shard_map/ppermute | solution.py:268
  36.2 8.6 %collective-permute-start.6 = (bf16[400,768]{1,0:T(8,128)(2,1)S(1)}, bf16[400,768]{1,0:T(8,128)(2,1)S(1)}, u32[]{:S(2)}, u32[]{:S(2)}) collective-permute-start(bf16[400,768]{1,0:T(8,128)(2,1)S(1)} %collective-permute-done.refs_0_), channel_id=1, source_target_pairs={{0,1},{1,0},{2,3},{3,2},{4,5},{5,4},{6,7},{7,6},{8,9},{9,8},{10,11... | collective-permute-start | bytes 1843208 | tf_op jit(solution)/shard_map/ppermute | solution.py:21
  36.2 8.6 %collective-permute-start.8 = (bf16[400,768]{1,0:T(8,128)(2,1)S(1)}, bf16[400,768]{1,0:T(8,128)(2,1)S(1)}, u32[]{:S(2)}, u32[]{:S(2)}) collective-permute-start(bf16[400,768]{1,0:T(8,128)(2,1)S(1)} %collective-permute-done.7.refs_2_), channel_id=1, source_target_pairs={{0,1},{1,0},{2,3},{3,2},{4,5},{5,4},{6,7},{7,6},{8,9},{9,8},{10,11... | collective-permute-start | bytes 1843208 | tf_op jit(solution)/shard_map/ppermute | solution.py:21
  42.7 15.0 %collective-permute-start.12 = (bf16[400,768]{1,0:T(8,128)(2,1)S(1)}, bf16[400,768]{1,0:T(8,128)(2,1)S(1)}, u32[]{:S(2)}, u32[]{:S(2)}) collective-permute-start(bf16[400,768]{1,0:T(8,128)(2,1)S(1)} %add.27.refs_0_), channel_id=1, source_target_pairs={{0,2},{1,3},{2,0},{3,1},{4,6},{5,7},{6,4},{7,5},{8,10},{9,11},{10,... | collective-permute-start | bytes 1843208 | tf_op jit(solution)/shard_map/ppermute | solution.py:21
  43.3 16.3 %collective-permute-start.5 = (bf16[400,768]{1,0:T(8,128)(2,1)S(1)}, bf16[400,768]{1,0:T(8,128)(2,1)S(1)}, u32[]{:S(2)}, u32[]{:S(2)}) collective-permute-start(bf16[400,768]{1,0:T(8,128)(2,1)S(1)} %collective-permute-done.1), channel_id=1, source_target_pairs={{4,0},{8,12},{5,1},{9,13},{6,2},{10,14},{7,3},{11,15},{20,16},{24,... | collective-permute-start | bytes 1843208 | tf_op jit(solution)/shard_map/ppermute | solution.py:271
  53.4 8.1 %collective-permute-start.11 = (bf16[400,768]{1,0:T(8,128)(2,1)S(1)}, bf16[400,768]{1,0:T(8,128)(2,1)S(1)}, u32[]{:S(2)}, u32[]{:S(2)}) collective-permute-start(bf16[400,768]{1,0:T(8,128)(2,1)S(1)} %add.27.refs_0_), channel_id=1, source_target_pairs={{0,1},{1,0},{2,3},{3,2},{4,5},{5,4},{6,7},{7,6},{8,9},{9,8},{10,11... | collective-permute-start | bytes 1843208 | tf_op jit(solution)/shard_map/ppermute | solution.py:21
  57.6 3.8 %collective-permute-start.13 = (bf16[400,768]{1,0:T(8,128)(2,1)S(1)}, bf16[400,768]{1,0:T(8,128)(2,1)S(1)}, u32[]{:S(2)}, u32[]{:S(2)}) collective-permute-start(bf16[400,768]{1,0:T(8,128)(2,1)S(1)} %collective-permute-done.12.refs_2_), channel_id=1, source_target_pairs={{0,1},{1,0},{2,3},{3,2},{4,5},{5,4},{6,7},{7,6},{8,9},{9,8},{10,11... | collective-permute-start | bytes 1843208 | tf_op jit(solution)/shard_map/ppermute | solution.py:21
  59.7 14.4 %collective-permute-start.15 = (bf16[400,768]{1,0:T(8,128)(2,1)S(1)}, bf16[400,768]{1,0:T(8,128)(2,1)S(1)}, u32[]{:S(2)}, u32[]{:S(2)}) collective-permute-start(bf16[400,768]{1,0:T(8,128)(2,1)S(1)} %add.26.refs_0_), channel_id=1, source_target_pairs={{0,2},{1,3},{2,0},{3,1},{4,6},{5,7},{6,4},{7,5},{8,10},{9,11},{10,... | collective-permute-start | bytes 1843208 | tf_op jit(solution)/shard_map/ppermute | solution.py:21
  70.1 4.0 %collective-permute-start.14 = (bf16[400,768]{1,0:T(8,128)(2,1)S(1)}, bf16[400,768]{1,0:T(8,128)(2,1)S(1)}, u32[]{:S(2)}, u32[]{:S(2)}) collective-permute-start(bf16[400,768]{1,0:T(8,128)(2,1)S(1)} %add.26.refs_0_), channel_id=1, source_target_pairs={{0,1},{1,0},{2,3},{3,2},{4,5},{5,4},{6,7},{7,6},{8,9},{9,8},{10,11... | collective-permute-start | bytes 1843208 | tf_op jit(solution)/shard_map/ppermute | solution.py:21
  74.1 2.0 %collective-permute-start.16 = (bf16[400,768]{1,0:T(8,128)(2,1)S(1)}, bf16[400,768]{1,0:T(8,128)(2,1)S(1)}, u32[]{:S(2)}, u32[]{:S(2)}) collective-permute-start(bf16[400,768]{1,0:T(8,128)(2,1)S(1)} %collective-permute-done.15.refs_2_), channel_id=1, source_target_pairs={{0,1},{1,0},{2,3},{3,2},{4,5},{5,4},{6,7},{7,6},{8,9},{9,8},{10,11... | collective-permute-start | bytes 1843208 | tf_op jit(solution)/shard_map/ppermute | solution.py:21
  76.2 11.1 %collective-permute-start.18 = (bf16[2,768,768]{2,1,0:T(8,128)(2,1)S(1)}, bf16[2,768,768]{2,1,0:T(8,128)(2,1)S(1)}, u32[]{:S(2)}, u32[]{:S(2)}) collective-permute-start(bf16[2,768,768]{2,1,0:T(8,128)(2,1)S(1)} %get-tuple-element.60), channel_id=1, source_target_pairs={{0,1},{1,0},{2,3},{3,2},{4,5},{5,4},{6,7},{7,6},{8,9},{9,8},{10,11... | collective-permute-start | bytes 7077896 | tf_op jit(solution)/shard_map/ppermute | solution.py:21
  85.2 2.1 %collective-permute-start.17 = (bf16[384,768]{1,0:T(8,128)(2,1)S(1)}, bf16[384,768]{1,0:T(8,128)(2,1)S(1)}, u32[]{:S(2)}, u32[]{:S(2)}) collective-permute-start(bf16[384,768]{1,0:T(8,128)(2,1)S(1)} %shard_map.81.mine_ref), channel_id=1, source_target_pairs={{0,1},{1,0},{2,3},{3,2},{4,5},{5,4},{6,7},{7,6},{8,9},{9,8},{10,11... | collective-permute-start | bytes 1769480 | tf_op jit(solution)/shard_map/ppermute | solution.py:21
  88.9 7.8 %collective-permute-start.19 = (bf16[128,768]{1,0:T(8,128)(2,1)S(1)}, bf16[128,768]{1,0:T(8,128)(2,1)S(1)}, u32[]{:S(2)}, u32[]{:S(2)}) collective-permute-start(bf16[128,768]{1,0:T(8,128)(2,1)S(1)} %get-tuple-element.62), channel_id=1, source_target_pairs={{0,2},{1,3},{2,0},{3,1},{4,6},{5,7},{6,4},{7,5},{8,10},{9,11},{10,... | collective-permute-start | bytes 589832 | tf_op jit(solution)/shard_map/ppermute | solution.py:21
  90.1 10.9 %collective-permute-start.20 = (bf16[128,768]{1,0:T(8,128)(2,1)S(1)}, bf16[128,768]{1,0:T(8,128)(2,1)S(1)}, u32[]{:S(2)}, u32[]{:S(2)}) collective-permute-start(bf16[128,768]{1,0:T(8,128)(2,1)S(1)} %get-tuple-element.66), channel_id=1, source_target_pairs={{0,2},{1,3},{2,0},{3,1},{4,6},{5,7},{6,4},{7,5},{8,10},{9,11},{10,... | collective-permute-start | bytes 589832 | tf_op jit(solution)/shard_map/ppermute | solution.py:21
  91.1 13.5 %collective-permute-start.21 = (bf16[128,768]{1,0:T(8,128)(2,1)S(1)}, bf16[128,768]{1,0:T(8,128)(2,1)S(1)}, u32[]{:S(2)}, u32[]{:S(2)}) collective-permute-start(bf16[128,768]{1,0:T(8,128)(2,1)S(1)} %get-tuple-element.68), channel_id=1, source_target_pairs={{0,2},{1,3},{2,0},{3,1},{4,6},{5,7},{6,4},{7,5},{8,10},{9,11},{10,... | collective-permute-start | bytes 589832 | tf_op jit(solution)/shard_map/ppermute | solution.py:21
  96.8 10.0 %collective-permute-start.22 = (bf16[128,768]{1,0:T(8,128)(2,1)S(1)}, bf16[128,768]{1,0:T(8,128)(2,1)S(1)}, u32[]{:S(2)}, u32[]{:S(2)}) collective-permute-start(bf16[128,768]{1,0:T(8,128)(2,1)S(1)} %fusion.7), channel_id=1, source_target_pairs={{4,0},{8,4},{12,8},{5,1},{9,5},{13,9},{6,2},{10,6},{14,10},{7,3},{... | collective-permute-start | bytes 589832 | tf_op jit(solution)/shard_map/ppermute | solution.py:27
  101.0 12.0 %copy-start.4 = (bf16[384,768]{1,0:T(8,128)(2,1)S(1)}, bf16[384,768]{1,0:T(8,128)(2,1)}, u32[]{:S(2)}) copy-start(bf16[384,768]{1,0:T(8,128)(2,1)} %param.11) | copy-start | bytes 1769476
  101.0 7.9 %collective-permute-start.23 = (bf16[128,768]{1,0:T(8,128)(2,1)S(1)}, bf16[128,768]{1,0:T(8,128)(2,1)S(1)}, u32[]{:S(2)}, u32[]{:S(2)}) collective-permute-start(bf16[128,768]{1,0:T(8,128)(2,1)S(1)} %fusion.6), channel_id=1, source_target_pairs={{4,0},{8,4},{12,8},{5,1},{9,5},{13,9},{6,2},{10,6},{14,10},{7,3},{... | collective-permute-start | bytes 589832 | tf_op jit(solution)/shard_map/ppermute | solution.py:27
  104.7 8.4 %collective-permute-start.24 = (bf16[128,768]{1,0:T(8,128)(2,1)S(1)}, bf16[128,768]{1,0:T(8,128)(2,1)S(1)}, u32[]{:S(2)}, u32[]{:S(2)}) collective-permute-start(bf16[128,768]{1,0:T(8,128)(2,1)S(1)} %fusion.5), channel_id=1, source_target_pairs={{4,0},{8,4},{12,8},{5,1},{9,5},{13,9},{6,2},{10,6},{14,10},{7,3},{... | collective-permute-start | bytes 589832 | tf_op jit(solution)/shard_map/ppermute | solution.py:27
  106.0 8.0 %copy-start.1 = (bf16[256,3,768]{2,0,1:T(8,128)(2,1)S(1)}, bf16[256,3,768]{2,0,1:T(8,128)(2,1)}, u32[]{:S(2)}) copy-start(bf16[256,3,768]{2,0,1:T(8,128)(2,1)} %param.8) | copy-start | bytes 3538948

commit v4 on v3

v4 whole, which is shorter than its diff:
```python
import functools
import math

import jax
import jax.numpy as jnp
from jax import lax
from jax.experimental import pallas as pl
from jax.experimental.pallas import tpu as pltpu
from jax.sharding import PartitionSpec as P

HD = 128
TDIM = 256
F32 = jnp.float32
BF16 = jnp.bfloat16
VMEM_LIMIT = 20 * 1024 * 1024
MOD_ROWS = 16
PARTS = 2


def flip(x, axis, bit):
    size = lax.axis_size(axis)
    return lax.ppermute(x, axis, [(i, i ^ bit) for i in range(size)])


def from_behind(x, axis, by):
    size = lax.axis_size(axis)
    pairs = [(i, i + by) for i in range(size) if 0 <= i + by < size]
    return lax.ppermute(x, axis, pairs)


def sinusoid(timesteps):
    half_width = TDIM // 2
    frequency = jnp.exp(-math.log(10000.0) * jnp.arange(half_width, dtype=F32) / half_width)
    angles = timesteps.astype(F32)[:, None] * frequency[None, :]
    return jnp.concatenate([jnp.cos(angles), jnp.sin(angles)], axis=1)


def unit_rms(vectors):
    return vectors * lax.rsqrt(jnp.mean(vectors * vectors, axis=-1, keepdims=True) + 1e-06)


def norm_rows(ha, pieces, hidden_ref, scale_ref, shift_ref):
    count = len(pieces)
    rows, full = hidden_ref.shape
    width = full // count
    step = 64
    spots = []
    for j, parts in enumerate(pieces):
        spot = pl.ds(pl.multiple_of(lax.bitwise_xor(ha, j) * width, HD), width)
        mod = parts[0][0:MOD_ROWS, :].astype(F32)
        shift_ref[j] = jnp.broadcast_to(mod[0:1], (8, width))
        scale_ref[j] = jnp.broadcast_to(1.0 + mod[1:2], (8, width))
        spots.append(spot)

    def sum_rows(tiles):
        total = None
        for tile in tiles:
            for k in range(0, width, HD):
                part = tile[:, k : k + HD]
                total = part if total is None else total + part
        return jnp.sum(total, axis=-1, keepdims=True) * (1.0 / full)

    def some_rows(sources, target, size):
        def one(i, carry):
            to = pl.ds(pl.multiple_of(target + i * step, step), step)
            spans = [(ref, pl.ds(pl.multiple_of(offset + i * step, 16), step)) for ref, offset in sources]
            mean = sum_rows(ref[at, :].astype(F32) for ref, at in spans)
            inverse = lax.rsqrt(sum_rows(jnp.square(ref[at, :].astype(F32) - mean) for ref, at in spans) + 1e-06)
            for j, (ref, at) in enumerate(spans):
                normed = ((ref[at, :].astype(F32) - mean) * inverse).reshape(step // 8, 8, width)
                out = normed * scale_ref[j][None] + shift_ref[j][None]
                hidden_ref[to, spots[j]] = out.reshape(step, width).astype(BF16)
            return carry

        lax.fori_loop(0, size // step, one, 0)

    cuts = [0] + [MOD_ROWS + rows * n // PARTS for n in range(1, PARTS + 1)]
    for n in range(PARTS):
        skip = MOD_ROWS if n == 0 else 0
        sources = [(parts[n], skip) if len(parts) > 1 else (parts[0], cuts[n] + skip) for parts in pieces]
        some_rows(sources, cuts[n] + skip - MOD_ROWS, cuts[n + 1] - cuts[n] - skip)


def attend(q, k, v, num, den):
    scores = lax.dot_general(q, k, (((1,), (1,)), ((), ())), preferred_element_type=F32)
    weights = jnp.exp(scores)
    for start in range(0, weights.shape[1], HD):
        part = weights[:, start : start + HD]
        if part.shape[1] < HD:
            part = jnp.concatenate([part, jnp.zeros((part.shape[0], HD - part.shape[1]), F32)], axis=1)
        den = part if den is None else den + part
    more = jnp.dot(weights.astype(BF16), v, preferred_element_type=F32)
    return more if num is None else num + more, den


def frame_body(own, fresh, last, splits, ids_ref, *refs):
    refs = list(refs)
    pieces = []
    for split in splits:
        pieces.append(refs[:split])
        refs = refs[split:]
    weight_ref, refs = refs[0], refs[1:]
    hidden_ref, scale_ref, shift_ref = refs[-3:]
    if own:
        q_out, k_out, v_out = refs[:-3]
    else:
        q_ref, *refs = refs[:-3]
        if not fresh:
            num_ref, den_ref, *refs = refs
        if last:
            (att_out,) = refs
        else:
            num_out, den_out = refs
    norm_rows(ids_ref[0], pieces, hidden_ref, scale_ref, shift_ref)
    width = weight_ref.shape[2]
    block = 2 * HD if width % (2 * HD) == 0 else HD
    for start in range(0, width, block):
        hidden = hidden_ref[...]
        columns = slice(start, start + block)
        key_all = jnp.dot(hidden, weight_ref[1, :, columns], preferred_element_type=F32)
        value_all = jnp.dot(hidden, weight_ref[2, :, columns], preferred_element_type=F32)
        query_all = jnp.dot(hidden, weight_ref[0, :, columns], preferred_element_type=F32) if own else None
        for head in range(0, block, HD):
            inner = slice(head, head + HD)
            at = slice(start + head, start + head + HD)
            k = unit_rms(key_all[:, inner]).astype(BF16)
            v = value_all[:, inner].astype(BF16)
            if own:
                q_out[:, at] = (unit_rms(query_all[:, inner]) * (1.0 / math.sqrt(HD))).astype(BF16)
                k_out[:, at] = k
                v_out[:, at] = v
                continue
            before = (None, None) if fresh else (num_ref[:, at], den_ref[:, at])
            num, den = attend(q_ref[:, at], k, v, *before)
            if last:
                att_out[:, at] = (num / jnp.sum(den, axis=-1, keepdims=True)).astype(BF16)
            else:
                num_out[:, at] = num
                den_out[:, at] = den


def frame_step(ids, pieces, weight, state, last=False):
    own = state is None
    pieces = [piece if isinstance(piece, tuple) else (piece,) for piece in pieces]
    count = len(pieces)
    width = pieces[0][0].shape[1]
    rows = sum(part.shape[0] for part in pieces[0]) - MOD_ROWS
    full = weight.shape[1]
    queries = rows if own else state[0].shape[0]
    args = [*(part for piece in pieces for part in piece), weight, *(state or ())]
    wide = jax.ShapeDtypeStruct((queries, width), F32)
    thin = jax.ShapeDtypeStruct((queries, width), BF16)
    outs = (thin, thin, thin) if own else (thin,) if last else (wide, wide)
    fresh = not own and len(state) == 1
    used = 3 if own else 2
    args = [pltpu.with_memory_space_constraint(x, pltpu.VMEM) if x is weight else x for x in args]
    vmem = pl.BlockSpec(memory_space=pltpu.VMEM)
    return pl.pallas_call(
        functools.partial(frame_body, own, fresh, last, [len(piece) for piece in pieces]),
        in_specs=[pl.BlockSpec(memory_space=pltpu.SMEM)] + [vmem] * len(args),
        out_specs=tuple(vmem for _ in outs),
        scratch_shapes=[
            pltpu.VMEM((rows, full), BF16),
            pltpu.VMEM((count, 8, width), F32),
            pltpu.VMEM((count, 8, width), F32),
        ],
        out_shape=outs,
        compiler_params=pltpu.CompilerParams(vmem_limit_bytes=VMEM_LIMIT),
        cost_estimate=pl.CostEstimate(
            flops=rows * full * width // 8, bytes_accessed=rows * full // 8, transcendentals=0
        ),
    )(ids, *args)


def own_body(q_ref, k_ref, v_ref, num_ref, den_ref, num_out, den_out):
    for start in range(0, q_ref.shape[1], HD):
        at = slice(start, start + HD)
        num_out[:, at], den_out[:, at] = attend(q_ref[:, at], k_ref[:, at], v_ref[:, at], num_ref[:, at], den_ref[:, at])


def own_step(q, k, v, num, den):
    vmem = pl.BlockSpec(memory_space=pltpu.VMEM)
    wide = jax.ShapeDtypeStruct(num.shape, F32)
    return pl.pallas_call(
        own_body,
        in_specs=[vmem] * 5,
        out_specs=(vmem, vmem),
        out_shape=(wide, wide),
        compiler_params=pltpu.CompilerParams(vmem_limit_bytes=VMEM_LIMIT),
        cost_estimate=pl.CostEstimate(flops=q.size, bytes_accessed=q.size, transcendentals=0),
    )(q, k, v, num, den)


def place_body(last_ref, incoming_ref, noise_ref, *refs):
    refs[-1][...] = jnp.where(last_ref[0] != 0, noise_ref[...], incoming_ref[...])


def place(n, is_last, incoming, noise_frame, queue):
    block = pl.BlockSpec(incoming.shape, lambda i: (n, 0))
    whole = pl.BlockSpec(incoming.shape, lambda i: (0, 0))
    before = [] if queue is None else [queue]
    return pl.pallas_call(
        place_body,
        grid=(1,),
        in_specs=[pl.BlockSpec(memory_space=pltpu.SMEM), whole, block] + [pl.BlockSpec(memory_space=pl.ANY)] * len(before),
        out_specs=block,
        out_shape=jax.ShapeDtypeStruct(noise_frame.shape, noise_frame.dtype),
        input_output_aliases={3: 0} if before else {},
        compiler_params=pltpu.CompilerParams(vmem_limit_bytes=VMEM_LIMIT),
        cost_estimate=pl.CostEstimate(flops=10**9, bytes_accessed=incoming.size, transcendentals=0),
    )(is_last, incoming, noise_frame, *before)


def add_body(a_ref, b_ref, out_ref):
    out_ref[...] = a_ref[...] + b_ref[...]


def add(a, b):
    vmem = pl.BlockSpec(memory_space=pltpu.VMEM)
    return pl.pallas_call(
        add_body,
        in_specs=[vmem, vmem],
        out_specs=vmem,
        out_shape=jax.ShapeDtypeStruct(a.shape, a.dtype),
        compiler_params=pltpu.CompilerParams(vmem_limit_bytes=VMEM_LIMIT),
        cost_estimate=pl.CostEstimate(flops=a.size // 8, bytes_accessed=a.size // 8, transcendentals=0),
    )(a, b)


def fetch_body(ids_ref, weight_ref, out_ref, weight_out, kept_out, sent_out, sems):
    width = out_ref.shape[0]
    copies = [pltpu.make_async_copy(weight_ref, weight_out, sems.at[0])]
    for n in range(kept_out.shape[0]):
        for core, target in enumerate((kept_out, sent_out)):
            at = pl.ds(pl.multiple_of(lax.bitwise_xor(ids_ref[0], 2 * n + core) * width, HD), width)
            copies.append(pltpu.make_async_copy(out_ref.at[:, at], target.at[n], sems.at[len(copies)]))
    for copy in copies:
        copy.start()
    for copy in copies:
        copy.wait()


def fetch(ids, weight, out_weight, ha_size):
    width = out_weight.shape[0]
    columns = ha_size // 2
    anywhere, vmem = pl.BlockSpec(memory_space=pl.ANY), pl.BlockSpec(memory_space=pltpu.VMEM)
    kept = pltpu.HBM((columns, width, width), out_weight.dtype)
    return pl.pallas_call(
        fetch_body,
        in_specs=[pl.BlockSpec(memory_space=pltpu.SMEM), anywhere, anywhere],
        out_specs=(vmem, anywhere, anywhere),
        out_shape=(pltpu.VMEM(weight.shape, weight.dtype), kept, kept),
        scratch_shapes=[pltpu.SemaphoreType.DMA((2 * columns + 1,))],
        compiler_params=pltpu.CompilerParams(vmem_limit_bytes=VMEM_LIMIT),
        cost_estimate=pl.CostEstimate(flops=0, bytes_accessed=weight.size // 8, transcendentals=0),
    )(ids, pltpu.with_memory_space_constraint(weight, pltpu.HBM), out_weight)


def project_body(step, cuts, mine_ref, theirs_ref, weight_ref, other_ref, *out_refs):
    first, end = cuts[0], cuts[-1]
    total = jnp.dot(mine_ref[first:end, :], weight_ref[step // 2], preferred_element_type=F32)
    total = total + jnp.dot(theirs_ref[first:end, :], other_ref[step // 2], preferred_element_type=F32)
    for start, stop, out_ref in zip(cuts, cuts[1:], out_refs):
        out_ref[...] = total[start - first : stop - first].astype(out_ref.dtype)


def project(mine, theirs, weight, other, step, cuts, dtype):
    width = mine.shape[1]
    rows = cuts[-1] - cuts[0]
    vmem = pl.BlockSpec(memory_space=pltpu.VMEM)
    pin = lambda x: pltpu.with_memory_space_constraint(x, pltpu.VMEM)
    outs = tuple(jax.ShapeDtypeStruct((stop - start, width), dtype) for start, stop in zip(cuts, cuts[1:]))
    return pl.pallas_call(
        functools.partial(project_body, step, cuts),
        in_specs=[vmem] * 4,
        out_specs=(vmem,) * len(outs),
        out_shape=outs,
        compiler_params=pltpu.CompilerParams(vmem_limit_bytes=VMEM_LIMIT),
        cost_estimate=pl.CostEstimate(
            flops=rows * width * width // 4, bytes_accessed=rows * width // 4, transcendentals=0
        ),
    )(mine, theirs, pin(weight), pin(other))


def cross(piece):
    size = lax.axis_size("ha")
    return [piece] + [flip(piece, "ha", step) for step in range(2, size, 2)]


def swap(piece):
    rows = piece.shape[0] - MOD_ROWS
    cuts = [0] + [MOD_ROWS + rows * n // PARTS for n in range(1, PARTS + 1)]
    return tuple(flip(piece[start:stop], "ha", 1) for start, stop in zip(cuts, cuts[1:]))


def paired(pieces):
    return [shard for piece in pieces for shard in (piece, swap(piece))]


def spread(piece):
    return paired(cross(piece))


def after_all(pieces, other):
    return [pieces[0]] + [after(piece, other) for piece in pieces[1:]]


def after(x, *others):
    return lax.optimization_barrier((x, *others))[0]


def on_device(latents, timesteps, mod_weight, qkv_weight, out_weight, noise_frame):
    frames, tok_count, width = latents.shape
    ha_size, pb_size = lax.axis_size("ha"), lax.axis_size("pb")
    ha, pb = lax.axis_index("ha"), lax.axis_index("pb")
    ids = jnp.stack([ha, pb]).astype(jnp.int32)
    piece = latents.reshape(tok_count, width)
    weight = jnp.transpose(qkv_weight, (1, 0, 2))

    embedding = sinusoid(timesteps).astype(BF16)
    modulation = jnp.einsum(
        "pe,jef->pjf", embedding, jnp.transpose(mod_weight, (1, 0, 2)), preferred_element_type=F32
    ).astype(BF16)
    gate = modulation[:, 2].astype(F32)
    mod_rows = jnp.pad(modulation[0, :2], ((0, MOD_ROWS - 2), (0, 0)))
    carried = jnp.concatenate([mod_rows, piece], axis=0)

    weight, out_local, columns = fetch(after(ids, carried), weight, out_weight, ha_size)

    def frame(pieces, state=None, last=False):
        got = frame_step(ids, pieces, weight, state, last)
        return got[0] if last else got if state is None else (state[0], *got)

    if pb_size == 4:
        pairs, middle, outward = [(0, 1), (1, 0), (2, 3), (3, 2)], [(1, 2), (2, 1)], [(1, 0), (2, 3)]
        own = cross(carried)
        first = after(lax.ppermute(carried, "pb", pairs), weight)
        first_over = cross(first)
        passed = lax.ppermute(first, "pb", middle)
        crossed = after(lax.ppermute(carried, "pb", middle), weight, first)
        beyond = lax.ppermute(crossed, "pb", outward)
        q, k, v = frame(paired(after_all(own, weight)))
        passed = after(passed, q)
        onward = lax.ppermute(passed, "pb", outward)
        second = add(crossed, after(beyond, passed))
        second_over = cross(second)
        state = frame(paired([after(p, passed) for p in first_over]), (q,))
        third = cross(add(passed, after(onward, state[1])))
        state = (q, *own_step(q, k, v, *state[1:]))
        state = frame(paired([after(p, state[1]) for p in second_over]), state)
        rest = paired([after(p, state[1]) for p in third])
        other_weight = flip(after(columns, rest), "ha", 1)
        attended = frame(rest, state, True)
    else:
        other_weight = flip(columns, "ha", 1)
        q, k, v = frame(spread(carried))
        state = (q,)
        for bit in range(1, pb_size):
            state = frame(spread(flip(carried, "pb", bit)), state, bit == pb_size - 1)
            if bit == 1:
                state = (q, *own_step(q, k, v, *state[1:]))
        attended = state

    is_last = (pb == pb_size - 1).astype(jnp.int32).reshape(1)
    done, following = [], []
    cuts = tuple(tok_count * n // 3 for n in range(4))
    theirs = flip(attended, "ha", 1)
    sent = []
    for step in range(2, ha_size, 2):
        parts = []
        for at in zip(cuts, cuts[1:]):
            parts += project(after(attended, *parts[-1:]), theirs, out_local, other_weight, step, at, BF16)
        sent.append([flip(part, "ha", step) for part in parts])
    mine = project(attended, theirs, out_local, other_weight, 0, cuts, F32)
    for n, (start, stop, branch) in enumerate(zip(cuts, cuts[1:], mine)):
        for parts in sent:
            part = after(parts[n], *mine, *done[-1:])
            branch = branch + part.astype(F32)
        advanced = (piece[start:stop].astype(F32) + gate * branch).astype(BF16)
        done.append(advanced)
        following.append(from_behind(advanced, "pb", -1))
    queue = None
    for n, incoming in enumerate(following):
        queue = place(n, is_last, incoming if n == 0 else after(incoming, queue), noise_frame, queue)
    return jnp.concatenate(done, axis=0)[None], queue[None]


def solution(mesh):
    placed = (
        P(("grp", "pb"), None, "ha"),
        P(("grp", "pb")),
        P(None, None, "ha"),
        P(None, None, "ha"),
        P("ha", None),
        P("grp", "ha"),
    )
    return jax.shard_map(
        on_device,
        mesh=mesh,
        in_specs=placed,
        out_specs=(P(("grp", "pb"), None, "ha"), P(("grp", "pb"), None, "ha")),
        check_vma=False,
    )
```

time: 114 us -> 111 us (0.974)
  waiting for transfers between devices: 37.5 us -> 26.1 us
  starting transfers between devices: 20.8 us -> 25.7 us
  local copies, waits for them, and re-layouts: 2.8 us -> 5.53 us
  Pallas kernels: 47.3 us -> 49.4 us
  other arithmetic: 3.63 us -> 2.2 us
    ppermute x17 -> x25, waiting for transfers between devices: 23.2 us -> 12.5 us  [flip(): return lax.ppermute(x, axis, [(i, i ^ bit) for i in range(size)])]
    ppermute x17 -> x25, starting transfers between devices: 10.3 us -> 14.5 us  [flip(): return lax.ppermute(x, axis, [(i, i ^ bit) for i in range(size)])]
    pallas_call x1, Pallas kernels: 5.6 us -> 7.32 us  [fetch(): pl.pallas_call(fetch_body, in_specs=[pl.BlockSpec(memory_space=pltpu.SMEM...]
    unnamed x10 -> x20, local copies, waits for them, and re-layouts: 2.77 us -> 4.45 us
    ppermute x1, starting transfers between devices: 1.58 us -> 3.09 us  [on_device(): first = after(lax.ppermute(carried, 'pb', pairs), weight)]
    add x2 -> x0, other arithmetic: 1.38 us -> none  [the longest x1 1.23 us: on_device(): second = crossed + after(beyond, passed)]
    pallas_call x6 -> x14, Pallas kernels: 41.7 us -> 42.1 us  [the longest x4 34.9 us: frame_step(): pl.pallas_call(functools.partial(frame_body, own, fresh, last, [len(piece...]
  transfers between devices with their start and end apart: 25 -> 33, of which waited for: 14 -> 17; matrix products, arithmetic and copies ran while one was open for 2% -> 3% of each run, Pallas kernels for 40% -> 43%
where the time goes in v4:
time: 111 us
  Pallas kernels  49.4 us (45%)
  waiting for transfers between devices  26.1 us (24%)
  starting transfers between devices  25.7 us (23%)
  local copies, waits for them, and re-layouts  5.53 us (5%)
  other arithmetic  2.2 us (2%)
  between operations  1.83 us (2%)
    pallas_call x4, Pallas kernels, frame_step(): pl.pallas_call(functools.partial(frame_body, own, fresh, last, [len(piece...  34.9 us
    ppermute x25, starting transfers between devices, flip(): return lax.ppermute(x, axis, [(i, i ^ bit) for i in range(size)])  14.5 us
    ppermute x25, waiting for transfers between devices, flip(): return lax.ppermute(x, axis, [(i, i ^ bit) for i in range(size)])  12.5 us
    pallas_call x1, Pallas kernels, fetch(): pl.pallas_call(fetch_body, in_specs=[pl.BlockSpec(memory_space=pltpu.SMEM...  7.32 us
    ppermute x3, waiting for transfers between devices, from_behind(): return lax.ppermute(x, axis, pairs)  6.3 us
    ppermute x1, waiting for transfers between devices, on_device(): beyond = lax.ppermute(crossed, 'pb', outward)  4.54 us
    unnamed x20, local copies, waits for them, and re-layouts  4.45 us
    ppermute x3, starting transfers between devices, from_behind(): return lax.ppermute(x, axis, pairs)  4.01 us
  transfers between devices with their start and end apart: 33, of which 17 were waited for; matrix products, arithmetic and copies ran while one was open for 3% of the time, Pallas kernels for 43%

profile of v4, /device:TPU:0, one launch (start us, length us, event | category | flops | bytes accessed | tf_op | source)
XLA Modules:
  0.0 111.0 jit_solution(17954688793682673430)
XLA Ops:
  2.3 3.1 %collective-permute-start = (bf16[400,768]{1,0:T(8,128)(2,1)S(1)}, bf16[400,768]{1,0:T(8,128)(2,1)S(1)}, u32[]{:S(2)}, u32[]{:S(2)}) collective-permute-start(bf16[400,768]{1,0:T(8,128)(2,1)S(1)} %fusion.3.refs_0_), channel_id=1, source_target_pairs={{0,4},{4,0},{8,12},{12,8},{1,5},{5,1},{9,13},{13,9},{2,6},{6,2},{1... | collective-permute-start | bytes 1843208 | tf_op jit(solution)/shard_map/ppermute | solution.py:337
  5.4 1.5 %collective-permute-start.4 = (bf16[400,768]{1,0:T(8,128)(2,1)S(1)}, bf16[400,768]{1,0:T(8,128)(2,1)S(1)}, u32[]{:S(2)}, u32[]{:S(2)}) collective-permute-start(bf16[400,768]{1,0:T(8,128)(2,1)S(1)} %fusion.3.refs_0_), channel_id=1, source_target_pairs={{0,2},{1,3},{2,0},{3,1},{4,6},{5,7},{6,4},{7,5},{8,10},{9,11},{10,... | collective-permute-start | bytes 1843208 | tf_op jit(solution)/shard_map/ppermute | solution.py:22
  9.0 2.3 %copy-done.5 = bf16[768,3072]{1,0:T(8,128)(2,1)S(1)} copy-done((bf16[768,3072]{1,0:T(8,128)(2,1)S(1)}, bf16[768,3072]{1,0:T(8,128)(2,1)}, u32[]{:S(2)}) %copy-start.5) | copy-done | bytes 4718616
  11.3 7.3 %shard_map.77 = (bf16[3,3072,768]{2,1,0:T(8,128)(2,1)S(1)}, bf16[2,768,768]{2,1,0:T(8,128)(2,1)}, bf16[2,768,768]{2,1,0:T(8,128)(2,1)}) custom-call(s32[2]{0:T(128)S(1)} %pad_add_fusion.ids_ref, bf16[3,3072,768]{2,1,0:T(8,128)(2,1)} %bitcast.34, bf16[768,3072]{1,0:T(8,128)(2,1)S(1)} %copy-done.5), custom_call_target="tpu_custom_call" | custom-call | bytes 884736 | tf_op jit(solution)/shard_map/pallas_call | solution.py:248
  19.9 1.7 %collective-permute-start.10 = (bf16[400,768]{1,0:T(8,128)(2,1)S(1)}, bf16[400,768]{1,0:T(8,128)(2,1)S(1)}, u32[]{:S(2)}, u32[]{:S(2)}) collective-permute-start(bf16[400,768]{1,0:T(8,128)(2,1)S(1)} %collective-permute-done.refs_0_), channel_id=1, source_target_pairs={{0,2},{1,3},{2,0},{3,1},{4,6},{5,7},{6,4},{7,5},{8,10},{9,11},{10,... | collective-permute-start | bytes 1843208 | tf_op jit(solution)/shard_map/ppermute | solution.py:22
  21.7 1.3 %collective-permute-start.14 = (bf16[400,768]{1,0:T(8,128)(2,1)S(1)}, bf16[400,768]{1,0:T(8,128)(2,1)S(1)}, u32[]{:S(2)}, u32[]{:S(2)}) collective-permute-start(bf16[400,768]{1,0:T(8,128)(2,1)S(1)} %collective-permute-done.13.a_ref), channel_id=1, source_target_pairs={{4,0},{8,12},{5,1},{9,13},{6,2},{10,14},{7,3},{11,15},{20,16},{24,... | collective-permute-start | bytes 1843208 | tf_op jit(solution)/shard_map/ppermute | solution.py:341
  23.7 1.4 %collective-permute-done.6.refs_5_ = bf16[192,768]{1,0:T(8,128)(2,1)S(1)} collective-permute-done((bf16[192,768]{1,0:T(8,128)(2,1)S(1)}, bf16[192,768]{1,0:T(8,128)(2,1)S(1)}, u32[]{:S(2)}, u32[]{:S(2)}) %collective-permute-start.6) | collective-permute-done | bytes 294944 | tf_op jit(solution)/shard_map/ppermute | solution.py:22
  25.1 8.7 %shard_map.78 = (bf16[384,768]{1,0:T(8,128)(2,1)S(1)}, bf16[384,768]{1,0:T(8,128)(2,1)S(1)}, bf16[384,768]{1,0:T(8,128)(2,1)S(1)}) custom-call(s32[2]{0:T(128)S(1)} %pad_add_fusion.ids_ref, bf16[400,768]{1,0:T(8,128)(2,1)S(1)} %fusion.3.refs_0_, bf16[208,768]{1,0:T(8,128)(2,1)S(1)} %collective-permute-done.2.refs_1_, ...), custom_call_target="tpu_custom_call" | custom-call | flops 113246208 | bytes 147456 | tf_op jit(solution)/shard_map/pallas_call | solution.py:158
  33.9 1.5 %collective-permute-start.7 = (bf16[400,768]{1,0:T(8,128)(2,1)S(1)}, bf16[400,768]{1,0:T(8,128)(2,1)S(1)}, u32[]{:S(2)}, u32[]{:S(2)}) collective-permute-start(bf16[400,768]{1,0:T(8,128)(2,1)S(1)} %collective-permute-done.1.a_ref), channel_id=1, source_target_pairs={{4,0},{8,12},{5,1},{9,13},{6,2},{10,14},{7,3},{11,15},{20,16},{24,... | collective-permute-start | bytes 1843208 | tf_op jit(solution)/shard_map/ppermute | solution.py:344
  36.0 4.5 %collective-permute-done.14.b_ref = bf16[400,768]{1,0:T(8,128)(2,1)S(1)} collective-permute-done((bf16[400,768]{1,0:T(8,128)(2,1)S(1)}, bf16[400,768]{1,0:T(8,128)(2,1)S(1)}, u32[]{:S(2)}, u32[]{:S(2)}) %collective-permute-start.14) | collective-permute-done | bytes 614432 | tf_op jit(solution)/shard_map/ppermute | solution.py:341
  40.6 1.6 %collective-permute-start.17 = (bf16[400,768]{1,0:T(8,128)(2,1)S(1)}, bf16[400,768]{1,0:T(8,128)(2,1)S(1)}, u32[]{:S(2)}, u32[]{:S(2)}) collective-permute-start(bf16[400,768]{1,0:T(8,128)(2,1)S(1)} %shard_map.81.refs_0_), channel_id=1, source_target_pairs={{0,2},{1,3},{2,0},{3,1},{4,6},{5,7},{6,4},{7,5},{8,10},{9,11},{10,... | collective-permute-start | bytes 1843208 | tf_op jit(solution)/shard_map/ppermute | solution.py:22
  42.9 1.4 %collective-permute-done.12.refs_5_ = bf16[192,768]{1,0:T(8,128)(2,1)S(1)} collective-permute-done((bf16[192,768]{1,0:T(8,128)(2,1)S(1)}, bf16[192,768]{1,0:T(8,128)(2,1)S(1)}, u32[]{:S(2)}, u32[]{:S(2)}) %collective-permute-start.12) | collective-permute-done | bytes 294944 | tf_op jit(solution)/shard_map/ppermute | solution.py:22
  44.3 8.6 %shard_map.79 = (f32[384,768]{1,0:T(8,128)S(1)}, f32[384,768]{1,0:T(8,128)S(1)}) custom-call(s32[2]{0:T(128)S(1)} %pad_add_fusion.ids_ref, bf16[400,768]{1,0:T(8,128)(2,1)S(1)} %collective-permute-done.refs_0_, bf16[208,768]{1,0:T(8,128)(2,1)S(1)} %collective-permute-done.8.refs_1_, bf16[192,768]{1,0:T(8,128)(2,1)S(1)} %collective-permute-done.9.refs_2_, ...), custom_call_target="tpu_custom_call" | custom-call | flops 113246208 | bytes 147456 | tf_op jit(solution)/shard_map/pallas_call | solution.py:158
  53.0 2.2 %collective-permute-done.7.b_ref = bf16[400,768]{1,0:T(8,128)(2,1)S(1)} collective-permute-done((bf16[400,768]{1,0:T(8,128)(2,1)S(1)}, bf16[400,768]{1,0:T(8,128)(2,1)S(1)}, u32[]{:S(2)}, u32[]{:S(2)}) %collective-permute-start.7) | collective-permute-done | bytes 614432 | tf_op jit(solution)/shard_map/ppermute | solution.py:344
  55.8 1.5 %shard_map.82 = (f32[384,768]{1,0:T(8,128)S(1)}, f32[384,768]{1,0:T(8,128)S(1)}) custom-call(bf16[384,768]{1,0:T(8,128)(2,1)S(1)} %get-tuple-element.42.refs_7_.q_ref, bf16[384,768]{1,0:T(8,128)(2,1)S(1)} %get-tuple-element.50.k_ref, bf16[384,768]{1,0:T(8,128)(2,1)S(1)} %get-tuple-element.51.v_ref, f32[384,768]{1,0:T(8,128)S(1)} %get-tuple-element.46.num_ref, ...), custom_call_target="tpu_custom_call" | custom-call | flops 294912 | bytes 294912 | tf_op jit(solution)/shard_map/pallas_call | solution.py:184
  58.7 1.2 %collective-permute-done.16.refs_2_ = bf16[192,768]{1,0:T(8,128)(2,1)S(1)} collective-permute-done((bf16[192,768]{1,0:T(8,128)(2,1)S(1)}, bf16[192,768]{1,0:T(8,128)(2,1)S(1)}, u32[]{:S(2)}, u32[]{:S(2)}) %collective-permute-start.16) | collective-permute-done | bytes 294944 | tf_op jit(solution)/shard_map/ppermute | solution.py:22
  60.3 8.9 %shard_map.83 = (f32[384,768]{1,0:T(8,128)S(1)}, f32[384,768]{1,0:T(8,128)S(1)}) custom-call(s32[2]{0:T(128)S(1)} %pad_add_fusion.ids_ref, bf16[400,768]{1,0:T(8,128)(2,1)S(1)} %shard_map.81.refs_0_, bf16[208,768]{1,0:T(8,128)(2,1)S(1)} %collective-permute-done.15.refs_1_, bf16[192,768]{1,0:T(8,128)(2,1)S(1)} %collective-permute-done.16.refs_2_, ...), custom_call_target="tpu_custom_call" | custom-call | flops 113246208 | bytes 147456 | tf_op jit(solution)/shard_map/pallas_call | solution.py:158
  70.6 1.2 %collective-permute-done.21.refs_2_ = bf16[192,768]{1,0:T(8,128)(2,1)S(1)} collective-permute-done((bf16[192,768]{1,0:T(8,128)(2,1)S(1)}, bf16[192,768]{1,0:T(8,128)(2,1)S(1)}, u32[]{:S(2)}, u32[]{:S(2)}) %collective-permute-start.21) | collective-permute-done | bytes 294944 | tf_op jit(solution)/shard_map/ppermute | solution.py:22
  72.4 8.7 %shard_map.84.mine_ref = bf16[384,768]{1,0:T(8,128)(2,1)S(1)} custom-call(s32[2]{0:T(128)S(1)} %pad_add_fusion.ids_ref, bf16[400,768]{1,0:T(8,128)(2,1)S(1)} %shard_map.80.refs_0_, bf16[208,768]{1,0:T(8,128)(2,1)S(1)} %collective-permute-done.20.refs_1_, bf16[192,768]{1,0:T(8,128)(2,1)S(1)} %collective-permute-done.21.refs_2_, ...), custom_call_target="tpu_custom_call" | custom-call | flops 113246208 | bytes 147456 | tf_op jit(solution)/shard_map/pallas_call | solution.py:158
  81.5 1.6 %collective-permute-done.25.theirs_ref = bf16[384,768]{1,0:T(8,128)(2,1)S(1)} collective-permute-done((bf16[384,768]{1,0:T(8,128)(2,1)S(1)}, bf16[384,768]{1,0:T(8,128)(2,1)S(1)}, u32[]{:S(2)}, u32[]{:S(2)}) %collective-permute-start.25) | collective-permute-done | bytes 589856 | tf_op jit(solution)/shard_map/ppermute | solution.py:22
  83.1 1.4 %shard_map.86 = bf16[128,768]{1,0:T(8,128)(2,1)} custom-call(bf16[384,768]{1,0:T(8,128)(2,1)S(1)} %shard_map.84.mine_ref, bf16[384,768]{1,0:T(8,128)(2,1)S(1)} %collective-permute-done.25.theirs_ref, bf16[2,768,768]{2,1,0:T(8,128)(2,1)S(1)} %copy-done.2, bf16[2,768,768]{2,1,0:T(8,128)(2,1)S(1)} %collective-permute-done.26.other_ref), custom_call_target="tpu_custom_call" | custom-call | flops 18874368 | bytes 24576 | tf_op jit(solution)/shard_map/pallas_call | solution.py:273
  84.6 1.5 %collective-permute-start.27 = (bf16[128,768]{1,0:T(8,128)(2,1)}, bf16[128,768]{1,0:T(8,128)(2,1)}, u32[]{:S(2)}, u32[]{:S(2)}) collective-permute-start(bf16[128,768]{1,0:T(8,128)(2,1)} %shard_map.86), channel_id=1, source_target_pairs={{0,2},{1,3},{2,0},{3,1},{4,6},{5,7},{6,4},{7,5},{8,10},{9,11},{10,... | collective-permute-start | bytes 589832 | tf_op jit(solution)/shard_map/ppermute | solution.py:22
  86.1 1.7 %copy-done.4 = bf16[2,768,768]{2,1,0:T(8,128)(2,1)S(1)} copy-done((bf16[2,768,768]{2,1,0:T(8,128)(2,1)S(1)}, bf16[2,768,768]{2,1,0:T(8,128)(2,1)}, u32[]{:S(2)}) %copy-start.4) | copy-done | bytes 2359320
  89.3 1.6 %collective-permute-start.29 = (bf16[128,768]{1,0:T(8,128)(2,1)S(1)}, bf16[128,768]{1,0:T(8,128)(2,1)S(1)}, u32[]{:S(2)}, u32[]{:S(2)}) collective-permute-start(bf16[128,768]{1,0:T(8,128)(2,1)S(1)} %shard_map.88), channel_id=1, source_target_pairs={{0,2},{1,3},{2,0},{3,1},{4,6},{5,7},{6,4},{7,5},{8,10},{9,11},{10,... | collective-permute-start | bytes 589832 | tf_op jit(solution)/shard_map/ppermute | solution.py:22
  90.9 1.1 shard_map.85
  93.6 1.3 %collective-permute-start.32 = (bf16[128,768]{1,0:T(8,128)(2,1)S(1)}, bf16[128,768]{1,0:T(8,128)(2,1)S(1)}, u32[]{:S(2)}, u32[]{:S(2)}) collective-permute-start(bf16[128,768]{1,0:T(8,128)(2,1)S(1)} %fusion.6), channel_id=1, source_target_pairs={{4,0},{8,4},{12,8},{5,1},{9,5},{13,9},{6,2},{10,6},{14,10},{7,3},{... | collective-permute-start | bytes 589832 | tf_op jit(solution)/shard_map/ppermute | solution.py:28
  94.9 1.8 %collective-permute-done.28 = bf16[128,768]{1,0:T(8,128)(2,1)S(1)} collective-permute-done((bf16[128,768]{1,0:T(8,128)(2,1)S(1)}, bf16[128,768]{1,0:T(8,128)(2,1)S(1)}, u32[]{:S(2)}, u32[]{:S(2)}) %collective-permute-start.28) | collective-permute-done | bytes 196640 | tf_op jit(solution)/shard_map/ppermute | solution.py:22
  96.8 1.4 %collective-permute-start.31 = (bf16[128,768]{1,0:T(8,128)(2,1)S(1)}, bf16[128,768]{1,0:T(8,128)(2,1)S(1)}, u32[]{:S(2)}, u32[]{:S(2)}) collective-permute-start(bf16[128,768]{1,0:T(8,128)(2,1)S(1)} %fusion.5), channel_id=1, source_target_pairs={{4,0},{8,4},{12,8},{5,1},{9,5},{13,9},{6,2},{10,6},{14,10},{7,3},{... | collective-permute-start | bytes 589832 | tf_op jit(solution)/shard_map/ppermute | solution.py:28
  98.2 2.1 %collective-permute-done.29 = bf16[128,768]{1,0:T(8,128)(2,1)S(1)} collective-permute-done((bf16[128,768]{1,0:T(8,128)(2,1)S(1)}, bf16[128,768]{1,0:T(8,128)(2,1)S(1)}, u32[]{:S(2)}, u32[]{:S(2)}) %collective-permute-start.29) | collective-permute-done | bytes 196640 | tf_op jit(solution)/shard_map/ppermute | solution.py:22
  100.4 1.3 %collective-permute-start.30 = (bf16[128,768]{1,0:T(8,128)(2,1)S(1)}, bf16[128,768]{1,0:T(8,128)(2,1)S(1)}, u32[]{:S(2)}, u32[]{:S(2)}) collective-permute-start(bf16[128,768]{1,0:T(8,128)(2,1)S(1)} %fusion.4), channel_id=1, source_target_pairs={{4,0},{8,4},{12,8},{5,1},{9,5},{13,9},{6,2},{10,6},{14,10},{7,3},{... | collective-permute-start | bytes 589832 | tf_op jit(solution)/shard_map/ppermute | solution.py:28
  103.4 3.5 %collective-permute-done.31.incoming_ref = bf16[128,768]{1,0:T(8,128)(2,1)S(1)} collective-permute-done((bf16[128,768]{1,0:T(8,128)(2,1)S(1)}, bf16[128,768]{1,0:T(8,128)(2,1)S(1)}, u32[]{:S(2)}, u32[]{:S(2)}) %collective-permute-start.31) | collective-permute-done | bytes 196640 | tf_op jit(solution)/shard_map/ppermute | solution.py:28
  107.6 2.7 %collective-permute-done.30.incoming_ref = bf16[128,768]{1,0:T(8,128)(2,1)S(1)} collective-permute-done((bf16[128,768]{1,0:T(8,128)(2,1)S(1)}, bf16[128,768]{1,0:T(8,128)(2,1)S(1)}, u32[]{:S(2)}, u32[]{:S(2)}) %collective-permute-start.30) | collective-permute-done | bytes 196640 | tf_op jit(solution)/shard_map/ppermute | solution.py:28
  (98 shorter events, 17.6 us)
Async XLA Ops:
  2.3 16.9 %collective-permute-start = (bf16[400,768]{1,0:T(8,128)(2,1)S(1)}, bf16[400,768]{1,0:T(8,128)(2,1)S(1)}, u32[]{:S(2)}, u32[]{:S(2)}) collective-permute-start(bf16[400,768]{1,0:T(8,128)(2,1)S(1)} %fusion.3.refs_0_), channel_id=1, source_target_pairs={{0,4},{4,0},{8,12},{12,8},{1,5},{5,1},{9,13},{13,9},{2,6},{6,2},{1... | collective-permute-start | bytes 1843208 | tf_op jit(solution)/shard_map/ppermute | solution.py:337
  5.4 16.3 %collective-permute-start.4 = (bf16[400,768]{1,0:T(8,128)(2,1)S(1)}, bf16[400,768]{1,0:T(8,128)(2,1)S(1)}, u32[]{:S(2)}, u32[]{:S(2)}) collective-permute-start(bf16[400,768]{1,0:T(8,128)(2,1)S(1)} %fusion.3.refs_0_), channel_id=1, source_target_pairs={{0,2},{1,3},{2,0},{3,1},{4,6},{5,7},{6,4},{7,5},{8,10},{9,11},{10,... | collective-permute-start | bytes 1843208 | tf_op jit(solution)/shard_map/ppermute | solution.py:22
  6.9 13.1 %collective-permute-start.13 = (bf16[400,768]{1,0:T(8,128)(2,1)S(1)}, bf16[400,768]{1,0:T(8,128)(2,1)S(1)}, u32[]{:S(2)}, u32[]{:S(2)}) collective-permute-start(bf16[400,768]{1,0:T(8,128)(2,1)S(1)} %fusion.3.refs_0_), channel_id=1, source_target_pairs={{4,8},{8,4},{5,9},{9,5},{6,10},{10,6},{7,11},{11,7},{20,24},{24,20... | collective-permute-start | bytes 1843208 | tf_op jit(solution)/shard_map/ppermute | solution.py:340
  7.6 15.5 %collective-permute-start.2 = (bf16[208,768]{1,0:T(8,128)(2,1)S(1)}, bf16[208,768]{1,0:T(8,128)(2,1)S(1)}, u32[]{:S(2)}, u32[]{:S(2)}) collective-permute-start(bf16[208,768]{1,0:T(8,128)(2,1)S(1)} %slice.93), channel_id=1, source_target_pairs={{0,1},{1,0},{2,3},{3,2},{4,5},{5,4},{6,7},{7,6},{8,9},{9,8},{10,11... | collective-permute-start | bytes 958472 | tf_op jit(solution)/shard_map/ppermute | solution.py:22
  8.4 14.6 %collective-permute-start.3 = (bf16[192,768]{1,0:T(8,128)(2,1)}, bf16[192,768]{1,0:T(8,128)(2,1)S(1)}, u32[]{:S(2)}, u32[]{:S(2)}) collective-permute-start(bf16[192,768]{1,0:T(8,128)(2,1)} %slice_bitcast_fusion), channel_id=1, source_target_pairs={{0,1},{1,0},{2,3},{3,2},{4,5},{5,4},{6,7},{7,6},{8,9},{9,8},{10,11... | collective-permute-start | bytes 884744 | tf_op jit(solution)/shard_map/ppermute | solution.py:22
  19.2 14.6 %collective-permute-start.1 = (bf16[400,768]{1,0:T(8,128)(2,1)S(1)}, bf16[400,768]{1,0:T(8,128)(2,1)S(1)}, u32[]{:S(2)}, u32[]{:S(2)}) collective-permute-start(bf16[400,768]{1,0:T(8,128)(2,1)S(1)} %collective-permute-done.refs_0_), channel_id=1, source_target_pairs={{4,8},{8,4},{5,9},{9,5},{6,10},{10,6},{7,11},{11,7},{20,24},{24,20... | collective-permute-start | bytes 1843208 | tf_op jit(solution)/shard_map/ppermute | solution.py:339
  19.9 22.3 %collective-permute-start.10 = (bf16[400,768]{1,0:T(8,128)(2,1)S(1)}, bf16[400,768]{1,0:T(8,128)(2,1)S(1)}, u32[]{:S(2)}, u32[]{:S(2)}) collective-permute-start(bf16[400,768]{1,0:T(8,128)(2,1)S(1)} %collective-permute-done.refs_0_), channel_id=1, source_target_pairs={{0,2},{1,3},{2,0},{3,1},{4,6},{5,7},{6,4},{7,5},{8,10},{9,11},{10,... | collective-permute-start | bytes 1843208 | tf_op jit(solution)/shard_map/ppermute | solution.py:22
  21.7 18.9 %collective-permute-start.14 = (bf16[400,768]{1,0:T(8,128)(2,1)S(1)}, bf16[400,768]{1,0:T(8,128)(2,1)S(1)}, u32[]{:S(2)}, u32[]{:S(2)}) collective-permute-start(bf16[400,768]{1,0:T(8,128)(2,1)S(1)} %collective-permute-done.13.a_ref), channel_id=1, source_target_pairs={{4,0},{8,12},{5,1},{9,13},{6,2},{10,14},{7,3},{11,15},{20,16},{24,... | collective-permute-start | bytes 1843208 | tf_op jit(solution)/shard_map/ppermute | solution.py:341
  23.0 2.1 %collective-permute-start.5 = (bf16[208,768]{1,0:T(8,128)(2,1)S(1)}, bf16[208,768]{1,0:T(8,128)(2,1)S(1)}, u32[]{:S(2)}, u32[]{:S(2)}) collective-permute-start(bf16[208,768]{1,0:T(8,128)(2,1)S(1)} %slice.75), channel_id=1, source_target_pairs={{0,1},{1,0},{2,3},{3,2},{4,5},{5,4},{6,7},{7,6},{8,9},{9,8},{10,11... | collective-permute-start | bytes 958472 | tf_op jit(solution)/shard_map/ppermute | solution.py:22
  23.1 2.0 %collective-permute-start.6 = (bf16[192,768]{1,0:T(8,128)(2,1)S(1)}, bf16[192,768]{1,0:T(8,128)(2,1)S(1)}, u32[]{:S(2)}, u32[]{:S(2)}) collective-permute-start(bf16[192,768]{1,0:T(8,128)(2,1)S(1)} %slice.76), channel_id=1, source_target_pairs={{0,1},{1,0},{2,3},{3,2},{4,5},{5,4},{6,7},{7,6},{8,9},{9,8},{10,11... | collective-permute-start | bytes 884744 | tf_op jit(solution)/shard_map/ppermute | solution.py:22
  33.9 21.3 %collective-permute-start.7 = (bf16[400,768]{1,0:T(8,128)(2,1)S(1)}, bf16[400,768]{1,0:T(8,128)(2,1)S(1)}, u32[]{:S(2)}, u32[]{:S(2)}) collective-permute-start(bf16[400,768]{1,0:T(8,128)(2,1)S(1)} %collective-permute-done.1.a_ref), channel_id=1, source_target_pairs={{4,0},{8,12},{5,1},{9,13},{6,2},{10,14},{7,3},{11,15},{20,16},{24,... | collective-permute-start | bytes 1843208 | tf_op jit(solution)/shard_map/ppermute | solution.py:344
  35.4 7.0 %collective-permute-start.9 = (bf16[192,768]{1,0:T(8,128)(2,1)S(1)}, bf16[192,768]{1,0:T(8,128)(2,1)S(1)}, u32[]{:S(2)}, u32[]{:S(2)}) collective-permute-start(bf16[192,768]{1,0:T(8,128)(2,1)S(1)} %slice.78), channel_id=1, source_target_pairs={{0,1},{1,0},{2,3},{3,2},{4,5},{5,4},{6,7},{7,6},{8,9},{9,8},{10,11... | collective-permute-start | bytes 884744 | tf_op jit(solution)/shard_map/ppermute | solution.py:22
  35.6 8.7 %collective-permute-start.8 = (bf16[208,768]{1,0:T(8,128)(2,1)S(1)}, bf16[208,768]{1,0:T(8,128)(2,1)S(1)}, u32[]{:S(2)}, u32[]{:S(2)}) collective-permute-start(bf16[208,768]{1,0:T(8,128)(2,1)S(1)} %slice.77), channel_id=1, source_target_pairs={{0,1},{1,0},{2,3},{3,2},{4,5},{5,4},{6,7},{7,6},{8,9},{9,8},{10,11... | collective-permute-start | bytes 958472 | tf_op jit(solution)/shard_map/ppermute | solution.py:22
  40.6 16.8 %collective-permute-start.17 = (bf16[400,768]{1,0:T(8,128)(2,1)S(1)}, bf16[400,768]{1,0:T(8,128)(2,1)S(1)}, u32[]{:S(2)}, u32[]{:S(2)}) collective-permute-start(bf16[400,768]{1,0:T(8,128)(2,1)S(1)} %shard_map.81.refs_0_), channel_id=1, source_target_pairs={{0,2},{1,3},{2,0},{3,1},{4,6},{5,7},{6,4},{7,5},{8,10},{9,11},{10,... | collective-permute-start | bytes 1843208 | tf_op jit(solution)/shard_map/ppermute | solution.py:22
  42.2 2.1 %collective-permute-start.11 = (bf16[208,768]{1,0:T(8,128)(2,1)S(1)}, bf16[208,768]{1,0:T(8,128)(2,1)S(1)}, u32[]{:S(2)}, u32[]{:S(2)}) collective-permute-start(bf16[208,768]{1,0:T(8,128)(2,1)S(1)} %slice.79), channel_id=1, source_target_pairs={{0,1},{1,0},{2,3},{3,2},{4,5},{5,4},{6,7},{7,6},{8,9},{9,8},{10,11... | collective-permute-start | bytes 958472 | tf_op jit(solution)/shard_map/ppermute | solution.py:22
  42.3 2.0 %collective-permute-start.12 = (bf16[192,768]{1,0:T(8,128)(2,1)S(1)}, bf16[192,768]{1,0:T(8,128)(2,1)S(1)}, u32[]{:S(2)}, u32[]{:S(2)}) collective-permute-start(bf16[192,768]{1,0:T(8,128)(2,1)S(1)} %slice.80), channel_id=1, source_target_pairs={{0,1},{1,0},{2,3},{3,2},{4,5},{5,4},{6,7},{7,6},{8,9},{9,8},{10,11... | collective-permute-start | bytes 884744 | tf_op jit(solution)/shard_map/ppermute | solution.py:22
  55.2 14.3 %collective-permute-start.22 = (bf16[400,768]{1,0:T(8,128)(2,1)S(1)}, bf16[400,768]{1,0:T(8,128)(2,1)S(1)}, u32[]{:S(2)}, u32[]{:S(2)}) collective-permute-start(bf16[400,768]{1,0:T(8,128)(2,1)S(1)} %shard_map.80.refs_0_), channel_id=1, source_target_pairs={{0,2},{1,3},{2,0},{3,1},{4,6},{5,7},{6,4},{7,5},{8,10},{9,11},{10,... | collective-permute-start | bytes 1843208 | tf_op jit(solution)/shard_map/ppermute | solution.py:22
  57.3 2.6 %collective-permute-start.15 = (bf16[208,768]{1,0:T(8,128)(2,1)S(1)}, bf16[208,768]{1,0:T(8,128)(2,1)S(1)}, u32[]{:S(2)}, u32[]{:S(2)}) collective-permute-start(bf16[208,768]{1,0:T(8,128)(2,1)S(1)} %slice.81), channel_id=1, source_target_pairs={{0,1},{1,0},{2,3},{3,2},{4,5},{5,4},{6,7},{7,6},{8,9},{9,8},{10,11... | collective-permute-start | bytes 958472 | tf_op jit(solution)/shard_map/ppermute | solution.py:22
  57.4 2.9 %collective-permute-start.18 = (bf16[208,768]{1,0:T(8,128)(2,1)S(1)}, bf16[208,768]{1,0:T(8,128)(2,1)S(1)}, u32[]{:S(2)}, u32[]{:S(2)}) collective-permute-start(bf16[208,768]{1,0:T(8,128)(2,1)S(1)} %slice.83), channel_id=1, source_target_pairs={{0,1},{1,0},{2,3},{3,2},{4,5},{5,4},{6,7},{7,6},{8,9},{9,8},{10,11... | collective-permute-start | bytes 958472 | tf_op jit(solution)/shard_map/ppermute | solution.py:22
  58.0 1.9 %collective-permute-start.16 = (bf16[192,768]{1,0:T(8,128)(2,1)S(1)}, bf16[192,768]{1,0:T(8,128)(2,1)S(1)}, u32[]{:S(2)}, u32[]{:S(2)}) collective-permute-start(bf16[192,768]{1,0:T(8,128)(2,1)S(1)} %slice.82), channel_id=1, source_target_pairs={{0,1},{1,0},{2,3},{3,2},{4,5},{5,4},{6,7},{7,6},{8,9},{9,8},{10,11... | collective-permute-start | bytes 884744 | tf_op jit(solution)/shard_map/ppermute | solution.py:22
  58.1 2.2 %collective-permute-start.19 = (bf16[192,768]{1,0:T(8,128)(2,1)S(1)}, bf16[192,768]{1,0:T(8,128)(2,1)S(1)}, u32[]{:S(2)}, u32[]{:S(2)}) collective-permute-start(bf16[192,768]{1,0:T(8,128)(2,1)S(1)} %slice.84), channel_id=1, source_target_pairs={{0,1},{1,0},{2,3},{3,2},{4,5},{5,4},{6,7},{7,6},{8,9},{9,8},{10,11... | collective-permute-start | bytes 884744 | tf_op jit(solution)/shard_map/ppermute | solution.py:22
  69.2 2.6 %collective-permute-start.20 = (bf16[208,768]{1,0:T(8,128)(2,1)S(1)}, bf16[208,768]{1,0:T(8,128)(2,1)S(1)}, u32[]{:S(2)}, u32[]{:S(2)}) collective-permute-start(bf16[208,768]{1,0:T(8,128)(2,1)S(1)} %slice.85), channel_id=1, source_target_pairs={{0,1},{1,0},{2,3},{3,2},{4,5},{5,4},{6,7},{7,6},{8,9},{9,8},{10,11... | collective-permute-start | bytes 958472 | tf_op jit(solution)/shard_map/ppermute | solution.py:22
  69.6 2.6 %collective-permute-start.23 = (bf16[208,768]{1,0:T(8,128)(2,1)S(1)}, bf16[208,768]{1,0:T(8,128)(2,1)S(1)}, u32[]{:S(2)}, u32[]{:S(2)}) collective-permute-start(bf16[208,768]{1,0:T(8,128)(2,1)S(1)} %slice.87), channel_id=1, source_target_pairs={{0,1},{1,0},{2,3},{3,2},{4,5},{5,4},{6,7},{7,6},{8,9},{9,8},{10,11... | collective-permute-start | bytes 958472 | tf_op jit(solution)/shard_map/ppermute | solution.py:22
  70.3 1.9 %collective-permute-start.24 = (bf16[192,768]{1,0:T(8,128)(2,1)S(1)}, bf16[192,768]{1,0:T(8,128)(2,1)S(1)}, u32[]{:S(2)}, u32[]{:S(2)}) collective-permute-start(bf16[192,768]{1,0:T(8,128)(2,1)S(1)} %slice.88), channel_id=1, source_target_pairs={{0,1},{1,0},{2,3},{3,2},{4,5},{5,4},{6,7},{7,6},{8,9},{9,8},{10,11... | collective-permute-start | bytes 884744 | tf_op jit(solution)/shard_map/ppermute | solution.py:22
  72.2 10.9 %collective-permute-start.26 = (bf16[2,768,768]{2,1,0:T(8,128)(2,1)S(1)}, bf16[2,768,768]{2,1,0:T(8,128)(2,1)S(1)}, u32[]{:S(2)}, u32[]{:S(2)}) collective-permute-start(bf16[2,768,768]{2,1,0:T(8,128)(2,1)S(1)} %copy-done.9), channel_id=1, source_target_pairs={{0,1},{1,0},{2,3},{3,2},{4,5},{5,4},{6,7},{7,6},{8,9},{9,8},{10,11... | collective-permute-start | bytes 7077896 | tf_op jit(solution)/shard_map/ppermute | solution.py:22
  81.0 2.1 %collective-permute-start.25 = (bf16[384,768]{1,0:T(8,128)(2,1)S(1)}, bf16[384,768]{1,0:T(8,128)(2,1)S(1)}, u32[]{:S(2)}, u32[]{:S(2)}) collective-permute-start(bf16[384,768]{1,0:T(8,128)(2,1)S(1)} %shard_map.84.mine_ref), channel_id=1, source_target_pairs={{0,1},{1,0},{2,3},{3,2},{4,5},{5,4},{6,7},{7,6},{8,9},{9,8},{10,11... | collective-permute-start | bytes 1769480 | tf_op jit(solution)/shard_map/ppermute | solution.py:22
  84.6 8.0 %collective-permute-start.27 = (bf16[128,768]{1,0:T(8,128)(2,1)}, bf16[128,768]{1,0:T(8,128)(2,1)}, u32[]{:S(2)}, u32[]{:S(2)}) collective-permute-start(bf16[128,768]{1,0:T(8,128)(2,1)} %shard_map.86), channel_id=1, source_target_pairs={{0,2},{1,3},{2,0},{3,1},{4,6},{5,7},{6,4},{7,5},{8,10},{9,11},{10,... | collective-permute-start | bytes 589832 | tf_op jit(solution)/shard_map/ppermute | solution.py:22
  88.2 8.5 %collective-permute-start.28 = (bf16[128,768]{1,0:T(8,128)(2,1)S(1)}, bf16[128,768]{1,0:T(8,128)(2,1)S(1)}, u32[]{:S(2)}, u32[]{:S(2)}) collective-permute-start(bf16[128,768]{1,0:T(8,128)(2,1)S(1)} %shard_map.87), channel_id=1, source_target_pairs={{0,2},{1,3},{2,0},{3,1},{4,6},{5,7},{6,4},{7,5},{8,10},{9,11},{10,... | collective-permute-start | bytes 589832 | tf_op jit(solution)/shard_map/ppermute | solution.py:22
  89.3 11.0 %collective-permute-start.29 = (bf16[128,768]{1,0:T(8,128)(2,1)S(1)}, bf16[128,768]{1,0:T(8,128)(2,1)S(1)}, u32[]{:S(2)}, u32[]{:S(2)}) collective-permute-start(bf16[128,768]{1,0:T(8,128)(2,1)S(1)} %shard_map.88), channel_id=1, source_target_pairs={{0,2},{1,3},{2,0},{3,1},{4,6},{5,7},{6,4},{7,5},{8,10},{9,11},{10,... | collective-permute-start | bytes 589832 | tf_op jit(solution)/shard_map/ppermute | solution.py:22
  93.6 9.1 %collective-permute-start.32 = (bf16[128,768]{1,0:T(8,128)(2,1)S(1)}, bf16[128,768]{1,0:T(8,128)(2,1)S(1)}, u32[]{:S(2)}, u32[]{:S(2)}) collective-permute-start(bf16[128,768]{1,0:T(8,128)(2,1)S(1)} %fusion.6), channel_id=1, source_target_pairs={{4,0},{8,4},{12,8},{5,1},{9,5},{13,9},{6,2},{10,6},{14,10},{7,3},{... | collective-permute-start | bytes 589832 | tf_op jit(solution)/shard_map/ppermute | solution.py:28
  96.8 10.1 %collective-permute-start.31 = (bf16[128,768]{1,0:T(8,128)(2,1)S(1)}, bf16[128,768]{1,0:T(8,128)(2,1)S(1)}, u32[]{:S(2)}, u32[]{:S(2)}) collective-permute-start(bf16[128,768]{1,0:T(8,128)(2,1)S(1)} %fusion.5), channel_id=1, source_target_pairs={{4,0},{8,4},{12,8},{5,1},{9,5},{13,9},{6,2},{10,6},{14,10},{7,3},{... | collective-permute-start | bytes 589832 | tf_op jit(solution)/shard_map/ppermute | solution.py:28
  100.4 9.9 %collective-permute-start.30 = (bf16[128,768]{1,0:T(8,128)(2,1)S(1)}, bf16[128,768]{1,0:T(8,128)(2,1)S(1)}, u32[]{:S(2)}, u32[]{:S(2)}) collective-permute-start(bf16[128,768]{1,0:T(8,128)(2,1)S(1)} %fusion.4), channel_id=1, source_target_pairs={{4,0},{8,4},{12,8},{5,1},{9,5},{13,9},{6,2},{10,6},{14,10},{7,3},{... | collective-permute-start | bytes 589832 | tf_op jit(solution)/shard_map/ppermute | solution.py:28
  (11 other events, 37.3 us)

commit v5 on v4

--- a/solution.py
+++ b/solution.py
@@ -191,12 +191,30 @@
     )(q, k, v, num, den)
 
 
+def finish_body(latent_ref, gate_ref, *refs):
+    *branch_refs, out_ref = refs
+    branch = sum(ref[...].astype(F32) for ref in branch_refs)
+    out_ref[...] = (latent_ref[...].astype(F32) + gate_ref[...] * branch).astype(BF16)
+
+
+def finish(latents, gate, *branches):
+    vmem = pl.BlockSpec(memory_space=pltpu.VMEM)
+    return pl.pallas_call(
+        finish_body,
+        in_specs=[vmem] * (2 + len(branches)),
+        out_specs=vmem,
+        out_shape=jax.ShapeDtypeStruct(latents.shape, BF16),
+        compiler_params=pltpu.CompilerParams(vmem_limit_bytes=VMEM_LIMIT),
+        cost_estimate=pl.CostEstimate(flops=latents.size, bytes_accessed=latents.size, transcendentals=0),
+    )(latents, gate, *branches)
+
+
 def place_body(last_ref, incoming_ref, noise_ref, *refs):
     refs[-1][...] = jnp.where(last_ref[0] != 0, noise_ref[...], incoming_ref[...])
 
 
 def place(n, is_last, incoming, noise_frame, queue):
-    block = pl.BlockSpec(incoming.shape, lambda i: (n, 0))
+    block = pl.BlockSpec((pl.Element(incoming.shape[0]), pl.Element(incoming.shape[1])), lambda i: (n, 0))
     whole = pl.BlockSpec(incoming.shape, lambda i: (0, 0))
     before = [] if queue is None else [queue]
     return pl.pallas_call(
@@ -363,7 +381,7 @@
 
     is_last = (pb == pb_size - 1).astype(jnp.int32).reshape(1)
     done, following = [], []
-    cuts = tuple(tok_count * n // 3 for n in range(4))
+    cuts = tuple(tok_count * n // 24 for n in (0, 7, 15, 24))
     theirs = flip(attended, "ha", 1)
     sent = []
     for step in range(2, ha_size, 2):
@@ -373,15 +391,13 @@
         sent.append([flip(part, "ha", step) for part in parts])
     mine = project(attended, theirs, out_local, other_weight, 0, cuts, F32)
     for n, (start, stop, branch) in enumerate(zip(cuts, cuts[1:], mine)):
-        for parts in sent:
-            part = after(parts[n], *mine, *done[-1:])
-            branch = branch + part.astype(F32)
-        advanced = (piece[start:stop].astype(F32) + gate * branch).astype(BF16)
+        others = [after(parts[n], *mine, *done[-1:]) for parts in sent]
+        advanced = finish(piece[start:stop], gate, branch, *others)
         done.append(advanced)
         following.append(from_behind(advanced, "pb", -1))
     queue = None
     for n, incoming in enumerate(following):
-        queue = place(n, is_last, incoming if n == 0 else after(incoming, queue), noise_frame, queue)
+        queue = place(cuts[n], is_last, incoming if n == 0 else after(incoming, queue), noise_frame, queue)
     return jnp.concatenate(done, axis=0)[None], queue[None]
 
 

time: 111 us -> 110 us (level)
  waiting for transfers between devices: 26.1 us -> 27.8 us
  local copies, waits for them, and re-layouts: 5.53 us -> 3.9 us
  other arithmetic: 2.2 us -> 1.04 us
    ppermute x25, waiting for transfers between devices: 12.5 us -> 14.8 us  [flip(): return lax.ppermute(x, axis, [(i, i ^ bit) for i in range(size)])]
    unnamed x20 -> x16, local copies, waits for them, and re-layouts: 4.45 us -> 2.78 us
    convert_element_type x3 -> x0, other arithmetic: 1.15 us -> none  [on_device(): advanced = (piece[start:stop].astype(F32) + gate * branch).astype(BF16)]
  transfers between devices with their start and end apart: 33 -> 33, of which waited for: 17 -> 16; matrix products, arithmetic and copies ran while one was open for 3% -> 2% of each run, Pallas kernels for 43% -> 43%
where the time goes in v5:
time: 110 us; the launch traced here: 109 us
  Pallas kernels  48.8 us (44%)
  waiting for transfers between devices  27.8 us (25%)
  starting transfers between devices  25.8 us (23%)
  local copies, waits for them, and re-layouts  3.9 us (4%)
  between operations  1.84 us (2%)
    pallas_call x4, Pallas kernels, frame_step(): pl.pallas_call(functools.partial(frame_body, own, fresh, last, [len(piece...  34.9 us
    ppermute x25, waiting for transfers between devices, flip(): return lax.ppermute(x, axis, [(i, i ^ bit) for i in range(size)])  14.8 us
    ppermute x25, starting transfers between devices, flip(): return lax.ppermute(x, axis, [(i, i ^ bit) for i in range(size)])  14.6 us
    pallas_call x1, Pallas kernels, fetch(): pl.pallas_call(fetch_body, in_specs=[pl.BlockSpec(memory_space=pltpu.SMEM...  7.32 us
    ppermute x3, waiting for transfers between devices, from_behind(): return lax.ppermute(x, axis, pairs)  5.76 us
    ppermute x1, waiting for transfers between devices, on_device(): beyond = lax.ppermute(crossed, 'pb', outward)  4.54 us
    ppermute x3, starting transfers between devices, from_behind(): return lax.ppermute(x, axis, pairs)  4.01 us
    ppermute x1, starting transfers between devices, on_device(): first = after(lax.ppermute(carried, 'pb', pairs), weight)  3.09 us
  transfers between devices with their start and end apart: 33, of which 16 were waited for; matrix products, arithmetic and copies ran while one was open for 2% of the time, Pallas kernels for 43%

profile of v5, /device:TPU:0, one launch (start us, length us, event | category | flops | bytes accessed | tf_op | source)
XLA Modules:
  0.0 109.4 jit_solution(16620743876278364804)
XLA Ops:
  2.3 3.1 %collective-permute-start = (bf16[400,768]{1,0:T(8,128)(2,1)S(1)}, bf16[400,768]{1,0:T(8,128)(2,1)S(1)}, u32[]{:S(2)}, u32[]{:S(2)}) collective-permute-start(bf16[400,768]{1,0:T(8,128)(2,1)S(1)} %fusion.3.refs_0_), channel_id=1, source_target_pairs={{0,4},{4,0},{8,12},{12,8},{1,5},{5,1},{9,13},{13,9},{2,6},{6,2},{1... | collective-permute-start | bytes 1843208 | tf_op jit(solution)/shard_map/ppermute | solution.py:355
  5.4 1.5 %collective-permute-start.4 = (bf16[400,768]{1,0:T(8,128)(2,1)S(1)}, bf16[400,768]{1,0:T(8,128)(2,1)S(1)}, u32[]{:S(2)}, u32[]{:S(2)}) collective-permute-start(bf16[400,768]{1,0:T(8,128)(2,1)S(1)} %fusion.3.refs_0_), channel_id=1, source_target_pairs={{0,2},{1,3},{2,0},{3,1},{4,6},{5,7},{6,4},{7,5},{8,10},{9,11},{10,... | collective-permute-start | bytes 1843208 | tf_op jit(solution)/shard_map/ppermute | solution.py:22
  9.0 2.3 %copy-done.3 = bf16[768,3072]{1,0:T(8,128)(2,1)S(1)} copy-done((bf16[768,3072]{1,0:T(8,128)(2,1)S(1)}, bf16[768,3072]{1,0:T(8,128)(2,1)}, u32[]{:S(2)}) %copy-start.3) | copy-done | bytes 4718616
  11.3 7.3 %shard_map.77 = (bf16[3,3072,768]{2,1,0:T(8,128)(2,1)S(1)}, bf16[2,768,768]{2,1,0:T(8,128)(2,1)}, bf16[2,768,768]{2,1,0:T(8,128)(2,1)}) custom-call(s32[2]{0:T(128)S(1)} %pad_add_fusion.ids_ref, bf16[3,3072,768]{2,1,0:T(8,128)(2,1)} %bitcast.36, bf16[768,3072]{1,0:T(8,128)(2,1)S(1)} %copy-done.3), custom_call_target="tpu_custom_call" | custom-call | bytes 884736 | tf_op jit(solution)/shard_map/pallas_call | solution.py:266
  19.9 1.7 %collective-permute-start.10 = (bf16[400,768]{1,0:T(8,128)(2,1)S(1)}, bf16[400,768]{1,0:T(8,128)(2,1)S(1)}, u32[]{:S(2)}, u32[]{:S(2)}) collective-permute-start(bf16[400,768]{1,0:T(8,128)(2,1)S(1)} %collective-permute-done.refs_0_), channel_id=1, source_target_pairs={{0,2},{1,3},{2,0},{3,1},{4,6},{5,7},{6,4},{7,5},{8,10},{9,11},{10,... | collective-permute-start | bytes 1843208 | tf_op jit(solution)/shard_map/ppermute | solution.py:22
  21.7 1.3 %collective-permute-start.14 = (bf16[400,768]{1,0:T(8,128)(2,1)S(1)}, bf16[400,768]{1,0:T(8,128)(2,1)S(1)}, u32[]{:S(2)}, u32[]{:S(2)}) collective-permute-start(bf16[400,768]{1,0:T(8,128)(2,1)S(1)} %collective-permute-done.13.a_ref), channel_id=1, source_target_pairs={{4,0},{8,12},{5,1},{9,13},{6,2},{10,14},{7,3},{11,15},{20,16},{24,... | collective-permute-start | bytes 1843208 | tf_op jit(solution)/shard_map/ppermute | solution.py:359
  23.7 1.4 %collective-permute-done.6.refs_5_ = bf16[192,768]{1,0:T(8,128)(2,1)S(1)} collective-permute-done((bf16[192,768]{1,0:T(8,128)(2,1)S(1)}, bf16[192,768]{1,0:T(8,128)(2,1)S(1)}, u32[]{:S(2)}, u32[]{:S(2)}) %collective-permute-start.6) | collective-permute-done | bytes 294944 | tf_op jit(solution)/shard_map/ppermute | solution.py:22
  25.1 8.7 %shard_map.78 = (bf16[384,768]{1,0:T(8,128)(2,1)S(1)}, bf16[384,768]{1,0:T(8,128)(2,1)S(1)}, bf16[384,768]{1,0:T(8,128)(2,1)S(1)}) custom-call(s32[2]{0:T(128)S(1)} %pad_add_fusion.ids_ref, bf16[400,768]{1,0:T(8,128)(2,1)S(1)} %fusion.3.refs_0_, bf16[208,768]{1,0:T(8,128)(2,1)S(1)} %collective-permute-done.2.refs_1_, ...), custom_call_target="tpu_custom_call" | custom-call | flops 113246208 | bytes 147456 | tf_op jit(solution)/shard_map/pallas_call | solution.py:158
  33.8 1.5 %collective-permute-start.7 = (bf16[400,768]{1,0:T(8,128)(2,1)S(1)}, bf16[400,768]{1,0:T(8,128)(2,1)S(1)}, u32[]{:S(2)}, u32[]{:S(2)}) collective-permute-start(bf16[400,768]{1,0:T(8,128)(2,1)S(1)} %collective-permute-done.1.a_ref), channel_id=1, source_target_pairs={{4,0},{8,12},{5,1},{9,13},{6,2},{10,14},{7,3},{11,15},{20,16},{24,... | collective-permute-start | bytes 1843208 | tf_op jit(solution)/shard_map/ppermute | solution.py:362
  36.0 4.5 %collective-permute-done.14.b_ref = bf16[400,768]{1,0:T(8,128)(2,1)S(1)} collective-permute-done((bf16[400,768]{1,0:T(8,128)(2,1)S(1)}, bf16[400,768]{1,0:T(8,128)(2,1)S(1)}, u32[]{:S(2)}, u32[]{:S(2)}) %collective-permute-start.14) | collective-permute-done | bytes 614432 | tf_op jit(solution)/shard_map/ppermute | solution.py:359
  40.6 1.6 %collective-permute-start.17 = (bf16[400,768]{1,0:T(8,128)(2,1)S(1)}, bf16[400,768]{1,0:T(8,128)(2,1)S(1)}, u32[]{:S(2)}, u32[]{:S(2)}) collective-permute-start(bf16[400,768]{1,0:T(8,128)(2,1)S(1)} %shard_map.81.refs_0_), channel_id=1, source_target_pairs={{0,2},{1,3},{2,0},{3,1},{4,6},{5,7},{6,4},{7,5},{8,10},{9,11},{10,... | collective-permute-start | bytes 1843208 | tf_op jit(solution)/shard_map/ppermute | solution.py:22
  42.9 1.4 %collective-permute-done.12.refs_5_ = bf16[192,768]{1,0:T(8,128)(2,1)S(1)} collective-permute-done((bf16[192,768]{1,0:T(8,128)(2,1)S(1)}, bf16[192,768]{1,0:T(8,128)(2,1)S(1)}, u32[]{:S(2)}, u32[]{:S(2)}) %collective-permute-start.12) | collective-permute-done | bytes 294944 | tf_op jit(solution)/shard_map/ppermute | solution.py:22
  44.3 8.6 %shard_map.79 = (f32[384,768]{1,0:T(8,128)S(1)}, f32[384,768]{1,0:T(8,128)S(1)}) custom-call(s32[2]{0:T(128)S(1)} %pad_add_fusion.ids_ref, bf16[400,768]{1,0:T(8,128)(2,1)S(1)} %collective-permute-done.refs_0_, bf16[208,768]{1,0:T(8,128)(2,1)S(1)} %collective-permute-done.8.refs_1_, bf16[192,768]{1,0:T(8,128)(2,1)S(1)} %collective-permute-done.9.refs_2_, ...), custom_call_target="tpu_custom_call" | custom-call | flops 113246208 | bytes 147456 | tf_op jit(solution)/shard_map/pallas_call | solution.py:158
  53.0 2.2 %collective-permute-done.7.b_ref = bf16[400,768]{1,0:T(8,128)(2,1)S(1)} collective-permute-done((bf16[400,768]{1,0:T(8,128)(2,1)S(1)}, bf16[400,768]{1,0:T(8,128)(2,1)S(1)}, u32[]{:S(2)}, u32[]{:S(2)}) %collective-permute-start.7) | collective-permute-done | bytes 614432 | tf_op jit(solution)/shard_map/ppermute | solution.py:362
  55.8 1.5 %shard_map.82 = (f32[384,768]{1,0:T(8,128)S(1)}, f32[384,768]{1,0:T(8,128)S(1)}) custom-call(bf16[384,768]{1,0:T(8,128)(2,1)S(1)} %get-tuple-element.42.refs_7_.q_ref, bf16[384,768]{1,0:T(8,128)(2,1)S(1)} %get-tuple-element.50.k_ref, bf16[384,768]{1,0:T(8,128)(2,1)S(1)} %get-tuple-element.51.v_ref, f32[384,768]{1,0:T(8,128)S(1)} %get-tuple-element.46.num_ref, ...), custom_call_target="tpu_custom_call" | custom-call | flops 294912 | bytes 294912 | tf_op jit(solution)/shard_map/pallas_call | solution.py:184
  58.7 1.2 %collective-permute-done.16.refs_2_ = bf16[192,768]{1,0:T(8,128)(2,1)S(1)} collective-permute-done((bf16[192,768]{1,0:T(8,128)(2,1)S(1)}, bf16[192,768]{1,0:T(8,128)(2,1)S(1)}, u32[]{:S(2)}, u32[]{:S(2)}) %collective-permute-start.16) | collective-permute-done | bytes 294944 | tf_op jit(solution)/shard_map/ppermute | solution.py:22
  60.3 8.9 %shard_map.83 = (f32[384,768]{1,0:T(8,128)S(1)}, f32[384,768]{1,0:T(8,128)S(1)}) custom-call(s32[2]{0:T(128)S(1)} %pad_add_fusion.ids_ref, bf16[400,768]{1,0:T(8,128)(2,1)S(1)} %shard_map.81.refs_0_, bf16[208,768]{1,0:T(8,128)(2,1)S(1)} %collective-permute-done.15.refs_1_, bf16[192,768]{1,0:T(8,128)(2,1)S(1)} %collective-permute-done.16.refs_2_, ...), custom_call_target="tpu_custom_call" | custom-call | flops 113246208 | bytes 147456 | tf_op jit(solution)/shard_map/pallas_call | solution.py:158
  70.6 1.2 %collective-permute-done.21.refs_2_ = bf16[192,768]{1,0:T(8,128)(2,1)S(1)} collective-permute-done((bf16[192,768]{1,0:T(8,128)(2,1)S(1)}, bf16[192,768]{1,0:T(8,128)(2,1)S(1)}, u32[]{:S(2)}, u32[]{:S(2)}) %collective-permute-start.21) | collective-permute-done | bytes 294944 | tf_op jit(solution)/shard_map/ppermute | solution.py:22
  72.4 8.7 %shard_map.84.mine_ref = bf16[384,768]{1,0:T(8,128)(2,1)S(1)} custom-call(s32[2]{0:T(128)S(1)} %pad_add_fusion.ids_ref, bf16[400,768]{1,0:T(8,128)(2,1)S(1)} %shard_map.80.refs_0_, bf16[208,768]{1,0:T(8,128)(2,1)S(1)} %collective-permute-done.20.refs_1_, bf16[192,768]{1,0:T(8,128)(2,1)S(1)} %collective-permute-done.21.refs_2_, ...), custom_call_target="tpu_custom_call" | custom-call | flops 113246208 | bytes 147456 | tf_op jit(solution)/shard_map/pallas_call | solution.py:158
  81.6 1.6 %collective-permute-done.25.theirs_ref = bf16[384,768]{1,0:T(8,128)(2,1)S(1)} collective-permute-done((bf16[384,768]{1,0:T(8,128)(2,1)S(1)}, bf16[384,768]{1,0:T(8,128)(2,1)S(1)}, u32[]{:S(2)}, u32[]{:S(2)}) %collective-permute-start.25) | collective-permute-done | bytes 589856 | tf_op jit(solution)/shard_map/ppermute | solution.py:22
  83.6 1.6 %collective-permute-start.27 = (bf16[112,768]{1,0:T(8,128)(2,1)S(1)}, bf16[112,768]{1,0:T(8,128)(2,1)S(1)}, u32[]{:S(2)}, u32[]{:S(2)}) collective-permute-start(bf16[112,768]{1,0:T(8,128)(2,1)S(1)} %shard_map.86), channel_id=1, source_target_pairs={{0,2},{1,3},{2,0},{3,1},{4,6},{5,7},{6,4},{7,5},{8,10},{9,11},{10,... | collective-permute-start | bytes 516104 | tf_op jit(solution)/shard_map/ppermute | solution.py:22
  86.8 1.6 %collective-permute-start.29 = (bf16[144,768]{1,0:T(8,128)(2,1)S(1)}, bf16[144,768]{1,0:T(8,128)(2,1)S(1)}, u32[]{:S(2)}, u32[]{:S(2)}) collective-permute-start(bf16[144,768]{1,0:T(8,128)(2,1)S(1)} %shard_map.90), channel_id=1, source_target_pairs={{0,2},{1,3},{2,0},{3,1},{4,6},{5,7},{6,4},{7,5},{8,10},{9,11},{10,... | collective-permute-start | bytes 663560 | tf_op jit(solution)/shard_map/ppermute | solution.py:22
  88.4 1.1 shard_map.85
  89.5 1.5 %collective-permute-done.27.refs_1_ = bf16[112,768]{1,0:T(8,128)(2,1)S(1)} collective-permute-done((bf16[112,768]{1,0:T(8,128)(2,1)S(1)}, bf16[112,768]{1,0:T(8,128)(2,1)S(1)}, u32[]{:S(2)}, u32[]{:S(2)}) %collective-permute-start.27) | collective-permute-done | bytes 172064 | tf_op jit(solution)/shard_map/ppermute | solution.py:22
  91.0 1.3 %collective-permute-start.32 = (bf16[112,768]{1,0:T(8,128)(2,1)S(1)}, bf16[112,768]{1,0:T(8,128)(2,1)S(1)}, u32[]{:S(2)}, u32[]{:S(2)}) collective-permute-start(bf16[112,768]{1,0:T(8,128)(2,1)S(1)} %shard_map.87), channel_id=1, source_target_pairs={{4,0},{8,4},{12,8},{5,1},{9,5},{13,9},{6,2},{10,6},{14,10},{7,3},{... | collective-permute-start | bytes 516104 | tf_op jit(solution)/shard_map/ppermute | solution.py:28
  92.3 2.8 %collective-permute-done.28.refs_1_ = bf16[128,768]{1,0:T(8,128)(2,1)S(1)} collective-permute-done((bf16[128,768]{1,0:T(8,128)(2,1)S(1)}, bf16[128,768]{1,0:T(8,128)(2,1)S(1)}, u32[]{:S(2)}, u32[]{:S(2)}) %collective-permute-start.28) | collective-permute-done | bytes 196640 | tf_op jit(solution)/shard_map/ppermute | solution.py:22
  95.2 1.4 %collective-permute-start.31 = (bf16[128,768]{1,0:T(8,128)(2,1)S(1)}, bf16[128,768]{1,0:T(8,128)(2,1)S(1)}, u32[]{:S(2)}, u32[]{:S(2)}) collective-permute-start(bf16[128,768]{1,0:T(8,128)(2,1)S(1)} %shard_map.89), channel_id=1, source_target_pairs={{4,0},{8,4},{12,8},{5,1},{9,5},{13,9},{6,2},{10,6},{14,10},{7,3},{... | collective-permute-start | bytes 589832 | tf_op jit(solution)/shard_map/ppermute | solution.py:28
  96.7 2.7 %collective-permute-done.29.refs_1_ = bf16[144,768]{1,0:T(8,128)(2,1)S(1)} collective-permute-done((bf16[144,768]{1,0:T(8,128)(2,1)S(1)}, bf16[144,768]{1,0:T(8,128)(2,1)S(1)}, u32[]{:S(2)}, u32[]{:S(2)}) %collective-permute-start.29) | collective-permute-done | bytes 221216 | tf_op jit(solution)/shard_map/ppermute | solution.py:22
  99.4 1.3 %collective-permute-start.30 = (bf16[144,768]{1,0:T(8,128)(2,1)S(1)}, bf16[144,768]{1,0:T(8,128)(2,1)S(1)}, u32[]{:S(2)}, u32[]{:S(2)}) collective-permute-start(bf16[144,768]{1,0:T(8,128)(2,1)S(1)} %shard_map.91), channel_id=1, source_target_pairs={{4,0},{8,4},{12,8},{5,1},{9,5},{13,9},{6,2},{10,6},{14,10},{7,3},{... | collective-permute-start | bytes 663560 | tf_op jit(solution)/shard_map/ppermute | solution.py:28
  100.7 0.9 maximum_bitcast_fusion
  102.3 1.3 %collective-permute-done.31.incoming_ref = bf16[128,768]{1,0:T(8,128)(2,1)S(1)} collective-permute-done((bf16[128,768]{1,0:T(8,128)(2,1)S(1)}, bf16[128,768]{1,0:T(8,128)(2,1)S(1)}, u32[]{:S(2)}, u32[]{:S(2)}) %collective-permute-start.31) | collective-permute-done | bytes 196640 | tf_op jit(solution)/shard_map/ppermute | solution.py:28
  104.3 4.4 %collective-permute-done.30.incoming_ref = bf16[144,768]{1,0:T(8,128)(2,1)S(1)} collective-permute-done((bf16[144,768]{1,0:T(8,128)(2,1)S(1)}, bf16[144,768]{1,0:T(8,128)(2,1)S(1)}, u32[]{:S(2)}, u32[]{:S(2)}) %collective-permute-start.30) | collective-permute-done | bytes 221216 | tf_op jit(solution)/shard_map/ppermute | solution.py:28
  (97 shorter events, 15.7 us)
Async XLA Ops:
  2.3 16.9 %collective-permute-start = (bf16[400,768]{1,0:T(8,128)(2,1)S(1)}, bf16[400,768]{1,0:T(8,128)(2,1)S(1)}, u32[]{:S(2)}, u32[]{:S(2)}) collective-permute-start(bf16[400,768]{1,0:T(8,128)(2,1)S(1)} %fusion.3.refs_0_), channel_id=1, source_target_pairs={{0,4},{4,0},{8,12},{12,8},{1,5},{5,1},{9,13},{13,9},{2,6},{6,2},{1... | collective-permute-start | bytes 1843208 | tf_op jit(solution)/shard_map/ppermute | solution.py:355
  5.4 16.3 %collective-permute-start.4 = (bf16[400,768]{1,0:T(8,128)(2,1)S(1)}, bf16[400,768]{1,0:T(8,128)(2,1)S(1)}, u32[]{:S(2)}, u32[]{:S(2)}) collective-permute-start(bf16[400,768]{1,0:T(8,128)(2,1)S(1)} %fusion.3.refs_0_), channel_id=1, source_target_pairs={{0,2},{1,3},{2,0},{3,1},{4,6},{5,7},{6,4},{7,5},{8,10},{9,11},{10,... | collective-permute-start | bytes 1843208 | tf_op jit(solution)/shard_map/ppermute | solution.py:22
  6.9 13.1 %collective-permute-start.13 = (bf16[400,768]{1,0:T(8,128)(2,1)S(1)}, bf16[400,768]{1,0:T(8,128)(2,1)S(1)}, u32[]{:S(2)}, u32[]{:S(2)}) collective-permute-start(bf16[400,768]{1,0:T(8,128)(2,1)S(1)} %fusion.3.refs_0_), channel_id=1, source_target_pairs={{4,8},{8,4},{5,9},{9,5},{6,10},{10,6},{7,11},{11,7},{20,24},{24,20... | collective-permute-start | bytes 1843208 | tf_op jit(solution)/shard_map/ppermute | solution.py:358
  7.6 15.5 %collective-permute-start.2 = (bf16[208,768]{1,0:T(8,128)(2,1)S(1)}, bf16[208,768]{1,0:T(8,128)(2,1)S(1)}, u32[]{:S(2)}, u32[]{:S(2)}) collective-permute-start(bf16[208,768]{1,0:T(8,128)(2,1)S(1)} %slice.102), channel_id=1, source_target_pairs={{0,1},{1,0},{2,3},{3,2},{4,5},{5,4},{6,7},{7,6},{8,9},{9,8},{10,11... | collective-permute-start | bytes 958472 | tf_op jit(solution)/shard_map/ppermute | solution.py:22
  8.4 14.6 %collective-permute-start.3 = (bf16[192,768]{1,0:T(8,128)(2,1)}, bf16[192,768]{1,0:T(8,128)(2,1)S(1)}, u32[]{:S(2)}, u32[]{:S(2)}) collective-permute-start(bf16[192,768]{1,0:T(8,128)(2,1)} %slice_bitcast_fusion), channel_id=1, source_target_pairs={{0,1},{1,0},{2,3},{3,2},{4,5},{5,4},{6,7},{7,6},{8,9},{9,8},{10,11... | collective-permute-start | bytes 884744 | tf_op jit(solution)/shard_map/ppermute | solution.py:22
  19.2 14.6 %collective-permute-start.1 = (bf16[400,768]{1,0:T(8,128)(2,1)S(1)}, bf16[400,768]{1,0:T(8,128)(2,1)S(1)}, u32[]{:S(2)}, u32[]{:S(2)}) collective-permute-start(bf16[400,768]{1,0:T(8,128)(2,1)S(1)} %collective-permute-done.refs_0_), channel_id=1, source_target_pairs={{4,8},{8,4},{5,9},{9,5},{6,10},{10,6},{7,11},{11,7},{20,24},{24,20... | collective-permute-start | bytes 1843208 | tf_op jit(solution)/shard_map/ppermute | solution.py:357
  19.9 22.3 %collective-permute-start.10 = (bf16[400,768]{1,0:T(8,128)(2,1)S(1)}, bf16[400,768]{1,0:T(8,128)(2,1)S(1)}, u32[]{:S(2)}, u32[]{:S(2)}) collective-permute-start(bf16[400,768]{1,0:T(8,128)(2,1)S(1)} %collective-permute-done.refs_0_), channel_id=1, source_target_pairs={{0,2},{1,3},{2,0},{3,1},{4,6},{5,7},{6,4},{7,5},{8,10},{9,11},{10,... | collective-permute-start | bytes 1843208 | tf_op jit(solution)/shard_map/ppermute | solution.py:22
  21.7 18.9 %collective-permute-start.14 = (bf16[400,768]{1,0:T(8,128)(2,1)S(1)}, bf16[400,768]{1,0:T(8,128)(2,1)S(1)}, u32[]{:S(2)}, u32[]{:S(2)}) collective-permute-start(bf16[400,768]{1,0:T(8,128)(2,1)S(1)} %collective-permute-done.13.a_ref), channel_id=1, source_target_pairs={{4,0},{8,12},{5,1},{9,13},{6,2},{10,14},{7,3},{11,15},{20,16},{24,... | collective-permute-start | bytes 1843208 | tf_op jit(solution)/shard_map/ppermute | solution.py:359
  23.0 2.1 %collective-permute-start.5 = (bf16[208,768]{1,0:T(8,128)(2,1)S(1)}, bf16[208,768]{1,0:T(8,128)(2,1)S(1)}, u32[]{:S(2)}, u32[]{:S(2)}) collective-permute-start(bf16[208,768]{1,0:T(8,128)(2,1)S(1)} %slice.82), channel_id=1, source_target_pairs={{0,1},{1,0},{2,3},{3,2},{4,5},{5,4},{6,7},{7,6},{8,9},{9,8},{10,11... | collective-permute-start | bytes 958472 | tf_op jit(solution)/shard_map/ppermute | solution.py:22
  23.1 2.0 %collective-permute-start.6 = (bf16[192,768]{1,0:T(8,128)(2,1)S(1)}, bf16[192,768]{1,0:T(8,128)(2,1)S(1)}, u32[]{:S(2)}, u32[]{:S(2)}) collective-permute-start(bf16[192,768]{1,0:T(8,128)(2,1)S(1)} %slice.83), channel_id=1, source_target_pairs={{0,1},{1,0},{2,3},{3,2},{4,5},{5,4},{6,7},{7,6},{8,9},{9,8},{10,11... | collective-permute-start | bytes 884744 | tf_op jit(solution)/shard_map/ppermute | solution.py:22
  33.8 21.3 %collective-permute-start.7 = (bf16[400,768]{1,0:T(8,128)(2,1)S(1)}, bf16[400,768]{1,0:T(8,128)(2,1)S(1)}, u32[]{:S(2)}, u32[]{:S(2)}) collective-permute-start(bf16[400,768]{1,0:T(8,128)(2,1)S(1)} %collective-permute-done.1.a_ref), channel_id=1, source_target_pairs={{4,0},{8,12},{5,1},{9,13},{6,2},{10,14},{7,3},{11,15},{20,16},{24,... | collective-permute-start | bytes 1843208 | tf_op jit(solution)/shard_map/ppermute | solution.py:362
  35.4 7.0 %collective-permute-start.9 = (bf16[192,768]{1,0:T(8,128)(2,1)S(1)}, bf16[192,768]{1,0:T(8,128)(2,1)S(1)}, u32[]{:S(2)}, u32[]{:S(2)}) collective-permute-start(bf16[192,768]{1,0:T(8,128)(2,1)S(1)} %slice.85), channel_id=1, source_target_pairs={{0,1},{1,0},{2,3},{3,2},{4,5},{5,4},{6,7},{7,6},{8,9},{9,8},{10,11... | collective-permute-start | bytes 884744 | tf_op jit(solution)/shard_map/ppermute | solution.py:22
  35.6 8.7 %collective-permute-start.8 = (bf16[208,768]{1,0:T(8,128)(2,1)S(1)}, bf16[208,768]{1,0:T(8,128)(2,1)S(1)}, u32[]{:S(2)}, u32[]{:S(2)}) collective-permute-start(bf16[208,768]{1,0:T(8,128)(2,1)S(1)} %slice.84), channel_id=1, source_target_pairs={{0,1},{1,0},{2,3},{3,2},{4,5},{5,4},{6,7},{7,6},{8,9},{9,8},{10,11... | collective-permute-start | bytes 958472 | tf_op jit(solution)/shard_map/ppermute | solution.py:22
  40.6 16.8 %collective-permute-start.17 = (bf16[400,768]{1,0:T(8,128)(2,1)S(1)}, bf16[400,768]{1,0:T(8,128)(2,1)S(1)}, u32[]{:S(2)}, u32[]{:S(2)}) collective-permute-start(bf16[400,768]{1,0:T(8,128)(2,1)S(1)} %shard_map.81.refs_0_), channel_id=1, source_target_pairs={{0,2},{1,3},{2,0},{3,1},{4,6},{5,7},{6,4},{7,5},{8,10},{9,11},{10,... | collective-permute-start | bytes 1843208 | tf_op jit(solution)/shard_map/ppermute | solution.py:22
  42.2 2.1 %collective-permute-start.11 = (bf16[208,768]{1,0:T(8,128)(2,1)S(1)}, bf16[208,768]{1,0:T(8,128)(2,1)S(1)}, u32[]{:S(2)}, u32[]{:S(2)}) collective-permute-start(bf16[208,768]{1,0:T(8,128)(2,1)S(1)} %slice.86), channel_id=1, source_target_pairs={{0,1},{1,0},{2,3},{3,2},{4,5},{5,4},{6,7},{7,6},{8,9},{9,8},{10,11... | collective-permute-start | bytes 958472 | tf_op jit(solution)/shard_map/ppermute | solution.py:22
  42.3 2.0 %collective-permute-start.12 = (bf16[192,768]{1,0:T(8,128)(2,1)S(1)}, bf16[192,768]{1,0:T(8,128)(2,1)S(1)}, u32[]{:S(2)}, u32[]{:S(2)}) collective-permute-start(bf16[192,768]{1,0:T(8,128)(2,1)S(1)} %slice.87), channel_id=1, source_target_pairs={{0,1},{1,0},{2,3},{3,2},{4,5},{5,4},{6,7},{7,6},{8,9},{9,8},{10,11... | collective-permute-start | bytes 884744 | tf_op jit(solution)/shard_map/ppermute | solution.py:22
  55.2 14.3 %collective-permute-start.22 = (bf16[400,768]{1,0:T(8,128)(2,1)S(1)}, bf16[400,768]{1,0:T(8,128)(2,1)S(1)}, u32[]{:S(2)}, u32[]{:S(2)}) collective-permute-start(bf16[400,768]{1,0:T(8,128)(2,1)S(1)} %shard_map.80.refs_0_), channel_id=1, source_target_pairs={{0,2},{1,3},{2,0},{3,1},{4,6},{5,7},{6,4},{7,5},{8,10},{9,11},{10,... | collective-permute-start | bytes 1843208 | tf_op jit(solution)/shard_map/ppermute | solution.py:22
  57.3 2.6 %collective-permute-start.15 = (bf16[208,768]{1,0:T(8,128)(2,1)S(1)}, bf16[208,768]{1,0:T(8,128)(2,1)S(1)}, u32[]{:S(2)}, u32[]{:S(2)}) collective-permute-start(bf16[208,768]{1,0:T(8,128)(2,1)S(1)} %slice.88), channel_id=1, source_target_pairs={{0,1},{1,0},{2,3},{3,2},{4,5},{5,4},{6,7},{7,6},{8,9},{9,8},{10,11... | collective-permute-start | bytes 958472 | tf_op jit(solution)/shard_map/ppermute | solution.py:22
  57.5 2.9 %collective-permute-start.18 = (bf16[208,768]{1,0:T(8,128)(2,1)S(1)}, bf16[208,768]{1,0:T(8,128)(2,1)S(1)}, u32[]{:S(2)}, u32[]{:S(2)}) collective-permute-start(bf16[208,768]{1,0:T(8,128)(2,1)S(1)} %slice.90), channel_id=1, source_target_pairs={{0,1},{1,0},{2,3},{3,2},{4,5},{5,4},{6,7},{7,6},{8,9},{9,8},{10,11... | collective-permute-start | bytes 958472 | tf_op jit(solution)/shard_map/ppermute | solution.py:22
  58.0 1.9 %collective-permute-start.16 = (bf16[192,768]{1,0:T(8,128)(2,1)S(1)}, bf16[192,768]{1,0:T(8,128)(2,1)S(1)}, u32[]{:S(2)}, u32[]{:S(2)}) collective-permute-start(bf16[192,768]{1,0:T(8,128)(2,1)S(1)} %slice.89), channel_id=1, source_target_pairs={{0,1},{1,0},{2,3},{3,2},{4,5},{5,4},{6,7},{7,6},{8,9},{9,8},{10,11... | collective-permute-start | bytes 884744 | tf_op jit(solution)/shard_map/ppermute | solution.py:22
  58.1 2.2 %collective-permute-start.19 = (bf16[192,768]{1,0:T(8,128)(2,1)S(1)}, bf16[192,768]{1,0:T(8,128)(2,1)S(1)}, u32[]{:S(2)}, u32[]{:S(2)}) collective-permute-start(bf16[192,768]{1,0:T(8,128)(2,1)S(1)} %slice.91), channel_id=1, source_target_pairs={{0,1},{1,0},{2,3},{3,2},{4,5},{5,4},{6,7},{7,6},{8,9},{9,8},{10,11... | collective-permute-start | bytes 884744 | tf_op jit(solution)/shard_map/ppermute | solution.py:22
  69.2 2.6 %collective-permute-start.20 = (bf16[208,768]{1,0:T(8,128)(2,1)S(1)}, bf16[208,768]{1,0:T(8,128)(2,1)S(1)}, u32[]{:S(2)}, u32[]{:S(2)}) collective-permute-start(bf16[208,768]{1,0:T(8,128)(2,1)S(1)} %slice.92), channel_id=1, source_target_pairs={{0,1},{1,0},{2,3},{3,2},{4,5},{5,4},{6,7},{7,6},{8,9},{9,8},{10,11... | collective-permute-start | bytes 958472 | tf_op jit(solution)/shard_map/ppermute | solution.py:22
  69.6 2.6 %collective-permute-start.23 = (bf16[208,768]{1,0:T(8,128)(2,1)S(1)}, bf16[208,768]{1,0:T(8,128)(2,1)S(1)}, u32[]{:S(2)}, u32[]{:S(2)}) collective-permute-start(bf16[208,768]{1,0:T(8,128)(2,1)S(1)} %slice.94), channel_id=1, source_target_pairs={{0,1},{1,0},{2,3},{3,2},{4,5},{5,4},{6,7},{7,6},{8,9},{9,8},{10,11... | collective-permute-start | bytes 958472 | tf_op jit(solution)/shard_map/ppermute | solution.py:22
  70.3 1.9 %collective-permute-start.24 = (bf16[192,768]{1,0:T(8,128)(2,1)S(1)}, bf16[192,768]{1,0:T(8,128)(2,1)S(1)}, u32[]{:S(2)}, u32[]{:S(2)}) collective-permute-start(bf16[192,768]{1,0:T(8,128)(2,1)S(1)} %slice.95), channel_id=1, source_target_pairs={{0,1},{1,0},{2,3},{3,2},{4,5},{5,4},{6,7},{7,6},{8,9},{9,8},{10,11... | collective-permute-start | bytes 884744 | tf_op jit(solution)/shard_map/ppermute | solution.py:22
  72.2 10.9 %collective-permute-start.26 = (bf16[2,768,768]{2,1,0:T(8,128)(2,1)S(1)}, bf16[2,768,768]{2,1,0:T(8,128)(2,1)S(1)}, u32[]{:S(2)}, u32[]{:S(2)}) collective-permute-start(bf16[2,768,768]{2,1,0:T(8,128)(2,1)S(1)} %copy-done.7), channel_id=1, source_target_pairs={{0,1},{1,0},{2,3},{3,2},{4,5},{5,4},{6,7},{7,6},{8,9},{9,8},{10,11... | collective-permute-start | bytes 7077896 | tf_op jit(solution)/shard_map/ppermute | solution.py:22
  81.1 2.1 %collective-permute-start.25 = (bf16[384,768]{1,0:T(8,128)(2,1)S(1)}, bf16[384,768]{1,0:T(8,128)(2,1)S(1)}, u32[]{:S(2)}, u32[]{:S(2)}) collective-permute-start(bf16[384,768]{1,0:T(8,128)(2,1)S(1)} %shard_map.84.mine_ref), channel_id=1, source_target_pairs={{0,1},{1,0},{2,3},{3,2},{4,5},{5,4},{6,7},{7,6},{8,9},{9,8},{10,11... | collective-permute-start | bytes 1769480 | tf_op jit(solution)/shard_map/ppermute | solution.py:22
  83.6 7.3 %collective-permute-start.27 = (bf16[112,768]{1,0:T(8,128)(2,1)S(1)}, bf16[112,768]{1,0:T(8,128)(2,1)S(1)}, u32[]{:S(2)}, u32[]{:S(2)}) collective-permute-start(bf16[112,768]{1,0:T(8,128)(2,1)S(1)} %shard_map.86), channel_id=1, source_target_pairs={{0,2},{1,3},{2,0},{3,1},{4,6},{5,7},{6,4},{7,5},{8,10},{9,11},{10,... | collective-permute-start | bytes 516104 | tf_op jit(solution)/shard_map/ppermute | solution.py:22
  85.7 9.4 %collective-permute-start.28 = (bf16[128,768]{1,0:T(8,128)(2,1)S(1)}, bf16[128,768]{1,0:T(8,128)(2,1)S(1)}, u32[]{:S(2)}, u32[]{:S(2)}) collective-permute-start(bf16[128,768]{1,0:T(8,128)(2,1)S(1)} %shard_map.88), channel_id=1, source_target_pairs={{0,2},{1,3},{2,0},{3,1},{4,6},{5,7},{6,4},{7,5},{8,10},{9,11},{10,... | collective-permute-start | bytes 589832 | tf_op jit(solution)/shard_map/ppermute | solution.py:22
  86.8 12.5 %collective-permute-start.29 = (bf16[144,768]{1,0:T(8,128)(2,1)S(1)}, bf16[144,768]{1,0:T(8,128)(2,1)S(1)}, u32[]{:S(2)}, u32[]{:S(2)}) collective-permute-start(bf16[144,768]{1,0:T(8,128)(2,1)S(1)} %shard_map.90), channel_id=1, source_target_pairs={{0,2},{1,3},{2,0},{3,1},{4,6},{5,7},{6,4},{7,5},{8,10},{9,11},{10,... | collective-permute-start | bytes 663560 | tf_op jit(solution)/shard_map/ppermute | solution.py:22
  91.0 10.6 %collective-permute-start.32 = (bf16[112,768]{1,0:T(8,128)(2,1)S(1)}, bf16[112,768]{1,0:T(8,128)(2,1)S(1)}, u32[]{:S(2)}, u32[]{:S(2)}) collective-permute-start(bf16[112,768]{1,0:T(8,128)(2,1)S(1)} %shard_map.87), channel_id=1, source_target_pairs={{4,0},{8,4},{12,8},{5,1},{9,5},{13,9},{6,2},{10,6},{14,10},{7,3},{... | collective-permute-start | bytes 516104 | tf_op jit(solution)/shard_map/ppermute | solution.py:28
  95.2 8.4 %collective-permute-start.31 = (bf16[128,768]{1,0:T(8,128)(2,1)S(1)}, bf16[128,768]{1,0:T(8,128)(2,1)S(1)}, u32[]{:S(2)}, u32[]{:S(2)}) collective-permute-start(bf16[128,768]{1,0:T(8,128)(2,1)S(1)} %shard_map.89), channel_id=1, source_target_pairs={{4,0},{8,4},{12,8},{5,1},{9,5},{13,9},{6,2},{10,6},{14,10},{7,3},{... | collective-permute-start | bytes 589832 | tf_op jit(solution)/shard_map/ppermute | solution.py:28
  99.4 9.3 %collective-permute-start.30 = (bf16[144,768]{1,0:T(8,128)(2,1)S(1)}, bf16[144,768]{1,0:T(8,128)(2,1)S(1)}, u32[]{:S(2)}, u32[]{:S(2)}) collective-permute-start(bf16[144,768]{1,0:T(8,128)(2,1)S(1)} %shard_map.91), channel_id=1, source_target_pairs={{4,0},{8,4},{12,8},{5,1},{9,5},{13,9},{6,2},{10,6},{14,10},{7,3},{... | collective-permute-start | bytes 663560 | tf_op jit(solution)/shard_map/ppermute | solution.py:28
  (9 other events, 42.2 us)
